TPU v7x, 32 devices: a whole 2x2x4 slice. The times are simulated.
32 devices in a mesh: dp: 8 (over y, x, core), mp: 4 (over z).
Axes of the slice: x: 2, y: 2, z: 4, core: 2. Of those that a mesh axis runs over, the one named last changes fastest.
Arguments:
- inputs: bfloat16 [12288, 768], P(('dp', 'mp')), may hold values from -6 to 6
- token_ids: int32 [12288], P(('dp', 'mp')), may hold values from 0 to 501152, as said below
- out_cot: bfloat16 [12288, 768], P(('dp', 'mp')), as said below
- pair_ids: int32 [96], replicated, may hold values from 0 to 108
- w_qkv: bfloat16 [3, 768, 768], P(None, None, 'mp'), may hold values from -0.21875 to 0.21875
- b_qv: bfloat16 [2, 768], P(None, 'mp'), may hold values from -3 to 3
- w_attn: bfloat16 [768, 768], P('mp'), may hold values from -0.875 to 0.875
- b_attn: bfloat16 [768], replicated, may hold values from -3 to 3
- norm1_gain: bfloat16 [768], replicated, may hold values from 0.5 to 1.5
- norm1_bias: bfloat16 [768], replicated, may hold values from -3 to 3
- w_in: bfloat16 [768, 3072], P(None, 'mp'), may hold values from -0.21875 to 0.21875
- b_in: bfloat16 [3072], P('mp'), may hold values from -3 to 3
- w_out: bfloat16 [3072, 768], P('mp'), may hold values from -0.109375 to 0.109375
- b_out: bfloat16 [768], replicated, may hold values from -3 to 3
- norm2_gain: bfloat16 [768], replicated, may hold values from 0.5 to 1.5
- norm2_bias: bfloat16 [768], replicated, may hold values from -3 to 3
- w_pool: bfloat16 [768, 768], replicated, may hold values from -0.21875 to 0.21875
- b_pool: bfloat16 [768], replicated, may hold values from -3 to 3
- scale: float32 [1], replicated, may hold values from 20 to 40
Outputs:
- layer_out: bfloat16 [12288, 768], P(('dp', 'mp'))
- input_grad: float32 [12288, 768], P(('dp', 'mp'))
- grad_qkv: float32 [3, 768, 768], P(None, None, 'mp')
- grad_b_qv: float32 [2, 768], P(None, 'mp')
- grad_attn: float32 [768, 768], P('mp')
- grad_b_attn: float32 [768], replicated
- grad_norm1_gain: float32 [768], replicated
- grad_norm1_bias: float32 [768], replicated
- grad_w_in: float32 [768, 3072], P(None, 'mp')
- grad_b_in: float32 [3072], P('mp')
- grad_w_out: float32 [3072, 768], P('mp')
- grad_b_out: float32 [768], replicated
- grad_norm2_gain: float32 [768], replicated
- grad_norm2_bias: float32 [768], replicated
- grad_pool: float32 [768, 768], replicated
- grad_b_pool: float32 [768], replicated
- new_scale: float32 [1], replicated
Inputs may be any that keep to these rules, and one draw needn't show every extreme that they name: `token_ids`: id 0 marks padding. Each sentence of 64 positions holds its nonzero ids first and its zeros after them; at least 8 ids of a sentence are nonzero, and some sentences hold no zero. `out_cot`: Real-valued entries, nonzero in every row.
All inputs are finite; a program needn't handle non-finite values.
Results may differ from a plain program's by a relative error of at most 0.02.
Values may be sent and summed in bfloat16 or wider, within the bound.
No kernel may reach another device: no remote copies, remote signals or barrier semaphores. Data moves between devices by JAX's collectives and lax.ppermute only.
A program may use at most 128 MiB of HBM per device.

v0:
```python
import jax
import jax.numpy as jnp
from jax import lax
from jax.sharding import PartitionSpec as P

HEAD_DIM = 64
SEQ = 64


eps_norm = 1e-12
margin = 0.3
step_rate = 1.0
masked_low = -1e30
high = lax.Precision.HIGHEST


def norm_forward(rows_in, gain, shift):
    center = rows_in - jnp.mean(rows_in, axis=-1, keepdims=True)
    inv_std = lax.rsqrt(jnp.mean(center * center, axis=-1, keepdims=True) + eps_norm)
    normed = center * inv_std
    return (normed * gain + shift, normed, inv_std)


def norm_backward(grad_out, normed, inv_std, gain):
    scaled = grad_out * gain
    inner = (
        scaled
        - jnp.mean(scaled, axis=-1, keepdims=True)
        - normed * jnp.mean(scaled * normed, axis=-1, keepdims=True)
    )
    return (inv_std * inner, jnp.sum(grad_out * normed, axis=0), jnp.sum(grad_out, axis=0))


def gelu_slope(pre_act):
    return (
        0.5 * (1.0 + lax.erf(pre_act * 0.7071067811865476))
        + pre_act * jnp.exp(-0.5 * pre_act * pre_act) * 0.3989422804014327
    )


def rank_terms(cosine, same, diag_mask, weight, scale_value, axis_of):
    shifted = cosine - margin * diag_mask
    logits = jnp.where(same, scale_value * shifted, masked_low)
    top = jnp.max(logits, axis=axis_of, keepdims=True)
    lse = top + jnp.log(jnp.sum(jnp.exp(logits - top), axis=axis_of, keepdims=True))
    probs = jnp.exp(logits - lse)
    grad_logit = weight * (probs - diag_mask)
    return (grad_logit, grad_logit * shifted)


def on_device(
    inputs,
    token_ids,
    out_cot,
    pair_ids,
    w_qkv,
    b_qv,
    w_attn,
    b_attn,
    norm1_gain,
    norm1_bias,
    w_in,
    b_in,
    w_out,
    b_out,
    norm2_gain,
    norm2_bias,
    w_pool,
    b_pool,
    scale,
):
    f32 = jnp.float32
    share = inputs.shape[0]
    width = inputs.shape[1]
    local_cols = w_qkv.shape[2]
    heads_here = local_cols // HEAD_DIM
    gain_one = norm1_gain.astype(f32)
    gain_two = norm2_gain.astype(f32)
    x_full, ids_full = (
        lax.all_gather(inputs, "mp", axis=0, tiled=True),
        lax.all_gather(token_ids, "mp", axis=0, tiled=True),
    )
    rows = x_full.shape[0]
    sents = rows // SEQ
    qkv = jnp.einsum("td,kde->kte", x_full, w_qkv, preferred_element_type=f32)
    biases = jnp.stack([b_qv[0].astype(f32), jnp.zeros((local_cols,), f32), b_qv[1].astype(f32)])
    qkv = (
        (qkv + biases[:, None, :]).astype(jnp.bfloat16).reshape(3, sents, SEQ, heads_here, HEAD_DIM)
    )
    query, key_part, value_part = (qkv[0], qkv[1], qkv[2])
    valid = (ids_full != 0).reshape(sents, 1, 1, SEQ)
    raw = jnp.einsum("sqhd,skhd->shqk", query, key_part, preferred_element_type=f32)
    scores = jnp.where(valid, raw * 0.125, masked_low)
    top = jnp.max(scores, axis=-1, keepdims=True)
    expd = jnp.exp(scores - top)
    totals = jnp.sum(expd, axis=-1, keepdims=True)
    lse = top + jnp.log(totals)
    probs_low = (expd / totals).astype(jnp.bfloat16)
    context = (
        jnp.einsum("shqk,skhd->sqhd", probs_low, value_part, preferred_element_type=f32)
        .reshape(rows, local_cols)
        .astype(jnp.bfloat16)
    )
    attn = lax.psum_scatter(
        jnp.dot(context, w_attn, preferred_element_type=f32), "mp", scatter_dimension=0, tiled=True
    )
    normed_one, hat_one, inv_one = norm_forward(
        inputs.astype(f32) + attn + b_attn.astype(f32), gain_one, norm1_bias.astype(f32)
    )
    normed_full = lax.all_gather(normed_one.astype(jnp.bfloat16), "mp", axis=0, tiled=True)
    pre_act = jnp.dot(normed_full, w_in, preferred_element_type=f32) + b_in.astype(f32)
    hidden = jax.nn.gelu(pre_act, approximate=False).astype(jnp.bfloat16)
    ffn = lax.psum_scatter(
        jnp.dot(hidden, w_out, preferred_element_type=f32), "mp", scatter_dimension=0, tiled=True
    )
    out_rows, hat_two, inv_two = norm_forward(
        normed_one + ffn + b_out.astype(f32), gain_two, norm2_bias.astype(f32)
    )
    layer_out = out_rows.astype(jnp.bfloat16)
    local_sents = share // SEQ
    own_pairs = local_sents // 2
    first_rows = out_rows.reshape(local_sents, SEQ, width)[:, 0, :].astype(jnp.bfloat16)
    pooled = jnp.tanh(jnp.dot(first_rows, w_pool, preferred_element_type=f32) + b_pool.astype(f32))
    inv_len = lax.rsqrt(jnp.sum(pooled * pooled, axis=-1, keepdims=True) + eps_norm)
    emb_full = pooled * inv_len
    emb_pairs = emb_full.astype(jnp.bfloat16).reshape(own_pairs, 2, width)
    src_own = emb_pairs[:, 0, :]
    tgt_own = emb_pairs[:, 1, :]
    all_src, all_tgt = (
        lax.all_gather(src_own, ("dp", "mp"), axis=0, tiled=True),
        lax.all_gather(tgt_own, ("dp", "mp"), axis=0, tiled=True),
    )
    npairs = all_src.shape[0]
    start = lax.axis_index(("dp", "mp")) * own_pairs
    scale_value = scale[0]
    all_src_f = all_src.astype(f32)
    all_tgt_f = all_tgt.astype(f32)
    cosine = jnp.einsum("kd,md->km", all_src, all_tgt, preferred_element_type=f32)
    same = pair_ids[:, None] == pair_ids[None, :]
    counts = jnp.sum(same.astype(f32), axis=1)
    index_all = jnp.arange(npairs)
    diag_mask = (index_all[:, None] == index_all[None, :]).astype(f32)
    grad_row, part_row = rank_terms(
        cosine, same, diag_mask, (1.0 / counts)[:, None], scale_value, 1
    )
    grad_col, part_col = rank_terms(
        cosine, same, diag_mask, (1.0 / counts)[None, :], scale_value, 0
    )
    grad_all = grad_row + grad_col
    own_rows = lax.dynamic_slice_in_dim(grad_all, start, own_pairs, 0)
    own_cols = lax.dynamic_slice_in_dim(grad_all, start, own_pairs, 1)
    grad_src = scale_value * jnp.dot(own_rows, all_tgt_f, precision=high)
    grad_tgt = scale_value * jnp.einsum("km,kd->md", own_cols, all_src_f, precision=high)
    scale_part = jnp.sum(lax.dynamic_slice_in_dim(part_row, start, own_pairs, 0)) + jnp.sum(
        lax.dynamic_slice_in_dim(part_col, start, own_pairs, 1)
    )
    grad_emb = jnp.stack([grad_src, grad_tgt], axis=1).reshape(local_sents, width)
    grad_pooled = inv_len * (
        grad_emb - emb_full * jnp.sum(emb_full * grad_emb, axis=-1, keepdims=True)
    )
    grad_ppre = (grad_pooled * (1.0 - pooled * pooled)).astype(jnp.bfloat16)
    grad_pool = jnp.einsum("sd,se->de", first_rows, grad_ppre, preferred_element_type=f32)
    grad_b_pool = jnp.sum(grad_ppre.astype(f32), axis=0)
    grad_first = jnp.einsum("se,de->sd", grad_ppre, w_pool, preferred_element_type=f32)
    grad_out = out_cot.astype(f32).reshape(local_sents, SEQ, width)
    grad_out = grad_out.at[:, 0, :].add(grad_first).reshape(share, width)
    grad_z2, grad_norm2_gain, grad_norm2_bias = norm_backward(grad_out, hat_two, inv_two, gain_two)
    grad_b_out = jnp.sum(grad_z2, axis=0)
    grad_ffn_full = lax.all_gather(grad_z2.astype(jnp.bfloat16), "mp", axis=0, tiled=True)
    grad_w_out = jnp.einsum("tf,td->fd", hidden, grad_ffn_full, preferred_element_type=f32)
    grad_hidden = jnp.einsum("td,fd->tf", grad_ffn_full, w_out, preferred_element_type=f32)
    grad_pre = (grad_hidden * gelu_slope(pre_act)).astype(jnp.bfloat16)
    grad_b_in = jnp.sum(grad_pre.astype(f32), axis=0)
    grad_w_in = jnp.einsum("td,tf->df", normed_full, grad_pre, preferred_element_type=f32)
    grad_h1 = (
        lax.psum_scatter(
            jnp.einsum("tf,df->td", grad_pre, w_in, preferred_element_type=f32),
            "mp",
            scatter_dimension=0,
            tiled=True,
        )
        + grad_z2
    )
    grad_z1, grad_norm1_gain, grad_norm1_bias = norm_backward(grad_h1, hat_one, inv_one, gain_one)
    grad_b_attn = jnp.sum(grad_z1, axis=0)
    grad_attn_full = lax.all_gather(grad_z1.astype(jnp.bfloat16), "mp", axis=0, tiled=True)
    grad_attn = jnp.einsum("te,td->ed", context, grad_attn_full, preferred_element_type=f32)
    grad_context = jnp.einsum("td,ed->te", grad_attn_full, w_attn, preferred_element_type=f32)
    grad_context = grad_context.astype(jnp.bfloat16).reshape(sents, SEQ, heads_here, HEAD_DIM)
    probs_again = jnp.exp(scores - lse)
    grad_value = jnp.einsum(
        "shqk,sqhd->skhd",
        probs_again.astype(jnp.bfloat16),
        grad_context,
        preferred_element_type=f32,
    )
    grad_probs = jnp.einsum("sqhd,skhd->shqk", grad_context, value_part, preferred_element_type=f32)
    inner_sum = jnp.sum(probs_again * grad_probs, axis=-1, keepdims=True)
    grad_raw = jnp.where(valid, probs_again * (grad_probs - inner_sum) * 0.125, 0.0).astype(
        jnp.bfloat16
    )
    grad_query = jnp.einsum("shqk,skhd->sqhd", grad_raw, key_part, preferred_element_type=f32)
    grad_key = jnp.einsum("shqk,sqhd->skhd", grad_raw, query, preferred_element_type=f32)
    grad_qkv_rows = (
        jnp.stack([grad_query, grad_key, grad_value])
        .astype(jnp.bfloat16)
        .reshape(3, rows, local_cols)
    )
    grad_b_qv = jnp.stack(
        [
            jnp.sum(grad_qkv_rows[0].astype(f32), axis=0),
            jnp.sum(grad_qkv_rows[2].astype(f32), axis=0),
        ]
    )
    grad_qkv = jnp.einsum("td,kte->kde", x_full, grad_qkv_rows, preferred_element_type=f32)
    input_grad = (
        lax.psum_scatter(
            jnp.einsum("kte,kde->td", grad_qkv_rows, w_qkv, preferred_element_type=f32),
            "mp",
            scatter_dimension=0,
            tiled=True,
        )
        + grad_z1
    )
    grad_qkv, grad_b_qv, grad_attn, grad_w_in, grad_b_in, grad_w_out = lax.psum(
        (grad_qkv, grad_b_qv, grad_attn, grad_w_in, grad_b_in, grad_w_out), "dp"
    )
    summed = lax.psum(
        (
            grad_b_attn,
            grad_norm1_gain,
            grad_norm1_bias,
            grad_b_out,
            grad_norm2_gain,
            grad_norm2_bias,
            grad_pool,
            grad_b_pool,
            jnp.reshape(scale_part, (1,)),
        ),
        ("dp", "mp"),
    )
    new_scale = scale - step_rate * summed[8]
    return (
        layer_out,
        input_grad,
        grad_qkv,
        grad_b_qv,
        grad_attn,
        summed[0],
        summed[1],
        summed[2],
        grad_w_in,
        grad_b_in,
        grad_w_out,
        summed[3],
        summed[4],
        summed[5],
        summed[6],
        summed[7],
        new_scale,
    )


def solution(mesh):
    in_specs = (
        P(("dp", "mp"), None),
        P(("dp", "mp")),
        P(("dp", "mp"), None),
        P(),
        P(None, None, "mp"),
        P(None, "mp"),
        P("mp", None),
        P(),
        P(),
        P(),
        P(None, "mp"),
        P("mp"),
        P("mp", None),
        P(),
        P(),
        P(),
        P(),
        P(),
        P(),
    )
    out_specs = (
        P(("dp", "mp"), None),
        P(("dp", "mp"), None),
        P(None, None, "mp"),
        P(None, "mp"),
        P("mp", None),
        P(),
        P(),
        P(),
        P(None, "mp"),
        P("mp"),
        P("mp", None),
        P(),
        P(),
        P(),
        P(),
        P(),
        P(),
    )
    return jax.shard_map(
        on_device, mesh=mesh, in_specs=in_specs, out_specs=out_specs, check_vma=False
    )
```

profile of v0, /device:TPU:0, one launch (start us, length us, event | category | flops | bytes accessed | tf_op | source)
XLA Modules:
  0.0 1100.1 jit_solution(3244285293392332224)
XLA Ops:
  8.7 13.5 %all-gather.2 = s32[4,1,384]{2,1,0:T(1,128)S(1)} all-gather(s32[1,1,384]{2,1,0:T(1,128)S(1)} %reshape.240), channel_id=1, replica_groups=mesh['dp'=8,'mp'=4] {'mp'}, dimensions={0}, use_global_device_ids=true | all-gather | bytes 7680 | tf_op jit(solution)/shard_map/all_gather | solution.py:81
  23.2 39.6 %all-gather.8.cloned.1.call-done = bf16[1536,768]{1,0:T(8,128)(2,1)} async-done(((bf16[384,768]{1,0:T(8,128)(2,1)}), bf16[1536,768]{1,0:T(8,128)(2,1)}) %all-gather.8.cloned.1.call-update) | async-done | bytes 2359312 | tf_op jit(solution)/shard_map/all_gather | solution.py:80
  62.8 3.5 fusion.17
  83.2 83.5 %reduce-scatter.5.cloned.1.call-done = f32[384,768]{1,0:T(8,128)} async-done(((f32[1536,768]{1,0:T(8,128)}), f32[384,768]{1,0:T(8,128)}) %reduce-scatter.5.cloned.1.call-update) | async-done | bytes 1179664 | tf_op jit(solution)/shard_map/reduce_scatter | solution.py:104
  169.9 50.8 %all-gather.10.cloned.1.call-done = bf16[1536,768]{1,0:T(8,128)(2,1)} async-done(((bf16[384,768]{1,0:T(8,128)(2,1)}), bf16[1536,768]{1,0:T(8,128)(2,1)}) %all-gather.10.cloned.1.call-update) | async-done | bytes 2359312 | tf_op jit(solution)/shard_map/all_gather | solution.py:110
  220.8 14.0 %fusion.3 = (bf16[1536,768]{1,0:T(8,128)(2,1)S(1)}, f32[1536,768]{1,0:T(8,128)}) fusion(f32[768]{0:T(1024)S(1)} %convert_element_type.130, bf16[1536,768]{1,0:T(8,128)(2,1)} %all-gather.10.cloned.1.call-done, bf16[768,768]{1,0:T(8,128)(2,1)S(1)} %copy-done), kind=kOutput, calls=%fused_computation.5 | convolution fusion | flops 1889796096 | bytes 10619904 | tf_op jit(solution)/shard_map/dot_general | solution.py:111
  236.1 4.2 fusion.108
  245.6 79.0 %reduce-scatter.7.cloned.1.call-done = f32[384,768]{1,0:T(8,128)} async-done(((f32[1536,768]{1,0:T(8,128)}), f32[384,768]{1,0:T(8,128)}) %reduce-scatter.7.cloned.1.call-update) | async-done | bytes 1179664 | tf_op jit(solution)/shard_map/reduce_scatter | solution.py:113
  330.2 69.8 %all-gather.1 = bf16[96,1,768]{2,1,0:T(2,128)(2,1)S(1)} all-gather(bf16[3,1,768]{2,1,0:T(2,128)(2,1)S(1)} %get-tuple-element.73), channel_id=3, replica_groups=mesh['dp'=8,'mp'=4] {'dp','mp'}, dimensions={0}, use_global_device_ids=true | all-gather | bytes 152064 | tf_op jit(solution)/shard_map/all_gather | solution.py:131
  400.0 65.7 %all-gather = bf16[96,1,768]{2,1,0:T(2,128)(2,1)S(1)} all-gather(bf16[3,1,768]{2,1,0:T(2,128)(2,1)S(1)} %get-tuple-element.74), channel_id=2, replica_groups=mesh['dp'=8,'mp'=4] {'dp','mp'}, dimensions={0}, use_global_device_ids=true | all-gather | bytes 152064 | tf_op jit(solution)/shard_map/all_gather | solution.py:130
  487.9 48.6 %all-gather.12.cloned.1.call-done = bf16[1536,768]{1,0:T(8,128)(2,1)} async-done(((bf16[384,768]{1,0:T(8,128)(2,1)}), bf16[1536,768]{1,0:T(8,128)(2,1)}) %all-gather.12.cloned.1.call-update) | async-done | bytes 2359312 | tf_op jit(solution)/shard_map/all_gather | solution.py:169
  536.5 6.5 convert_reduce_fusion
  544.5 4.2 fusion.109
  548.8 84.2 %reduce-scatter.9.cloned.1.call-done = f32[384,768]{1,0:T(8,128)} async-done(((f32[1536,768]{1,0:T(8,128)}), f32[384,768]{1,0:T(8,128)}) %reduce-scatter.9.cloned.1.call-update) | async-done | bytes 1179664 | tf_op jit(solution)/shard_map/reduce_scatter | solution.py:176
  637.4 8.7 reduce-scatter.11.cloned.1.call-start
  646.8 41.8 %all-gather.14.cloned.1.call-done = bf16[1536,768]{1,0:T(8,128)(2,1)} async-done(((bf16[384,768]{1,0:T(8,128)(2,1)}), bf16[1536,768]{1,0:T(8,128)(2,1)}) %all-gather.14.cloned.1.call-update) | async-done | bytes 2359312 | tf_op jit(solution)/shard_map/all_gather | solution.py:186
  699.0 6.6 fusion.43
  705.7 7.3 convert_reduce_fusion.2
  731.8 5.9 convolution_bitcast_fusion
  740.4 6.3 fusion.113
  758.6 47.5 %all-reduce = (f32[768]{0:T(1024)}, f32[768]{0:T(1024)}, f32[768]{0:T(1024)}, f32[768]{0:T(1024)}, f32[768]{0:T(1024)}, /*index=5*/f32[768]{0:T(1024)}, f32[768]{0:T(1024)}, f32[1]{0:T(128)}) all-reduce(f32[768]{0:T(1024)S(1)} %copy-done.46, f32[768]{0:T(1024)S(1)} %copy-done.50, ...), channel_id=1, replica_groups=mesh['dp'=8,'mp'=4] {'dp','mp'}, use_global_device_ids=true, to_apply=%region_28.29 | all-reduce | flops 5377 | bytes 43016 | tf_op jit(solution)/shard_map/psum | solution.py:228
  806.9 14.0 %all-reduce.1 = (f32[2,192]{1,0:T(2,128)}, f32[768]{0:T(1024)}) all-reduce(f32[2,192]{1,0:T(2,128)S(1)} %pad_maximum_fusion.2, f32[768]{0:T(1024)S(1)} %copy-done.53), channel_id=1, replica_groups=mesh['dp'=8,'mp'=4] {'dp'}, use_global_device_ids=true, to_apply=%region_25.26 | all-reduce | flops 1152 | bytes 9216 | tf_op jit(solution)/shard_map/psum | solution.py:225
  825.4 138.7 %all-reduce.6.cloned.1.call-done = f32[768,768]{1,0:T(8,128)} async-done(((f32[768,768]{1,0:T(8,128)}), f32[768,768]{1,0:T(8,128)}) %all-reduce.6.cloned.1.call-update) | async-done | bytes 2359312 | tf_op jit(solution)/shard_map/psum | solution.py:228
  964.1 117.6 %all-reduce.8.cloned.1.call-done = (f32[3,768,192]{1,2,0:T(8,128)}, f32[192,768]{1,0:T(8,128)}, f32[768,768]{1,0:T(8,128)}, f32[768,768]{1,0:T(8,128)}) async-done(((f32[3,768,192]{1,2,0:T(8,128)}, f32[192,768]{1,0:T(8,128)}, f32[768,768]{1,0:T(8,128)}, f32[768,768]{1,0:T(8,128)}), (f32[3,768,192]{1,2,0:T(8,128)}, f32[192,768]{1,0:T(8,128)}, f32[768,768]{1,0:T(8,128)}, ...) | async-done | bytes 7077904 | tf_op jit(solution)/shard_map/psum | solution.py:225
  (261 shorter events, 119.6 us)
Async XLA Ops:
  7.2 213.6 %copy-start = (bf16[768,768]{1,0:T(8,128)(2,1)S(1)}, bf16[768,768]{1,0:T(8,128)(2,1)}, u32[]{:S(2)}) copy-start(bf16[768,768]{1,0:T(8,128)(2,1)} %param.31) | copy-start | bytes 3538948
  7.2 55.6 %all-gather.8.cloned.1.call-start = ((), (), s32[]{:S(2)}) async-start(), calls=%async_computation.4 | async-start | bytes 2949120 | tf_op jit(solution)/shard_map/all_gather | solution.py:80
  7.9 158.8 %reduce-scatter.5.cloned.1.call-start = ((), (), s32[]{:S(2)}) async-start(), calls=%async_computation.5 | async-start | bytes 5898240 | tf_op jit(solution)/shard_map/reduce_scatter | solution.py:104
  22.3 51.4 %copy-start.56 = (pred[24,64]{1,0:T(8,128)(4,1)}, pred[24,64]{1,0:T(8,128)(4,1)S(1)}, u32[]{:S(2)}) copy-start(pred[24,64]{1,0:T(8,128)(4,1)S(1)} %broadcast_in_dim.24) | copy-start | bytes 4612
  82.4 84.3 %copy-start.13 = (bf16[384,768]{1,0:T(8,128)(2,1)S(1)}, bf16[384,768]{1,0:T(8,128)(2,1)}, u32[]{:S(2)}) copy-start(bf16[384,768]{1,0:T(8,128)(2,1)} %param.21) | copy-start | bytes 1769476
  82.5 138.3 %all-gather.10.cloned.1.call-start = ((), (), s32[]{:S(2)}) async-start(), calls=%async_computation.6 | async-start | bytes 2949120 | tf_op jit(solution)/shard_map/all_gather | solution.py:110
  83.1 241.5 %copy-start.32 = (f32[768]{0:T(1024)}, f32[768]{0:T(1024)S(1)}, u32[]{:S(2)}) copy-start(f32[768]{0:T(1024)S(1)} %convert_element_type.127) | copy-start | bytes 9220
  83.1 86.4 %copy-start.41 = (f32[768]{0:T(1024)}, f32[768]{0:T(1024)S(1)}, u32[]{:S(2)}) copy-start(f32[768]{0:T(1024)S(1)} %convert_element_type.128) | copy-start | bytes 9220
  168.2 156.4 %copy-start.36 = (f32[384]{0:T(512)}, f32[384]{0:T(512)S(1)}, u32[]{:S(2)}) copy-start(f32[384]{0:T(512)S(1)} %broadcast_multiply_fusion.5) | copy-start | bytes 4612
  168.5 156.1 %copy-start.38 = (f32[384]{0:T(512)}, f32[384]{0:T(512)S(1)}, u32[]{:S(2)}) copy-start(f32[384]{0:T(512)S(1)} %add_rsqrt_fusion.1) | copy-start | bytes 4612
  169.6 155.0 %reduce-scatter.7.cloned.1.call-start = ((), (), s32[]{:S(2)}) async-start(), calls=%async_computation.7 | async-start | bytes 5898240 | tf_op jit(solution)/shard_map/reduce_scatter | solution.py:113
  169.9 64.8 %copy-start.54 = (f32[768]{0:T(1024)}, f32[768]{0:T(1024)S(1)}, u32[]{:S(2)}) copy-start(f32[768]{0:T(1024)S(1)} %convert_element_type.130) | copy-start | bytes 9220
  240.4 296.2 %all-gather.12.cloned.1.call-start = ((), (), s32[]{:S(2)}) async-start(), calls=%async_computation.8 | async-start | bytes 2949120 | tf_op jit(solution)/shard_map/all_gather | solution.py:169
  485.9 50.6 %copy-start.55 = (f32[768]{0:T(1024)S(1)}, f32[768]{0:T(1024)}, u32[]{:S(2)}) copy-start(f32[768]{0:T(1024)} %copy-done.54) | copy-start | bytes 9220
  487.8 145.1 %reduce-scatter.9.cloned.1.call-start = ((), (), s32[]{:S(2)}) async-start(), calls=%async_computation.9 | async-start | bytes 5898240 | tf_op jit(solution)/shard_map/reduce_scatter | solution.py:176
  548.7 84.3 %copy-start.3 = (f32[384,768]{1,0:T(8,128)S(1)}, f32[384,768]{1,0:T(8,128)}, u32[]{:S(2)}) copy-start(f32[384,768]{1,0:T(8,128)} %copy-done.2) | copy-start | bytes 3538948
  548.7 84.3 %copy-start.33 = (f32[768]{0:T(1024)S(1)}, f32[768]{0:T(1024)}, u32[]{:S(2)}) copy-start(f32[768]{0:T(1024)} %copy-done.32) | copy-start | bytes 9220
  548.7 139.9 %all-gather.14.cloned.1.call-start = ((), (), s32[]{:S(2)}) async-start(), calls=%async_computation.10 | async-start | bytes 2949120 | tf_op jit(solution)/shard_map/all_gather | solution.py:186
  636.5 52.1 %copy-start.25 = (bf16[192,768]{1,0:T(8,128)(2,1)S(1)}, bf16[192,768]{1,0:T(8,128)(2,1)}, u32[]{:S(2)}) copy-start(bf16[192,768]{1,0:T(8,128)(2,1)} %param.27) | copy-start | bytes 884740
  637.4 185.5 %reduce-scatter.11.cloned.1.call-start = ((), (), s32[]{:S(2)}) async-start(), calls=%async_computation.11 | async-start | bytes 5898240 | tf_op jit(solution)/shard_map/reduce_scatter | solution.py:217
  737.7 226.4 %all-reduce.6.cloned.1.call-start = ((), (), s32[]{:S(2)}) async-start(), calls=%async_computation.12 | async-start | bytes 4718592 | tf_op jit(solution)/shard_map/psum | solution.py:228
  740.3 341.4 %all-reduce.8.cloned.1.call-start = ((), (), s32[]{:S(2)}) async-start(), calls=%async_computation.13 | async-start | bytes 14155776 | tf_op jit(solution)/shard_map/psum | solution.py:225
  754.5 52.3 %copy-start.66 = (f32[3,64]{1,0:T(4,128)S(1)}, f32[3,64]{1,0:T(4,128)}, u32[]{:S(2)}) copy-start(f32[3,64]{1,0:T(4,128)} %get-tuple-element.86) | copy-start | bytes 2308
  754.5 52.4 %copy-start.53 = (f32[768]{0:T(1024)S(1)}, f32[768]{0:T(1024)}, u32[]{:S(2)}) copy-start(f32[768]{0:T(1024)} %get-tuple-element.88) | copy-start | bytes 9220
  (56 other events, 168.9 us)
Sparse Core Ops, SparseCore 0:
  9.6 53.1 all-gather.7
  82.6 84.0 reduce-scatter.4
  169.7 50.9 all-gather.9
  240.5 84.0 reduce-scatter.6
  488.0 48.5 all-gather.11
  548.8 84.0 reduce-scatter.8
  637.5 50.9 all-gather.13
  737.8 85.0 reduce-scatter.10
  828.5 135.5 all-reduce.5
  969.2 112.4 all-reduce.7
where the time goes:
time: 1110 us; the launch traced here: 1100 us
  waiting for transfers between devices  687 us (62%)
  blocking collectives  211 us (19%)
  matrix products  87.5 us (8%)
  local copies, waits for them, and re-layouts  54.9 us (5%)
  other arithmetic  31.9 us (3%)
  between operations  18.9 us (2%)
    psum x1, waiting for transfers between devices, on_device(): lax.psum((grad_b_attn, grad_norm1_gain, grad_norm1_bias, grad_b_out, grad...  139 us
    psum x1, waiting for transfers between devices, on_device(): lax.psum((grad_qkv, grad_b_qv, grad_attn, grad_w_in, grad_b_in, grad_w_ou...  118 us
    reduce_scatter x1, waiting for transfers between devices, on_device(): lax.psum_scatter(jnp.einsum('tf,df->td', grad_pre, w_in, preferred_elemen...  84.2 us
    reduce_scatter x1, waiting for transfers between devices, on_device(): lax.psum_scatter(jnp.dot(context, w_attn, preferred_element_type=f32), 'm...  83.5 us
    reduce_scatter x1, waiting for transfers between devices, on_device(): lax.psum_scatter(jnp.dot(hidden, w_out, preferred_element_type=f32), 'mp'...  79 us
    all_gather x1, blocking collectives, on_device(): lax.all_gather(tgt_own, ('dp', 'mp'), axis=0, tiled=True)  69.8 us
    all_gather x1, blocking collectives, on_device(): lax.all_gather(src_own, ('dp', 'mp'), axis=0, tiled=True)  65.7 us
    all_gather x1, waiting for transfers between devices, on_device(): lax.all_gather(normed_one.astype(jnp.bfloat16), 'mp', axis=0, tiled=True)  50.8 us
  transfers between devices with their start and end apart: 10, of which 10 were waited for; matrix products, arithmetic and copies ran while one was open for 2% of the time, Pallas kernels for 0%

commit v1 on v0

v1 whole, which is shorter than its diff:
```python
import jax
import jax.numpy as jnp
from jax import lax
from jax.sharding import PartitionSpec as P

HEAD_DIM = 64
SEQ = 64
SLICES = 8

eps_norm = 1e-12
margin = 0.3
step_rate = 1.0
masked_low = -1e30
high = lax.Precision.HIGHEST
f32 = jnp.float32
low = jnp.bfloat16


def norm_forward(rows_in, gain, shift):
    center = rows_in - jnp.mean(rows_in, axis=-1, keepdims=True)
    inv_std = lax.rsqrt(jnp.mean(center * center, axis=-1, keepdims=True) + eps_norm)
    normed = center * inv_std
    return (normed * gain + shift, normed, inv_std)


def norm_backward(grad_out, normed, inv_std, gain):
    scaled = grad_out * gain
    inner = (
        scaled
        - jnp.mean(scaled, axis=-1, keepdims=True)
        - normed * jnp.mean(scaled * normed, axis=-1, keepdims=True)
    )
    return (inv_std * inner, jnp.sum(grad_out * normed, axis=0), jnp.sum(grad_out, axis=0))


def gelu_slope(pre_act):
    return (
        0.5 * (1.0 + lax.erf(pre_act * 0.7071067811865476))
        + pre_act * jnp.exp(-0.5 * pre_act * pre_act) * 0.3989422804014327
    )


def rank_terms(cosine, same, diag_mask, weight, scale_value, axis_of):
    shifted = cosine - margin * diag_mask
    logits = jnp.where(same, scale_value * shifted, masked_low)
    top = jnp.max(logits, axis=axis_of, keepdims=True)
    lse = top + jnp.log(jnp.sum(jnp.exp(logits - top), axis=axis_of, keepdims=True))
    probs = jnp.exp(logits - lse)
    grad_logit = weight * (probs - diag_mask)
    return (grad_logit, grad_logit * shifted)


def make(mesh):
    n_dp = mesh.shape["dp"]
    n_mp = mesh.shape["mp"]

    def dpx(x, bit):
        return lax.ppermute(x, "dp", [(i, i ^ bit) for i in range(n_dp)])

    def mpx(x, bit):
        return lax.ppermute(x, "mp", [(i, i ^ bit) for i in range(n_mp)])

    def bit_of(axis, bit):
        return (lax.axis_index(axis) & bit) != 0

    def flips(v, axis, bits, dims):
        for bit, dim in zip(bits, dims):
            v = jnp.where(bit_of(axis, bit), jnp.flip(v, dim), v)
        return v

    def gather_plane(r):
        half = r.shape[1] // 2
        at_x, at_y = dpx(r, 2), dpx(r, 4)
        at_d = jnp.concatenate([dpx(at_y[:, :half], 2), dpx(at_x[:, half:], 4)], 1)
        z = jnp.stack([r, at_x, at_y, at_d])
        c = dpx(z, 1)
        v = jnp.stack([z, c], 1)
        return v.reshape((2, 2, 2) + r.shape)

    def gather_block(shard, tie):
        rows = shard.shape[0] // SLICES
        piece = lax.dynamic_slice_in_dim(shard, (lax.axis_index("dp") % SLICES) * rows, rows, 0)
        if tie is not None:
            piece, _ = lax.optimization_barrier((piece, tie))
        r = jnp.stack([mpx(piece, s) for s in range(1, n_mp)])
        v = gather_plane(r)
        v = flips(v, "dp", (4, 2, 1), (0, 1, 2))
        v = v.reshape((SLICES, n_mp - 1, rows, -1)).transpose(1, 0, 2, 3)
        v = v.reshape((n_mp - 1,) + shard.shape)
        return jnp.concatenate([shard[None], v], 0), r

    def reduce_block(g):
        rows = g.shape[1] // SLICES
        half = rows // 2
        v = g.reshape(n_mp, 2, 2, 2, rows, g.shape[2]).transpose(1, 2, 3, 0, 4, 5)
        v = flips(v, "dp", (4, 2, 1), (0, 1, 2)).astype(low)
        v = v[:, :, 0].astype(f32) + dpx(v[:, :, 1], 1).astype(f32)
        a, b = v[..., :half, :].astype(low), v[..., half:, :].astype(low)
        a = a[:, 0].astype(f32) + dpx(a[:, 1], 2).astype(f32)
        b = b[0].astype(f32) + dpx(b[1], 4).astype(f32)
        a, b = a.astype(low), b.astype(low)
        a = a[0].astype(f32) + dpx(a[1], 4).astype(f32)
        b = b[0].astype(f32) + dpx(b[1], 2).astype(f32)
        u = jnp.concatenate([a, b], 1)
        bit = SLICES
        while bit < n_dp:
            w = u.astype(low)
            u = w.astype(f32) + dpx(w, bit).astype(f32)
            bit *= 2
        w = u.astype(low)
        total = w[0].astype(f32)
        for s in range(1, n_mp):
            total = total + mpx(w[s], s).astype(f32)
        return total

    def regather(total):
        v = gather_plane(total.astype(low)[None])
        v = flips(v, "dp", (4, 2, 1), (0, 1, 2))
        return v.reshape(SLICES * total.shape[0], total.shape[1]).astype(f32)

    def sum_all(v):
        bit = 1
        while bit < n_dp:
            v = v + dpx(v, bit)
            bit *= 2
        bit = 1
        while bit < n_mp:
            v = v + mpx(v, bit)
            bit *= 2
        return v

    def mp_natural(v):
        bits = [1 << i for i in reversed(range(n_mp.bit_length() - 1))]
        shape = v.shape
        v = v.reshape((2,) * len(bits) + shape[1:])
        return flips(v, "mp", bits, range(len(bits))).reshape(shape)

    def gather_all(own):
        r = jnp.stack([own] + [mpx(own, s) for s in range(1, n_mp)])
        r = mp_natural(r)
        z = jnp.stack([r] + [dpx(r, b) for b in (2, 4, 6)])
        v = jnp.stack([z, dpx(z, 1)], 1).reshape((2, 2, 2) + r.shape)
        v = flips(v, "dp", (4, 2, 1), (0, 1, 2)).reshape((SLICES,) + r.shape)
        bit = SLICES
        while bit < n_dp:
            o = dpx(v, bit)
            up = bit_of("dp", bit)
            v = jnp.concatenate([jnp.where(up, o, v), jnp.where(up, v, o)], 0)
            bit *= 2
        return v.reshape((n_dp * n_mp,) + own.shape)

    def on_device(
        inputs,
        token_ids,
        out_cot,
        pair_ids,
        w_qkv,
        b_qv,
        w_attn,
        b_attn,
        norm1_gain,
        norm1_bias,
        w_in,
        b_in,
        w_out,
        b_out,
        norm2_gain,
        norm2_bias,
        w_pool,
        b_pool,
        scale,
    ):
        rows = inputs.shape[0]
        width = inputs.shape[1]
        cols = w_qkv.shape[2]
        heads = cols // HEAD_DIM
        sents = rows // SEQ
        gain_one = norm1_gain.astype(f32)
        gain_two = norm2_gain.astype(f32)

        small = jnp.concatenate([b_qv.reshape(-1), b_in])
        small = jnp.stack([small] + [mpx(small, s) for s in range(1, n_mp)]).astype(f32)
        b_q, b_v = small[:, :cols], small[:, cols : 2 * cols]
        b_mid = small[:, 2 * cols :]
        att_shard = jnp.concatenate([w_qkv.transpose(0, 2, 1).reshape(3 * cols, width), w_attn])
        att_all, tie = gather_block(att_shard, None)
        in_all, tie = gather_block(w_in.T, tie)
        out_all, _ = gather_block(w_out, tie)
        att_all = att_all.reshape(n_mp, 4, cols, width)

        qkv = jnp.einsum("td,skcd->kstc", inputs, att_all[:, :3], preferred_element_type=f32)
        biases = jnp.stack([b_q, jnp.zeros_like(b_q), b_v])[:, :, None, :]
        qkv = (qkv + biases).astype(low).reshape(3, n_mp, sents, SEQ, heads, HEAD_DIM)
        query, key_part, value_part = (qkv[0], qkv[1], qkv[2])
        valid = (token_ids != 0).reshape(1, sents, 1, 1, SEQ)
        raw = jnp.einsum("msqhd,mskhd->mshqk", query, key_part, preferred_element_type=f32)
        scores = jnp.where(valid, raw * 0.125, masked_low)
        top = jnp.max(scores, axis=-1, keepdims=True)
        expd = jnp.exp(scores - top)
        totals = jnp.sum(expd, axis=-1, keepdims=True)
        probs = expd / totals
        probs_low = probs.astype(low)
        context = jnp.einsum("mshqk,mskhd->msqhd", probs_low, value_part, preferred_element_type=f32)
        context = context.reshape(n_mp, rows, cols).astype(low)
        attn = jnp.einsum("mte,med->td", context, att_all[:, 3], preferred_element_type=f32)
        normed_one, hat_one, inv_one = norm_forward(
            inputs.astype(f32) + attn + b_attn.astype(f32), gain_one, norm1_bias.astype(f32)
        )
        normed_low = normed_one.astype(low)
        pre_act = jnp.einsum("td,mfd->mtf", normed_low, in_all, preferred_element_type=f32)
        pre_act = pre_act + b_mid[:, None, :]
        hidden = jax.nn.gelu(pre_act, approximate=False).astype(low)
        ffn = jnp.einsum("mtf,mfd->td", hidden, out_all, preferred_element_type=f32)
        out_rows, hat_two, inv_two = norm_forward(
            normed_one + ffn + b_out.astype(f32), gain_two, norm2_bias.astype(f32)
        )
        layer_out = out_rows.astype(low)

        own_first = layer_out.reshape(sents, SEQ, width)[:, 0, :]
        n_all = n_dp * n_mp
        first_rows = gather_all(own_first).reshape(n_all * sents, width)
        npairs = n_all * sents // 2
        pooled = jnp.tanh(
            jnp.dot(first_rows, w_pool, preferred_element_type=f32) + b_pool.astype(f32)
        )
        inv_len = lax.rsqrt(jnp.sum(pooled * pooled, axis=-1, keepdims=True) + eps_norm)
        emb_full = pooled * inv_len
        emb_pairs = emb_full.astype(low).reshape(npairs, 2, width)
        all_src, all_tgt = emb_pairs[:, 0, :], emb_pairs[:, 1, :]
        scale_value = scale[0]
        cosine = jnp.einsum("kd,md->km", all_src, all_tgt, preferred_element_type=f32)
        same = pair_ids[:, None] == pair_ids[None, :]
        counts = jnp.sum(same.astype(f32), axis=1)
        index_all = jnp.arange(npairs)
        diag_mask = (index_all[:, None] == index_all[None, :]).astype(f32)
        grad_row, part_row = rank_terms(
            cosine, same, diag_mask, (1.0 / counts)[:, None], scale_value, 1
        )
        grad_col, part_col = rank_terms(
            cosine, same, diag_mask, (1.0 / counts)[None, :], scale_value, 0
        )
        grad_all = grad_row + grad_col
        grad_src = scale_value * jnp.dot(grad_all, all_tgt.astype(f32), precision=high)
        grad_tgt = scale_value * jnp.einsum(
            "km,kd->md", grad_all, all_src.astype(f32), precision=high
        )
        new_scale = scale - step_rate * (jnp.sum(part_row) + jnp.sum(part_col))
        grad_emb = jnp.stack([grad_src, grad_tgt], axis=1).reshape(2 * npairs, width)
        grad_pooled = inv_len * (
            grad_emb - emb_full * jnp.sum(emb_full * grad_emb, axis=-1, keepdims=True)
        )
        grad_ppre = (grad_pooled * (1.0 - pooled * pooled)).astype(low)
        grad_pool = jnp.einsum("sd,se->de", first_rows, grad_ppre, preferred_element_type=f32)
        grad_b_pool = jnp.sum(grad_ppre.astype(f32), axis=0)
        own_ppre = lax.dynamic_slice_in_dim(
            grad_ppre, lax.axis_index(("dp", "mp")) * sents, sents, 0
        )
        grad_first = jnp.einsum("se,de->sd", own_ppre, w_pool, preferred_element_type=f32)
        grad_out = out_cot.astype(f32).reshape(sents, SEQ, width)
        grad_out = grad_out.at[:, 0, :].add(grad_first).reshape(rows, width)

        grad_z2, grad_norm2_gain, grad_norm2_bias = norm_backward(
            grad_out, hat_two, inv_two, gain_two
        )
        grad_b_out = jnp.sum(grad_z2, axis=0)
        grad_ffn = grad_z2.astype(low)
        grad_w_out = jnp.einsum("mtf,td->mfd", hidden, grad_ffn, preferred_element_type=f32)
        red_out = reduce_block(grad_w_out)
        grad_hidden = jnp.einsum("td,mfd->mtf", grad_ffn, out_all, preferred_element_type=f32)
        grad_pre = (grad_hidden * gelu_slope(pre_act)).astype(low)
        grad_b_in = jnp.sum(grad_pre.astype(f32), axis=1)
        grad_w_in = jnp.einsum("mtf,td->mfd", grad_pre, normed_low, preferred_element_type=f32)
        red_in = reduce_block(grad_w_in)
        grad_h1 = grad_z2 + jnp.einsum(
            "mtf,mfd->td", grad_pre, in_all, preferred_element_type=f32
        )
        grad_z1, grad_norm1_gain, grad_norm1_bias = norm_backward(
            grad_h1, hat_one, inv_one, gain_one
        )
        grad_b_attn = jnp.sum(grad_z1, axis=0)
        grad_att_low = grad_z1.astype(low)
        grad_attn = jnp.einsum("mte,td->med", context, grad_att_low, preferred_element_type=f32)
        grad_context = jnp.einsum(
            "td,med->mte", grad_att_low, att_all[:, 3], preferred_element_type=f32
        )
        grad_context = grad_context.astype(low).reshape(n_mp, sents, SEQ, heads, HEAD_DIM)
        grad_value = jnp.einsum(
            "mshqk,msqhd->mskhd", probs_low, grad_context, preferred_element_type=f32
        )
        grad_probs = jnp.einsum(
            "msqhd,mskhd->mshqk", grad_context, value_part, preferred_element_type=f32
        )
        inner_sum = jnp.sum(probs * grad_probs, axis=-1, keepdims=True)
        grad_raw = jnp.where(valid, probs * (grad_probs - inner_sum) * 0.125, 0.0).astype(low)
        grad_query = jnp.einsum("mshqk,mskhd->msqhd", grad_raw, key_part, preferred_element_type=f32)
        grad_key = jnp.einsum("mshqk,msqhd->mskhd", grad_raw, query, preferred_element_type=f32)
        grad_rows = (
            jnp.stack([grad_query, grad_key, grad_value], 1).astype(low).reshape(n_mp, 3, rows, cols)
        )
        grad_b_qv = jnp.sum(grad_rows[:, 0::2].astype(f32), axis=2)
        grad_qkv = jnp.einsum("mkte,td->mked", grad_rows, inputs, preferred_element_type=f32)
        grad_att = jnp.concatenate([grad_qkv, grad_attn[:, None]], 1).reshape(
            n_mp, 4 * cols, width
        )
        red_att = reduce_block(grad_att)
        input_grad = grad_z1 + jnp.einsum(
            "mkte,mked->td", grad_rows, att_all[:, :3], preferred_element_type=f32
        )
        late = jnp.concatenate(
            [mp_natural(grad_b_qv).reshape(-1), grad_b_attn, grad_norm1_gain, grad_norm1_bias]
        )
        early = jnp.concatenate(
            [mp_natural(grad_b_in).reshape(-1), grad_b_out, grad_norm2_gain, grad_norm2_bias]
        )
        late, early = sum_all(late), sum_all(early)
        n_qv, n_in = n_mp * 2 * cols, early.shape[0] - 3 * width
        take = lax.axis_index("mp")
        out_b_qv = lax.dynamic_slice_in_dim(late[:n_qv].reshape(n_mp, 2, cols), take, 1, 0)[0]
        out_b_in = lax.dynamic_slice_in_dim(early[:n_in].reshape(n_mp, -1), take, 1, 0)[0]
        late, early = late[n_qv:].reshape(3, width), early[n_in:].reshape(3, width)
        done_out = regather(red_out)
        done_in = regather(red_in).T
        done_att = regather(red_att)
        done_qkv = done_att[: 3 * cols].reshape(3, cols, width).transpose(0, 2, 1)
        return (
            layer_out,
            input_grad,
            done_qkv,
            out_b_qv,
            done_att[3 * cols :],
            late[0],
            late[1],
            late[2],
            done_in,
            out_b_in,
            done_out,
            early[0],
            early[1],
            early[2],
            grad_pool,
            grad_b_pool,
            new_scale,
        )

    return on_device


def solution(mesh):
    rows, whole = P(("dp", "mp"), None), P()
    in_specs = (
        rows,
        P(("dp", "mp")),
        rows,
        whole,
        P(None, None, "mp"),
        P(None, "mp"),
        P("mp", None),
        whole,
        whole,
        whole,
        P(None, "mp"),
        P("mp"),
        P("mp", None),
        whole,
        whole,
        whole,
        whole,
        whole,
        whole,
    )
    out_specs = (
        rows,
        rows,
        P(None, None, "mp"),
        P(None, "mp"),
        P("mp", None),
        whole,
        whole,
        whole,
        P(None, "mp"),
        P("mp"),
        P("mp", None),
        whole,
        whole,
        whole,
        whole,
        whole,
        whole,
    )
    return jax.shard_map(
        make(mesh), mesh=mesh, in_specs=in_specs, out_specs=out_specs, check_vma=False
    )
```

time: 1110 us -> 452 us (0.41)
  waiting for transfers between devices: 687 us -> 101 us
  blocking collectives: 211 us -> 0 us
  starting transfers between devices: 9.51 us -> 98.6 us
  other arithmetic: 31.9 us -> 86.9 us
  between operations: 18.9 us -> 6.35 us
    psum x2 -> x0, waiting for transfers between devices: 256 us -> none  [the longest x1 139 us: on_device(): lax.psum((grad_b_attn, grad_norm1_gain, grad_norm1_bias, grad_b_out, grad...]
    reduce_scatter x4 -> x0, waiting for transfers between devices: 249 us -> none  [the longest x1 84.2 us: on_device(): lax.psum_scatter(jnp.einsum('tf,df->td', grad_pre, w_in, preferred_elemen...]
    all_gather x4 -> x0, waiting for transfers between devices: 181 us -> none  [the longest x1 50.8 us: on_device(): lax.all_gather(normed_one.astype(jnp.bfloat16), 'mp', axis=0, tiled=True)]
    all_gather x3 -> x0, blocking collectives: 149 us -> none  [the longest x1 69.8 us: on_device(): lax.all_gather(tgt_own, ('dp', 'mp'), axis=0, tiled=True)]
    ppermute x0 -> x83, waiting for transfers between devices: none -> 101 us  [the longest x55 71 us: dpx(): return lax.ppermute(x, 'dp', [(i, i ^ bit) for i in range(n_dp)])]
    ppermute x0 -> x83, starting transfers between devices: none -> 98.6 us  [the longest x55 52.3 us: dpx(): return lax.ppermute(x, 'dp', [(i, i ^ bit) for i in range(n_dp)])]
    psum x2 -> x0, blocking collectives: 61.5 us -> none  [the longest x1 47.5 us: on_device(): lax.psum((grad_b_attn, grad_norm1_gain, grad_norm1_bias, grad_b_out, grad...]
    select_n x0 -> x32, other arithmetic: none -> 31.3 us  [flips(): v = jnp.where(bit_of(axis, bit), jnp.flip(v, dim), v)]
  transfers between devices with their start and end apart: 10 -> 83, of which waited for: 10 -> 35; matrix products, arithmetic and copies ran while one was open for 2% -> 30% of each run, Pallas kernels for 0% -> 0%
where the time goes in v1:
time: 452 us; the launch traced here: 443 us
  waiting for transfers between devices  101 us (22%)
  starting transfers between devices  98.6 us (22%)
  other arithmetic  86.9 us (19%)
  matrix products  85 us (19%)
  local copies, waits for them, and re-layouts  65.1 us (14%)
  between operations  6.35 us (1%)
    ppermute x55, waiting for transfers between devices, dpx(): return lax.ppermute(x, 'dp', [(i, i ^ bit) for i in range(n_dp)])  71 us
    ppermute x55, starting transfers between devices, dpx(): return lax.ppermute(x, 'dp', [(i, i ^ bit) for i in range(n_dp)])  52.3 us
    ppermute x28, starting transfers between devices, mpx(): return lax.ppermute(x, 'mp', [(i, i ^ bit) for i in range(n_mp)])  46.3 us
    select_n x32, other arithmetic, flips(): v = jnp.where(bit_of(axis, bit), jnp.flip(v, dim), v)  31.3 us
    ppermute x28, waiting for transfers between devices, mpx(): return lax.ppermute(x, 'mp', [(i, i ^ bit) for i in range(n_mp)])  30.4 us
    dot_general x1, matrix products, on_device(): jnp.einsum('td,mfd->mtf', normed_low, in_all, preferred_element_type=f32)  22.9 us
    unnamed x201, local copies, waits for them, and re-layouts  15.1 us
  transfers between devices with their start and end apart: 83, of which 35 were waited for; matrix products, arithmetic and copies ran while one was open for 30% of the time, Pallas kernels for 0%

profile of v1, /device:TPU:0, one launch (start us, length us, event | category | flops | bytes accessed | tf_op | source)
XLA Modules:
  0.0 443.4 jit_solution(10484175440407273289)
XLA Ops:
  1.8 5.1 %collective-permute-start.2 = (bf16[96,768]{1,0:T(8,128)(2,1)S(1)}, bf16[96,768]{1,0:T(8,128)(2,1)S(1)}, u32[]{:S(2)}, u32[]{:S(2)}) collective-permute-start(bf16[96,768]{1,0:T(8,128)(2,1)S(1)} %fusion.134), channel_id=1, source_target_pairs={{0,3},{1,2},{2,1},{3,0},{4,7},{5,6},{6,5},{7,4},{8,11},{9,10},{10,... | collective-permute-start | bytes 442376 | tf_op jit(solution)/shard_map/ppermute | solution.py:61
  7.5 4.1 collective-permute-done.2
  11.7 7.7 %collective-permute-done.1 = bf16[96,768]{1,0:T(8,128)(2,1)S(1)} collective-permute-done((bf16[96,768]{1,0:T(8,128)(2,1)S(1)}, bf16[96,768]{1,0:T(8,128)(2,1)S(1)}, u32[]{:S(2)}, u32[]{:S(2)}) %collective-permute-start.1) | collective-permute-done | bytes 147488 | tf_op jit(solution)/shard_map/ppermute | solution.py:61
  22.5 8.2 %collective-permute-done.4 = bf16[3,96,768]{2,1,0:T(8,128)(2,1)S(1)} collective-permute-done((bf16[3,96,768]{2,1,0:T(8,128)(2,1)S(1)}, bf16[3,96,768]{2,1,0:T(8,128)(2,1)S(1)}, u32[]{:S(2)}, u32[]{:S(2)}) %collective-permute-start.4) | collective-permute-done | bytes 442400 | tf_op jit(solution)/shard_map/ppermute | solution.py:58
  74.0 5.8 %collective-permute-done.15 = bf16[3,96,768]{2,1,0:T(8,128)(2,1)S(1)} collective-permute-done((bf16[3,96,768]{2,1,0:T(8,128)(2,1)}, bf16[3,96,768]{2,1,0:T(8,128)(2,1)S(1)}, u32[]{:S(2)}, u32[]{:S(2)}) %collective-permute-start.15) | collective-permute-done | bytes 442400 | tf_op jit(solution)/shard_map/ppermute | solution.py:58
  82.0 7.8 %collective-permute-done.22 = bf16[3,96,768]{2,1,0:T(8,128)(2,1)S(1)} collective-permute-done((bf16[3,96,768]{2,1,0:T(8,128)(2,1)S(1)}, bf16[3,96,768]{2,1,0:T(8,128)(2,1)S(1)}, u32[]{:S(2)}, u32[]{:S(2)}) %collective-permute-start.22) | collective-permute-done | bytes 442400 | tf_op jit(solution)/shard_map/ppermute | solution.py:58
  113.0 4.6 %fusion.207 = (f32[4,6,3,64]{3,2,1,0:T(4,128)S(1)}, f32[4,6,3,64,64]{3,4,2,1,0:T(8,128)}) fusion(pred[6,64]{1,0:T(8,128)(4,1)S(1)} %copy-done.85, bf16[4,6,64,3,64]{2,1,4,3,0:T(8,128)(2,1)} %squeeze.129, bf16[4,6,64,3,64]{2,1,4,3,0:T(8,128)(2,1)} %squeeze.128), kind=kOutput, calls=%fused_computation.408 | convolution fusion | flops 38928448 | bytes 2378112 | tf_op jit(solution)/shard_map/sub | solution.py:199
  131.0 22.9 %fusion.7 = (bf16[4,384,768]{2,1,0:T(8,128)(2,1)S(1)}, f32[4,768,384]{1,2,0:T(8,128)}) fusion(f32[4,768]{1,0:T(4,128)S(1)} %fusion.163, f32[384,768]{1,0:T(8,128)S(1)} %get-tuple-element.142, f32[768]{0:T(1024)S(1)} %copy-done.69, f32[768]{0:T(1024)S(1)} %convert_element_type.346, f32[384]{0:T(512)S(1)} %add_rsqrt_fusion.1, ...), kind=kOutput, calls=%fused_computation.28 | convolution fusion | flops 1893629952 | bytes 12997632 | tf_op jit(solution)/shard_map/td,mfd->mtf/dot_general | solution.py:210
  207.8 5.6 %convert_reduce_fusion = (f32[4,768]{1,0:T(4,128)S(1)}, bf16[4,384,768]{2,1,0:T(8,128)(2,1)S(1)}) fusion(f32[4,768,384]{1,2,0:T(8,128)} %get-tuple-element.144, f32[4,768]{1,0:T(4,128)} %copy-done.62, f32[384,768]{1,0:T(8,128)S(1)} %get-tuple-element.100, bf16[3,768,768]{2,1,0:T(8,128)(2,1)S(1)} %bitcast.496, bf16[1,768,768]{2,1,0:T(8,128)(2,1)} %bitcast.551), kind=kOutput, calls=%fused_computation.54 | convolution fusion | flops 1829925888 | bytes 13000704 | tf_op jit(solution)/shard_map/td,mfd->mtf/dot_general | solution.py:269
  219.8 4.5 %fusion.191 = bf16[4,768,768]{2,1,0:T(8,128)(2,1)} fusion(bf16[4,384,768]{2,1,0:T(8,128)(2,1)S(1)} %get-tuple-element.153, f32[384,768]{1,0:T(8,128)S(1)} %copy-done.9, f32[768]{0:T(1024)S(1)} %copy-done.70, f32[768]{0:T(1024)S(1)} %copy-done.55, f32[384]{0:T(512)S(1)} %copy-done.64, f32[384]{0:T(512)S(1)} %copy-done.50), kind=kOutput, calls=%fused_computation.394 | convolution fusion | flops 1813413888 | bytes 8266752 | tf_op jit(solution)/shard_map/mtf,td->mfd/dot_general | solution.py:272
  230.3 6.4 %fusion.54 = bf16[4,6,64,3,64]{2,4,3,1,0:T(8,128)(2,1)} fusion(f32[4,6,3,64,64]{3,4,2,1,0:T(8,128)} %fusion.97, pred[6,64]{1,0:T(8,128)(4,1)S(1)} %copy-done.86, bf16[4,6,64,3,64]{2,1,4,3,0:T(8,128)(2,1)} %squeeze.129, f32[4,6,3,64,64]{3,4,2,1,0:T(8,128)} %get-tuple-element.140, f32[4,6,3,64]{3,2,1,0:T(4,128)S(1)} %copy-done.91), kind=kOutput, calls=%fused_computation.118 | convolution fusion | flops 40407616 | bytes 3557760 | tf_op jit(solution)/shard_map/mshqk,mskhd->msqhd/dot_general | solution.py:295
  236.8 6.0 %fusion.57 = bf16[4,6,64,3,64]{2,4,3,1,0:T(8,128)(2,1)} fusion(f32[4,6,3,64,64]{3,4,2,1,0:T(8,128)} %fusion.97, pred[6,64]{1,0:T(8,128)(4,1)S(1)} %copy-done.86, bf16[4,6,64,3,64]{2,1,4,3,0:T(8,128)(2,1)S(1)} %copy-done.24, f32[4,6,3,64,64]{3,4,2,1,0:T(8,128)} %get-tuple-element.140, f32[4,6,3,64]{3,2,1,0:T(4,128)S(1)} %copy-done.91), kind=kOutput, calls=%fused_computation.119 | convolution fusion | flops 40407616 | bytes 3557760 | tf_op jit(solution)/shard_map/mshqk,msqhd->mskhd/dot_general | solution.py:296
  255.7 4.5 %fusion.70 = f32[384,768]{1,0:T(8,128)} fusion(f32[384,768]{1,0:T(8,128)S(1)} %get-tuple-element.102, bf16[4,3,384,192]{2,3,0,1:T(8,128)(2,1)S(1)} %constant_dynamic-update-slice_fusion, bf16[3,4,192,768]{3,2,1,0:T(8,128)(2,1)} %bitcast.486, bf16[1,4,192,768]{3,2,1,0:T(8,128)(2,1)S(1)} %bitcast.490), kind=kOutput, calls=%fused_computation.129 | convolution fusion | flops 1361018880 | bytes 8847360 | tf_op jit(solution)/shard_map/mkte,mked->td/dot_general | solution.py:306
  260.6 4.3 fusion.116
  264.9 3.8 fusion.48
  270.5 12.4 %reverse_select_fusion.2 = (bf16[2,2,2,4,96,768]{5,4,2,1,0,3:T(8,128)(2,1)}, bf16[2,2,2,4,96,768]{5,4,2,1,0,3:T(8,128)(2,1)S(1)}) fusion(bf16[2,2,2,4,96,768]{5,4,2,1,0,3:T(8,128)(2,1)} %bitcast.492, pred[]{:T(512)S(6)} %ne.26, bf16[2,2,2,4,96,768]{5,4,2,1,0,3:T(8,128)(2,1)} %bitcast.491), kind=kLoop, calls=%fused_computation.4 | loop fusion | flops 4718592 | bytes 18874368 | tf_op jit(solution)/shard_map/jit(_where)/select_n | solution.py:68
  282.9 5.5 %reverse_select_fusion.1 = bf16[2,2,2,4,96,768]{5,4,2,1,0,3:T(8,128)(2,1)S(1)} fusion(bf16[2,2,2,4,96,768]{5,4,2,1,0,3:T(8,128)(2,1)} %get-tuple-element.154, pred[]{:T(512)S(6)} %ne.25), kind=kLoop, calls=%fused_computation.3 | loop fusion | flops 2359296 | bytes 9437185 | tf_op jit(solution)/shard_map/jit(_where)/select_n | solution.py:68
  338.4 6.5 %collective-permute-done.73 = bf16[2,4,48,768]{3,2,0,1:T(8,128)(2,1)S(1)} collective-permute-done((bf16[2,4,48,768]{3,2,0,1:T(8,128)(2,1)S(1)}, bf16[2,4,48,768]{3,2,0,1:T(8,128)(2,1)S(1)}, u32[]{:S(2)}, u32[]{:S(2)}) %collective-permute-start.73) | collective-permute-done | bytes 589856 | tf_op jit(solution)/shard_map/ppermute | solution.py:58
  347.9 9.6 %collective-permute-done.37 = bf16[2,4,48,768]{3,2,0,1:T(8,128)(2,1)S(1)} collective-permute-done((bf16[2,4,48,768]{3,2,0,1:T(8,128)(2,1)S(1)}, bf16[2,4,48,768]{3,2,0,1:T(8,128)(2,1)S(1)}, u32[]{:S(2)}, u32[]{:S(2)}) %collective-permute-start.37) | collective-permute-done | bytes 589856 | tf_op jit(solution)/shard_map/ppermute | solution.py:58
  360.5 9.6 %collective-permute-done.55 = bf16[2,4,48,768]{3,2,0,1:T(8,128)(2,1)S(1)} collective-permute-done((bf16[2,4,48,768]{3,2,0,1:T(8,128)(2,1)S(1)}, bf16[2,4,48,768]{3,2,0,1:T(8,128)(2,1)S(1)}, u32[]{:S(2)}, u32[]{:S(2)}) %collective-permute-start.55) | collective-permute-done | bytes 589856 | tf_op jit(solution)/shard_map/ppermute | solution.py:58
  373.2 4.8 %collective-permute-done.74 = bf16[4,48,768]{2,1,0:T(8,128)(2,1)S(1)} collective-permute-done((bf16[4,48,768]{2,1,0:T(8,128)(2,1)S(1)}, bf16[4,48,768]{2,1,0:T(8,128)(2,1)S(1)}, u32[]{:S(2)}, u32[]{:S(2)}) %collective-permute-start.74) | collective-permute-done | bytes 294944 | tf_op jit(solution)/shard_map/ppermute | solution.py:58
  388.0 3.9 collective-permute-done.39
  396.4 9.2 %collective-permute-start.57 = (bf16[96,768]{1,0:T(8,128)(2,1)S(1)}, bf16[96,768]{1,0:T(8,128)(2,1)S(1)}, u32[]{:S(2)}, u32[]{:S(2)}) collective-permute-start(bf16[96,768]{1,0:T(8,128)(2,1)S(1)} %get-tuple-element.115), channel_id=1, source_target_pairs={{0,1},{1,0},{2,3},{3,2},{4,5},{5,4},{6,7},{7,6},{8,9},{9,8},{10,11... | collective-permute-start | bytes 442376 | tf_op jit(solution)/shard_map/ppermute | solution.py:61
  412.8 4.5 %collective-permute-done.43 = bf16[1,96,768]{2,1,0:T(8,128)(2,1)S(1)} collective-permute-done((bf16[1,96,768]{2,1,0:T(8,128)(2,1)S(1)}, bf16[1,96,768]{2,1,0:T(8,128)(2,1)S(1)}, u32[]{:S(2)}, u32[]{:S(2)}) %collective-permute-start.43) | collective-permute-done | bytes 147488 | tf_op jit(solution)/shard_map/ppermute | solution.py:58
  (589 shorter events, 269.6 us)
Async XLA Ops:
  44.5 54.4 %collective-permute-start.7 = (bf16[4,3,96,768]{3,2,1,0:T(8,128)(2,1)S(1)}, bf16[4,3,96,768]{3,2,1,0:T(8,128)(2,1)}, u32[]{:S(2)}, u32[]{:S(2)}) collective-permute-start(bf16[4,3,96,768]{3,2,1,0:T(8,128)(2,1)S(1)} %pad_maximum_fusion.13), channel_id=1, source_target_pairs={{0,4},{4,0},{8,12},{12,8},{16,20},{20,16},{24,28},{28,24},{1,5},{5... | collective-permute-start | bytes 5308424 | tf_op jit(solution)/shard_map/ppermute | solution.py:58
  70.8 19.0 %collective-permute-start.22 = (bf16[3,96,768]{2,1,0:T(8,128)(2,1)S(1)}, bf16[3,96,768]{2,1,0:T(8,128)(2,1)S(1)}, u32[]{:S(2)}, u32[]{:S(2)}) collective-permute-start(bf16[3,96,768]{2,1,0:T(8,128)(2,1)S(1)} %get-tuple-element.122), channel_id=1, source_target_pairs={{0,8},{4,12},{8,0},{12,4},{16,24},{20,28},{24,16},{28,20},{1,9},{5... | collective-permute-start | bytes 1327112 | tf_op jit(solution)/shard_map/ppermute | solution.py:58
  72.4 19.1 %collective-permute-start.23 = (bf16[3,96,768]{2,1,0:T(8,128)(2,1)S(1)}, bf16[3,96,768]{2,1,0:T(8,128)(2,1)S(1)}, u32[]{:S(2)}, u32[]{:S(2)}) collective-permute-start(bf16[3,96,768]{2,1,0:T(8,128)(2,1)S(1)} %get-tuple-element.122), channel_id=1, source_target_pairs={{0,16},{4,20},{8,24},{12,28},{16,0},{20,4},{24,8},{28,12},{1,17},{... | collective-permute-start | bytes 1327112 | tf_op jit(solution)/shard_map/ppermute | solution.py:58
  95.9 28.9 %collective-permute-start.18 = (bf16[4,3,96,768]{3,2,1,0:T(8,128)(2,1)}, bf16[4,3,96,768]{3,2,1,0:T(8,128)(2,1)}, u32[]{:S(2)}, u32[]{:S(2)}) collective-permute-start(bf16[4,3,96,768]{3,2,1,0:T(8,128)(2,1)} %pad_maximum_fusion.14), channel_id=1, source_target_pairs={{0,4},{4,0},{8,12},{12,8},{16,20},{20,16},{24,28},{28,24},{1,5},{5... | collective-permute-start | bytes 5308424 | tf_op jit(solution)/shard_map/ppermute | solution.py:58
  98.9 55.0 %collective-permute-start.26 = (bf16[4,3,96,768]{3,2,1,0:T(8,128)(2,1)}, bf16[4,3,96,768]{3,2,1,0:T(8,128)(2,1)}, u32[]{:S(2)}, u32[]{:S(2)}) collective-permute-start(bf16[4,3,96,768]{3,2,1,0:T(8,128)(2,1)} %pad_maximum_fusion.15), channel_id=1, source_target_pairs={{0,4},{4,0},{8,12},{12,8},{16,20},{20,16},{24,28},{28,24},{1,5},{5... | collective-permute-start | bytes 5308424 | tf_op jit(solution)/shard_map/ppermute | solution.py:58
  269.8 36.8 %collective-permute-start.65 = (f32[5376]{0:T(1024)}, f32[5376]{0:T(1024)}, u32[]{:S(2)}, u32[]{:S(2)}) collective-permute-start(f32[5376]{0:T(1024)} %pad_maximum_fusion.43), channel_id=1, source_target_pairs={{0,4},{4,0},{8,12},{12,8},{16,20},{20,16},{24,28},{28,24},{1,5},{5... | collective-permute-start | bytes 64520 | tf_op jit(solution)/shard_map/ppermute | solution.py:58
  270.5 31.4 %collective-permute-start.47 = (f32[3840]{0:T(1024)S(1)}, f32[3840]{0:T(1024)S(1)}, u32[]{:S(2)}, u32[]{:S(2)}) collective-permute-start(f32[3840]{0:T(1024)S(1)} %pad_maximum_fusion.45), channel_id=1, source_target_pairs={{0,4},{4,0},{8,12},{12,8},{16,20},{20,16},{24,28},{28,24},{1,5},{5... | collective-permute-start | bytes 46088 | tf_op jit(solution)/shard_map/ppermute | solution.py:58
  298.6 26.6 %collective-permute-start.70 = (bf16[2,2,4,96,768]{4,3,1,0,2:T(8,128)(2,1)}, bf16[2,2,4,96,768]{4,3,1,0,2:T(8,128)(2,1)}, u32[]{:S(2)}, u32[]{:S(2)}) collective-permute-start(bf16[2,2,4,96,768]{4,3,1,0,2:T(8,128)(2,1)} %slice_bitcast_fusion), channel_id=1, source_target_pairs={{0,4},{4,0},{8,12},{12,8},{16,20},{20,16},{24,28},{28,24},{1,5},{5... | collective-permute-start | bytes 7077896 | tf_op jit(solution)/shard_map/ppermute | solution.py:58
  299.1 32.4 %collective-permute-start.34 = (bf16[2,2,4,96,768]{4,3,1,0,2:T(8,128)(2,1)}, bf16[2,2,4,96,768]{4,3,1,0,2:T(8,128)(2,1)S(1)}, u32[]{:S(2)}, u32[]{:S(2)}) collective-permute-start(bf16[2,2,4,96,768]{4,3,1,0,2:T(8,128)(2,1)} %slice_bitcast_fusion.4), channel_id=1, source_target_pairs={{0,4},{4,0},{8,12},{12,8},{16,20},{20,16},{24,28},{28,24},{1,5},{5... | collective-permute-start | bytes 7077896 | tf_op jit(solution)/shard_map/ppermute | solution.py:58
  305.1 27.2 %collective-permute-start.52 = (bf16[2,2,4,96,768]{4,3,1,0,2:T(8,128)(2,1)}, bf16[2,2,4,96,768]{4,3,1,0,2:T(8,128)(2,1)}, u32[]{:S(2)}, u32[]{:S(2)}) collective-permute-start(bf16[2,2,4,96,768]{4,3,1,0,2:T(8,128)(2,1)} %slice_bitcast_fusion.2), channel_id=1, source_target_pairs={{0,4},{4,0},{8,12},{12,8},{16,20},{20,16},{24,28},{28,24},{1,5},{5... | collective-permute-start | bytes 7077896 | tf_op jit(solution)/shard_map/ppermute | solution.py:58
  328.5 16.3 %collective-permute-start.73 = (bf16[2,4,48,768]{3,2,0,1:T(8,128)(2,1)S(1)}, bf16[2,4,48,768]{3,2,0,1:T(8,128)(2,1)S(1)}, u32[]{:S(2)}, u32[]{:S(2)}) collective-permute-start(bf16[2,4,48,768]{3,2,0,1:T(8,128)(2,1)S(1)} %slice_bitcast_fusion.6), channel_id=1, source_target_pairs={{0,16},{4,20},{8,24},{12,28},{16,0},{20,4},{24,8},{28,12},{1,17},{... | collective-permute-start | bytes 1769480 | tf_op jit(solution)/shard_map/ppermute | solution.py:58
  330.1 16.4 %collective-permute-start.71 = (bf16[2,4,48,768]{3,2,1,0:T(8,128)(2,1)S(1)}, bf16[2,4,48,768]{3,2,1,0:T(8,128)(2,1)S(1)}, u32[]{:S(2)}, u32[]{:S(2)}) collective-permute-start(bf16[2,4,48,768]{3,2,1,0:T(8,128)(2,1)S(1)} %bitcast.524), channel_id=1, source_target_pairs={{0,8},{4,12},{8,0},{12,4},{16,24},{20,28},{24,16},{28,20},{1,9},{5... | collective-permute-start | bytes 1769480 | tf_op jit(solution)/shard_map/ppermute | solution.py:58
  334.9 22.6 %collective-permute-start.37 = (bf16[2,4,48,768]{3,2,0,1:T(8,128)(2,1)S(1)}, bf16[2,4,48,768]{3,2,0,1:T(8,128)(2,1)S(1)}, u32[]{:S(2)}, u32[]{:S(2)}) collective-permute-start(bf16[2,4,48,768]{3,2,0,1:T(8,128)(2,1)S(1)} %slice_bitcast_fusion.10), channel_id=1, source_target_pairs={{0,16},{4,20},{8,24},{12,28},{16,0},{20,4},{24,8},{28,12},{1,17},{... | collective-permute-start | bytes 1769480 | tf_op jit(solution)/shard_map/ppermute | solution.py:58
  335.8 23.2 %collective-permute-start.35 = (bf16[2,4,48,768]{3,2,1,0:T(8,128)(2,1)S(1)}, bf16[2,4,48,768]{3,2,1,0:T(8,128)(2,1)S(1)}, u32[]{:S(2)}, u32[]{:S(2)}) collective-permute-start(bf16[2,4,48,768]{3,2,1,0:T(8,128)(2,1)S(1)} %bitcast.525), channel_id=1, source_target_pairs={{0,8},{4,12},{8,0},{12,4},{16,24},{20,28},{24,16},{28,20},{1,9},{5... | collective-permute-start | bytes 1769480 | tf_op jit(solution)/shard_map/ppermute | solution.py:58
  337.2 33.0 %collective-permute-start.55 = (bf16[2,4,48,768]{3,2,0,1:T(8,128)(2,1)S(1)}, bf16[2,4,48,768]{3,2,0,1:T(8,128)(2,1)S(1)}, u32[]{:S(2)}, u32[]{:S(2)}) collective-permute-start(bf16[2,4,48,768]{3,2,0,1:T(8,128)(2,1)S(1)} %slice_bitcast_fusion.8), channel_id=1, source_target_pairs={{0,16},{4,20},{8,24},{12,28},{16,0},{20,4},{24,8},{28,12},{1,17},{... | collective-permute-start | bytes 1769480 | tf_op jit(solution)/shard_map/ppermute | solution.py:58
  344.8 26.9 %collective-permute-start.53 = (bf16[2,4,48,768]{3,2,1,0:T(8,128)(2,1)S(1)}, bf16[2,4,48,768]{3,2,1,0:T(8,128)(2,1)S(1)}, u32[]{:S(2)}, u32[]{:S(2)}) collective-permute-start(bf16[2,4,48,768]{3,2,1,0:T(8,128)(2,1)S(1)} %bitcast.523), channel_id=1, source_target_pairs={{0,8},{4,12},{8,0},{12,4},{16,24},{20,28},{24,16},{28,20},{1,9},{5... | collective-permute-start | bytes 1769480 | tf_op jit(solution)/shard_map/ppermute | solution.py:58
  346.5 31.5 %collective-permute-start.74 = (bf16[4,48,768]{2,1,0:T(8,128)(2,1)S(1)}, bf16[4,48,768]{2,1,0:T(8,128)(2,1)S(1)}, u32[]{:S(2)}, u32[]{:S(2)}) collective-permute-start(bf16[4,48,768]{2,1,0:T(8,128)(2,1)S(1)} %slice_bitcast_fusion.12), channel_id=1, source_target_pairs={{0,8},{4,12},{8,0},{12,4},{16,24},{20,28},{24,16},{28,20},{1,9},{5... | collective-permute-start | bytes 884744 | tf_op jit(solution)/shard_map/ppermute | solution.py:58
  357.5 21.3 %collective-permute-start.72 = (bf16[4,48,768]{2,1,0:T(8,128)(2,1)S(1)}, bf16[4,48,768]{2,1,0:T(8,128)(2,1)S(1)}, u32[]{:S(2)}, u32[]{:S(2)}) collective-permute-start(bf16[4,48,768]{2,1,0:T(8,128)(2,1)S(1)} %slice_bitcast_fusion.14), channel_id=1, source_target_pairs={{0,16},{4,20},{8,24},{12,28},{16,0},{20,4},{24,8},{28,12},{1,17},{... | collective-permute-start | bytes 884744 | tf_op jit(solution)/shard_map/ppermute | solution.py:58
  359.1 22.9 %collective-permute-start.38 = (bf16[4,48,768]{2,1,0:T(8,128)(2,1)S(1)}, bf16[4,48,768]{2,1,0:T(8,128)(2,1)S(1)}, u32[]{:S(2)}, u32[]{:S(2)}) collective-permute-start(bf16[4,48,768]{2,1,0:T(8,128)(2,1)S(1)} %slice_bitcast_fusion.20), channel_id=1, source_target_pairs={{0,8},{4,12},{8,0},{12,4},{16,24},{20,28},{24,16},{28,20},{1,9},{5... | collective-permute-start | bytes 884744 | tf_op jit(solution)/shard_map/ppermute | solution.py:58
  378.9 31.5 %collective-permute-start.75 = (bf16[96,768]{1,0:T(8,128)(2,1)S(1)}, bf16[96,768]{1,0:T(8,128)(2,1)S(1)}, u32[]{:S(2)}, u32[]{:S(2)}) collective-permute-start(bf16[96,768]{1,0:T(8,128)(2,1)S(1)} %get-tuple-element.112), channel_id=1, source_target_pairs={{0,1},{1,0},{2,3},{3,2},{4,5},{5,4},{6,7},{7,6},{8,9},{9,8},{10,11... | collective-permute-start | bytes 442376 | tf_op jit(solution)/shard_map/ppermute | solution.py:61
  382.0 28.5 %collective-permute-start.77 = (bf16[96,768]{1,0:T(8,128)(2,1)S(1)}, bf16[96,768]{1,0:T(8,128)(2,1)S(1)}, u32[]{:S(2)}, u32[]{:S(2)}) collective-permute-start(bf16[96,768]{1,0:T(8,128)(2,1)S(1)} %get-tuple-element.113), channel_id=1, source_target_pairs={{0,3},{1,2},{2,1},{3,0},{4,7},{5,6},{6,5},{7,4},{8,11},{9,10},{10,... | collective-permute-start | bytes 442376 | tf_op jit(solution)/shard_map/ppermute | solution.py:61
  387.2 21.1 %collective-permute-start.40 = (bf16[96,768]{1,0:T(8,128)(2,1)S(1)}, bf16[96,768]{1,0:T(8,128)(2,1)S(1)}, u32[]{:S(2)}, u32[]{:S(2)}) collective-permute-start(bf16[96,768]{1,0:T(8,128)(2,1)S(1)} %get-tuple-element.120), channel_id=1, source_target_pairs={{0,2},{1,3},{2,0},{3,1},{4,6},{5,7},{6,4},{7,5},{8,10},{9,11},{10,... | collective-permute-start | bytes 442376 | tf_op jit(solution)/shard_map/ppermute | solution.py:61
  391.9 19.7 %collective-permute-start.76 = (bf16[96,768]{1,0:T(8,128)(2,1)S(1)}, bf16[96,768]{1,0:T(8,128)(2,1)S(1)}, u32[]{:S(2)}, u32[]{:S(2)}) collective-permute-start(bf16[96,768]{1,0:T(8,128)(2,1)S(1)} %get-tuple-element.114), channel_id=1, source_target_pairs={{0,2},{1,3},{2,0},{3,1},{4,6},{5,7},{6,4},{7,5},{8,10},{9,11},{10,... | collective-permute-start | bytes 442376 | tf_op jit(solution)/shard_map/ppermute | solution.py:61
  396.4 23.1 %collective-permute-start.57 = (bf16[96,768]{1,0:T(8,128)(2,1)S(1)}, bf16[96,768]{1,0:T(8,128)(2,1)S(1)}, u32[]{:S(2)}, u32[]{:S(2)}) collective-permute-start(bf16[96,768]{1,0:T(8,128)(2,1)S(1)} %get-tuple-element.115), channel_id=1, source_target_pairs={{0,1},{1,0},{2,3},{3,2},{4,5},{5,4},{6,7},{7,6},{8,9},{9,8},{10,11... | collective-permute-start | bytes 442376 | tf_op jit(solution)/shard_map/ppermute | solution.py:61
  (155 other events, 1529.4 us)

commit v2 on v1

v2 whole, which is shorter than its diff:
```python
import functools

import jax
import jax.numpy as jnp
from jax import lax
from jax.experimental import pallas as pl
from jax.experimental.pallas import tpu as pltpu
from jax.sharding import PartitionSpec as P

HEAD_DIM = 64
SEQ = 64
SLICES = 8
PARTS = 10
PAIR = 2 * SEQ
LANES = 2 * HEAD_DIM
BLOCK = 8

eps_norm = 1e-12
margin = 0.3
step_rate = 1.0
masked_low = -1e30
high = lax.Precision.HIGHEST
f32 = jnp.float32
low = jnp.bfloat16
VMEM_BYTES = 58 << 20


def nn(a, b):
    return jnp.dot(a, b, preferred_element_type=f32)


def nt(a, b):
    return lax.dot_general(a, b, (((1,), (1,)), ((), ())), preferred_element_type=f32)


def tn(a, b):
    return lax.dot_general(a, b, (((0,), (0,)), ((), ())), preferred_element_type=f32)


def rank_terms(cosine, same, diag_mask, weight, scale_value, axis_of):
    shifted = cosine - margin * diag_mask
    logits = jnp.where(same, scale_value * shifted, masked_low)
    top = jnp.max(logits, axis=axis_of, keepdims=True)
    lse = top + jnp.log(jnp.sum(jnp.exp(logits - top), axis=axis_of, keepdims=True))
    probs = jnp.exp(logits - lse)
    grad_logit = weight * (probs - diag_mask)
    return (grad_logit, grad_logit * shifted)


def call(body, ins, outs, scratch, micros):
    def spec(vmem):
        return pl.BlockSpec(memory_space=pltpu.VMEM if vmem else pl.ANY)

    return pl.pallas_call(
        body,
        out_shape=[jax.ShapeDtypeStruct(o.shape, o.dtype) for o, _ in outs],
        in_specs=[spec(v) for _, v in ins],
        out_specs=[spec(v) for _, v in outs],
        scratch_shapes=scratch,
        compiler_params=pltpu.CompilerParams(vmem_limit_bytes=VMEM_BYTES),
        cost_estimate=pl.CostEstimate(flops=int(micros * 1.1e9), bytes_accessed=0, transcendentals=0),
    )(*[a for a, _ in ins])


def slot(p):
    me = lax.rem(lax.axis_index("dp"), SLICES)
    return jnp.bitwise_xor(me, p)


def start_all(copies):
    for c in copies:
        c.start()
    return copies


def wait_all(copies):
    for c in copies:
        c.wait()


def att_spot(ref, s, p, cols, size, first=0, rows=None):
    at = slot(p)
    row = pl.multiple_of(s * cols + lax.rem(at, 2) * size + first, 16)
    return ref.at[at // 2, pl.ds(row, rows or size)]


def row_spot(ref, s, p, size, first=0, rows=None):
    return ref.at[s, pl.ds(pl.multiple_of(slot(p) * size + first, 16), rows or size)]


def slices_of(parts):
    full = parts[0].shape[-2]
    half = full // 2
    count = len(parts) // 2
    out = []
    for c in (0, 1):
        own, at_x, at_y, *rest = parts[count * c : count * (c + 1)]
        out += [(own, c, 0, full), (at_x, 2 + c, 0, full), (at_y, 4 + c, 0, full)]
        if len(rest) == 1:
            out += [(rest[0], 6 + c, 0, full)]
        else:
            out += [(rest[0], 6 + c, 0, half), (rest[1], 6 + c, half, half)]
    return out


def fetch_att(own_qkv, own_o, parts, dst, sem, cols):
    copies = []
    for i in range(3):
        copies.append(pltpu.make_async_copy(own_qkv.at[i], dst.at[i, pl.ds(0, cols)], sem.at[i]))
    copies.append(pltpu.make_async_copy(own_o, dst.at[3, pl.ds(0, cols)], sem.at[3]))
    k = 4
    size = parts[0].shape[1]
    for part, p, at, n in slices_of(parts):
        for s in range(part.shape[0]):
            spot = att_spot(dst, s + 1, p, cols, size, at, n)
            copies.append(pltpu.make_async_copy(part.at[s], spot, sem.at[k]))
            k += 1
    return start_all(copies)


def fetch_rows(own, parts, dst, sem, base):
    copies = [pltpu.make_async_copy(own, dst.at[0], sem.at[base])]
    k = base + 1
    size = parts[0].shape[1]
    for part, p, at, n in slices_of(parts):
        for s in range(part.shape[0]):
            spot = row_spot(dst, s + 1, p, size, at, n)
            copies.append(pltpu.make_async_copy(part.at[s], spot, sem.at[k]))
            k += 1
    return start_all(copies)


def n_copies(n_mp):
    return 4 + PARTS * (n_mp - 1)


def send_slices(src_of, g_keep, g_send, sem, n_mp):
    copies = []
    k = 0
    for p in range(SLICES):
        dst = g_send if p & 1 else g_keep
        for s in range(n_mp):
            spot = dst.at[s // 2, p >> 2, (p >> 1) & 1, s % 2]
            copies.append(pltpu.make_async_copy(src_of(s, p), spot, sem.at[k]))
            k += 1
    return start_all(copies)


def mean_of(v):
    return jnp.sum(v, axis=-1, keepdims=True) * (1.0 / v.shape[-1])


def norm_rows(z):
    center = z - mean_of(z)
    inv = lax.rsqrt(mean_of(center * center) + eps_norm)
    return center * inv, inv


def norm_back(grad_out, hat, inv, gain):
    scaled = grad_out * gain
    return inv * (scaled - mean_of(scaled) - hat * mean_of(scaled * hat))


def pair_mask(ids_row):
    row = lax.broadcasted_iota(jnp.int32, (PAIR, PAIR), 0) >= SEQ
    col = lax.broadcasted_iota(jnp.int32, (PAIR, PAIR), 1) >= SEQ
    return jnp.logical_and(row == col, ids_row != 0)


def split_heads(v):
    first = lax.broadcasted_iota(jnp.int32, v.shape, 1) < HEAD_DIM
    zero = jnp.zeros_like(v)
    return jnp.concatenate([jnp.where(first, v, zero), jnp.where(first, zero, v)], axis=0)


def join_heads(v):
    half = v.shape[0] // 2
    first = lax.broadcasted_iota(jnp.int32, (half, v.shape[1]), 1) < HEAD_DIM
    return jnp.where(first, v[:half], v[half:])


def softmax_of(scores, mask):
    scores = jnp.where(mask, scores * 0.125, masked_low)
    expd = jnp.exp(scores - jnp.max(scores, axis=-1, keepdims=True))
    return expd / jnp.sum(expd, axis=-1, keepdims=True)


def attention_forward(n_mp, cols, *refs):
    x, ids, b_q, b_v, b_attn, gain, shift, own_qkv, own_o = refs[:9]
    parts = refs[9 : 9 + PARTS]
    q, k, v, ctx, hat_out, inv_out, h1 = refs[19:26]
    w, sem = refs[26:]
    copies = fetch_att(own_qkv, own_o, parts, w, sem, cols)
    wait_all(copies)
    rows, width = x.shape
    q[...] = (nt(x[...], w[0]) + b_q[...]).astype(low)
    k[...] = nt(x[...], w[1]).astype(low)
    v[...] = (nt(x[...], w[2]) + b_v[...]).astype(low)

    @pl.loop(0, rows // PAIR)
    def _(t):
        at = pl.ds(pl.multiple_of(t * PAIR, PAIR), PAIR)
        mask = pair_mask(ids[t])
        for j in range(width // LANES):
            lanes = slice(j * LANES, (j + 1) * LANES)
            raw = nt(q[at, lanes], split_heads(k[at, lanes]))
            probs = [softmax_of(raw[:, i * PAIR : (i + 1) * PAIR], mask).astype(low) for i in (0, 1)]
            out = nn(jnp.concatenate(probs, axis=1), split_heads(v[at, lanes]))
            ctx[at, lanes] = out.astype(low)

    z = x[...].astype(f32) + nn(ctx[...], w[3]) + b_attn[...]
    hat, inv = norm_rows(z)
    hat_out[...] = hat
    inv_out[...] = jnp.broadcast_to(inv, inv_out.shape)
    h1[...] = (hat * gain[...] + shift[...]).astype(low)


def gelu_pair(pre):
    size = jnp.abs(pre)
    t = 1.0 / (1.0 + 0.2316418882663604 * size)
    bell = jnp.exp(-0.5 * pre * pre)
    poly = t * (
        0.127414796
        + t * (-0.142248368 + t * (0.7107068705 + t * (-0.7265760135 + t * 0.5307027145)))
    )
    tail = poly * bell
    phi = jnp.where(pre >= 0.0, 1.0 - tail, tail)
    return pre * phi, phi + pre * (bell * 0.3989422804014327)


def ffn_in_forward(n_mp, *refs):
    h1, b_mid, own_in = refs[:3]
    parts = refs[3 : 3 + SLICES]
    hidden, slope, w_in, sem = refs[11:]
    wait_all(fetch_rows(own_in, parts, w_in, sem, 0))

    @pl.loop(0, n_mp)
    def _(s):
        pre = nn(h1[...], w_in[s]) + b_mid[s]
        act, grad = gelu_pair(pre)
        hidden[s] = act.astype(low)
        slope[s] = grad.astype(low)


def ffn_out_forward(n_mp, *refs):
    hidden, hat1, gain1, shift1, b_out, gain2, shift2, own_out = refs[:8]
    parts = refs[8 : 8 + SLICES]
    layer_out, hat_out, inv_out, first = refs[16:20]
    w_out, acc, sem = refs[20:]
    copies = fetch_rows(own_out, parts, w_out, sem, 0)
    acc[...] = hat1[...] * gain1[...] + shift1[...] + b_out[...]
    wait_all(copies)

    @pl.loop(0, n_mp)
    def _(s):
        acc[...] += nn(hidden[s], w_out[s])

    hat, inv = norm_rows(acc[...])
    hat_out[...] = hat
    inv_out[...] = jnp.broadcast_to(inv, inv_out.shape)
    out = (hat * gain2[...] + shift2[...]).astype(low)
    layer_out[...] = out
    first[...] = jnp.zeros_like(first)
    for i in range(out.shape[0] // SEQ):
        first[i : i + 1] = out[i * SEQ : i * SEQ + 1].astype(f32)


def out_backward(n_mp, *refs):
    cot, g_first, hat, inv, gain, hidden = refs[:6]
    g_z2, small, keep, send = refs[6:10]
    g_w, sem = refs[10:]
    rows = cot.shape[0]
    g_z2[...] = cot[...].astype(f32)
    for i in range(rows // SEQ):
        g_z2[i * SEQ : i * SEQ + 1] += g_first[i : i + 1]
    g_y = g_z2[...]
    small[...] = jnp.zeros_like(small)
    small[1:2] = jnp.sum(g_y * hat[...], axis=0, keepdims=True)
    small[2:3] = jnp.sum(g_y, axis=0, keepdims=True)
    g_z = norm_back(g_y, hat[...], inv[:, :1], gain[...])
    g_z2[...] = g_z
    small[0:1] = jnp.sum(g_z, axis=0, keepdims=True)
    g_ffn = g_z.astype(low)

    @pl.loop(0, n_mp)
    def _(s):
        g_w[s] = tn(hidden[s], g_ffn).astype(low)

    size = keep.shape[-2]
    wait_all(send_slices(lambda s, p: row_spot(g_w, s, p, size), keep, send, sem, n_mp))


def in_backward(n_mp, *refs):
    g_z2, slope, h1, hat, inv, gain, own_in, own_out = refs[:8]
    in_parts = refs[8 : 8 + SLICES]
    out_parts = refs[16 : 16 + SLICES]
    g_z1, g_mid, small, keep, send = refs[24:29]
    w_in, w_out, g_w, acc, sem, sem2 = refs[29:]
    copies = fetch_rows(own_in, in_parts, w_in, sem, 0)
    copies += fetch_rows(own_out, out_parts, w_out, sem, n_copies(n_mp))
    wait_all(copies)
    acc[...] = g_z2[...]
    g_ffn = g_z2[...].astype(low)

    @pl.loop(0, n_mp)
    def _(s):
        g_pre = (nt(g_ffn, w_out[s]) * slope[s].astype(f32)).astype(low)
        g_mid[s] = jnp.sum(g_pre.astype(f32), axis=0, keepdims=True)
        g_w[s] = tn(h1[...], g_pre).astype(low)
        acc[...] += nt(g_pre, w_in[s])

    size = keep.shape[-2]
    copies = send_slices(lambda s, p: row_spot(g_w, s, p, size), keep, send, sem2, n_mp)
    g_h1 = acc[...]
    small[...] = jnp.zeros_like(small)
    small[1:2] = jnp.sum(g_h1 * hat[...], axis=0, keepdims=True)
    small[2:3] = jnp.sum(g_h1, axis=0, keepdims=True)
    g_z = norm_back(g_h1, hat[...], inv[:, :1], gain[...])
    g_z1[...] = g_z
    small[0:1] = jnp.sum(g_z, axis=0, keepdims=True)
    wait_all(copies)


def attention_backward(n_mp, cols, *refs):
    g_z1, q, k, v, ctx, ids, own_qkv, own_o = refs[:8]
    parts = refs[8 : 8 + PARTS]
    g_q, g_k, g_v, g_bias, g_wo = refs[18:23]
    w, g_ctx, sem = refs[23:]
    copies = fetch_att(own_qkv, own_o, parts, w, sem, cols)
    rows, width = g_z1.shape
    g_attn = g_z1[...].astype(low)
    wait_all(copies)
    g_ctx[...] = nt(g_attn, w[3]).astype(low)

    @pl.loop(0, rows // PAIR)
    def _(t):
        at = pl.ds(pl.multiple_of(t * PAIR, PAIR), PAIR)
        mask = pair_mask(ids[t])
        for j in range(width // LANES):
            lanes = slice(j * LANES, (j + 1) * LANES)
            q2, g2 = q[at, lanes], g_ctx[at, lanes]
            k2, v2 = split_heads(k[at, lanes]), split_heads(v[at, lanes])
            raw = nt(q2, k2)
            g_p = nt(g2, v2)
            p_low, g_raw = [], []
            for i in (0, 1):
                half = slice(i * PAIR, (i + 1) * PAIR)
                p = softmax_of(raw[:, half], mask)
                inner = jnp.sum(p * g_p[:, half], axis=-1, keepdims=True)
                p_low.append(p.astype(low))
                g_raw.append((p * (g_p[:, half] - inner) * 0.125).astype(low))
            p_low = jnp.concatenate(p_low, axis=1)
            g_raw = jnp.concatenate(g_raw, axis=1)
            g_v[at, lanes] = join_heads(tn(p_low, g2)).astype(low)
            g_q[at, lanes] = nn(g_raw, k2).astype(low)
            g_k[at, lanes] = join_heads(tn(g_raw, q2)).astype(low)

    g_wo[...] = tn(ctx[...], g_attn).astype(low)
    g_bias[...] = jnp.zeros_like(g_bias)
    g_bias[0:1] = jnp.sum(g_q[...].astype(f32), axis=0, keepdims=True)
    g_bias[1:2] = jnp.sum(g_v[...].astype(f32), axis=0, keepdims=True)


def attention_weights(n_mp, cols, *refs):
    x, g_q, g_k, g_v, g_wo, keep, send, g_w, sem = refs
    g_w[3] = g_wo[...]
    g_w[0] = tn(g_q[...], x[...]).astype(low)
    g_w[1] = tn(g_k[...], x[...]).astype(low)
    g_w[2] = tn(g_v[...], x[...]).astype(low)
    size = keep.shape[-2]
    wait_all(send_slices(lambda s, p: att_spot(g_w, s, p, cols, size), keep, send, sem, n_mp))


def attention_inputs(n_mp, cols, *refs):
    g_z1, g_q, g_k, g_v, own_qkv, own_o = refs[:6]
    parts = refs[6 : 6 + PARTS]
    g_x, w, sem = refs[16:]
    wait_all(fetch_att(own_qkv, own_o, parts, w, sem, cols))
    g_x[...] = g_z1[...] + nn(g_q[...], w[0]) + nn(g_k[...], w[1]) + nn(g_v[...], w[2])


def finish_rows(*refs):
    parts = refs[:SLICES]
    out_a, out_b, got, sem = refs[SLICES:]
    size = parts[0].shape[0] // 2
    copies = []
    for p in range(SLICES):
        for i in (0, 1):
            part = parts[p].at[pl.ds(i * size, size)]
            spot = row_spot(got, i, p, size)
            copies.append(pltpu.make_async_copy(part, spot, sem.at[2 * p + i]))
    wait_all(start_all(copies))
    out_a[...] = got[0].astype(f32)
    out_b[...] = got[1].astype(f32)


def finish_att(cols, *refs):
    parts = refs[:SLICES]
    out_qkv, out_o, got, sem = refs[SLICES:]
    size = parts[0].shape[0]
    copies = [
        pltpu.make_async_copy(parts[p], att_spot(got, 0, p, cols, size), sem.at[p])
        for p in range(SLICES)
    ]
    wait_all(start_all(copies))
    for i in range(3):
        out_qkv[i] = got[i].astype(f32).T
    out_o[...] = got[3].astype(f32)


def make(mesh):
    n_dp = mesh.shape["dp"]
    n_mp = mesh.shape["mp"]

    def dpx(x, bit):
        return lax.ppermute(x, "dp", [(i, i ^ bit) for i in range(n_dp)])

    def mpx(x, bit):
        return lax.ppermute(x, "mp", [(i, i ^ bit) for i in range(n_mp)])

    def bit_of(axis, bit):
        return (lax.axis_index(axis) & bit) != 0

    def flips(v, axis, bits, dims):
        for bit, dim in zip(bits, dims):
            v = jnp.where(bit_of(axis, bit), jnp.flip(v, dim), v)
        return v

    def plane_parts(r):
        got = [None] * SLICES
        for p in (0, 2, 4, 6):
            got[p] = dpx(r, p) if p else r
        for p in (0, 2, 4, 6):
            got[p + 1] = dpx(got[p], 1)
        return got

    def over_z(piece):
        return [mpx(piece, i) for i in range(1, n_mp)]

    def over_xy(r):
        return [dpx(r, 2), dpx(r, 4)]

    def over_plane(r):
        return [dpx(r, 2), dpx(r, 4), dpx(r, 6)]

    def over_corner(near):
        at_x, at_y = near
        half = at_x.shape[1] // 2
        return [dpx(at_y[:, :half], 2), dpx(at_x[:, half:], 4)]

    def over_core(parts):
        return parts + [dpx(part, 1) for part in parts]

    def after(x, *deps):
        return lax.optimization_barrier((x, deps))[0]

    def own_piece(shard):
        rows = shard.shape[0] // SLICES
        return lax.dynamic_slice_in_dim(shard, (lax.axis_index("dp") % SLICES) * rows, rows, 0)

    def add(a, b):
        return (a.astype(f32) + b.astype(f32)).astype(low)

    def reduce_one(keep, got):
        return (
            add(keep[0, :, 1], got[0, :, 1]),
            add(keep[1, 1], got[1, 1]),
            add(keep[0, :, 0], got[0, :, 0]),
            add(keep[1, 0], got[1, 0]),
        )

    def reduce_two(a0, b0, a1, b1):
        return add(a0[1], a1[1]), add(b0[1], b1[1]), a0[0], a1[0], b0[0], b1[0]

    def reduce_three(a0, a1, b0, b1, a2, b2):
        a = a0.astype(f32) + a1.astype(f32) + a2.astype(f32)
        b = b0.astype(f32) + b1.astype(f32) + b2.astype(f32)
        u = [a[0], a[1], b[0], b[1]]
        bit = SLICES
        while bit < n_dp:
            u = [w.astype(low) for w in u]
            u = [w.astype(f32) + dpx(w, bit).astype(f32) for w in u]
            bit *= 2
        return [w.astype(low) for w in u]

    def reduce_last(u):
        total = u[0].astype(f32)
        for w in u[1:]:
            total = total + w.astype(f32)
        return total.astype(low)

    def sum_all(v):
        bit = 1
        while bit < n_dp:
            v = v + dpx(v, bit)
            bit *= 2
        bit = 1
        while bit < n_mp:
            v = v + mpx(v, bit)
            bit *= 2
        return v

    def mp_natural(v):
        bits = [1 << i for i in reversed(range(n_mp.bit_length() - 1))]
        shape = v.shape
        v = v.reshape((2,) * len(bits) + shape[1:])
        return flips(v, "mp", bits, range(len(bits))).reshape(shape)

    def gather_all(own):
        r = jnp.stack([own] + [mpx(own, s) for s in range(1, n_mp)])
        r = mp_natural(r)
        z = jnp.stack([r] + [dpx(r, b) for b in (2, 4, 6)])
        v = jnp.stack([z, dpx(z, 1)], 1).reshape((2, 2, 2) + r.shape)
        v = flips(v, "dp", (4, 2, 1), (0, 1, 2)).reshape((SLICES,) + r.shape)
        bit = SLICES
        while bit < n_dp:
            o = dpx(v, bit)
            up = bit_of("dp", bit)
            v = jnp.concatenate([jnp.where(up, o, v), jnp.where(up, v, o)], 0)
            bit *= 2
        return v.reshape((n_dp * n_mp,) + own.shape)

    def rank_part(first_rows, sents, pair_ids, w_pool, b_pool, scale):
        n_all = n_dp * n_mp
        width = first_rows.shape[-1]
        first_rows = first_rows[:, :sents].reshape(n_all * sents, width).astype(low)
        npairs = n_all * sents // 2
        pooled = jnp.tanh(
            jnp.dot(first_rows, w_pool, preferred_element_type=f32) + b_pool.astype(f32)
        )
        inv_len = lax.rsqrt(jnp.sum(pooled * pooled, axis=-1, keepdims=True) + eps_norm)
        emb_full = pooled * inv_len
        emb_pairs = emb_full.astype(low).reshape(npairs, 2, width)
        all_src, all_tgt = emb_pairs[:, 0, :], emb_pairs[:, 1, :]
        scale_value = scale[0]
        cosine = jnp.einsum("kd,md->km", all_src, all_tgt, preferred_element_type=f32)
        same = pair_ids[:, None] == pair_ids[None, :]
        counts = jnp.sum(same.astype(f32), axis=1)
        index_all = jnp.arange(npairs)
        diag_mask = (index_all[:, None] == index_all[None, :]).astype(f32)
        grad_row, part_row = rank_terms(
            cosine, same, diag_mask, (1.0 / counts)[:, None], scale_value, 1
        )
        grad_col, part_col = rank_terms(
            cosine, same, diag_mask, (1.0 / counts)[None, :], scale_value, 0
        )
        grad_all = grad_row + grad_col
        grad_src = scale_value * jnp.dot(grad_all, all_tgt.astype(f32), precision=high)
        grad_tgt = scale_value * jnp.einsum(
            "km,kd->md", grad_all, all_src.astype(f32), precision=high
        )
        new_scale = scale - step_rate * (jnp.sum(part_row) + jnp.sum(part_col))
        grad_emb = jnp.stack([grad_src, grad_tgt], axis=1).reshape(2 * npairs, width)
        grad_pooled = inv_len * (
            grad_emb - emb_full * jnp.sum(emb_full * grad_emb, axis=-1, keepdims=True)
        )
        grad_ppre = (grad_pooled * (1.0 - pooled * pooled)).astype(low)
        grad_pool = jnp.einsum("sd,se->de", first_rows, grad_ppre, preferred_element_type=f32)
        grad_b_pool = jnp.sum(grad_ppre.astype(f32), axis=0)
        own_ppre = lax.dynamic_slice_in_dim(
            grad_ppre, lax.axis_index(("dp", "mp")) * sents, sents, 0
        )
        grad_first = jnp.einsum("se,de->sd", own_ppre, w_pool, preferred_element_type=f32)
        grad_first = jnp.pad(grad_first, ((0, BLOCK - sents), (0, 0)))
        return grad_first, grad_pool, grad_b_pool, new_scale

    def on_device(
        inputs,
        token_ids,
        out_cot,
        pair_ids,
        w_qkv,
        b_qv,
        w_attn,
        b_attn,
        norm1_gain,
        norm1_bias,
        w_in,
        b_in,
        w_out,
        b_out,
        norm2_gain,
        norm2_bias,
        w_pool,
        b_pool,
        scale,
    ):
        rows, width = inputs.shape
        cols = w_qkv.shape[2]
        units = w_in.shape[1]
        sents = rows // SEQ
        shape = jax.ShapeDtypeStruct
        dma = pltpu.SemaphoreType.DMA
        vmem = pltpu.VMEM

        def row(v):
            return v.astype(f32)[None, :]

        qkv_t = w_qkv.transpose(0, 2, 1)
        att_shard = jnp.concatenate([qkv_t.reshape(3 * cols, width), w_attn])
        size = att_shard.shape[0] // SLICES
        small = jnp.pad(jnp.concatenate([b_qv.reshape(-1), b_in]), (0, 2 * width - 2 * cols - units))
        small = small.reshape(2, width)
        att_r = over_z(jnp.concatenate([own_piece(att_shard), small]))
        small = jnp.stack([small] + [r[size:] for r in att_r]).reshape(n_mp, -1).astype(f32)
        b_q, b_v = small[:, :cols].reshape(1, -1), small[:, cols : 2 * cols].reshape(1, -1)
        b_mid = small[:, None, 2 * cols : 2 * cols + units]
        att_r = jnp.stack([r[:size] for r in att_r])
        att_near = over_xy(att_r)
        in_r = jnp.stack(over_z(after(own_piece(w_in), att_r)))
        att_parts = over_core([att_r] + att_near + over_corner(att_near))
        in_near = over_plane(after(in_r, *att_near))
        out_own = after(own_piece(w_out), in_r, *att_near)
        out_z = [mpx(out_own, 1)]
        bit = 2
        while bit < n_mp:
            far = mpx(jnp.stack([out_own] + out_z), bit)
            out_z += [far[i] for i in range(bit)]
            bit *= 2
        nc = n_copies(n_mp)
        own_qkv = att_shard[: 3 * cols].reshape(3, cols, width)

        def here(*arrays):
            return [(a, True) for a in arrays]

        def away(*arrays):
            return [(a, False) for a in arrays]

        gain_one, shift_one = row(norm1_gain), row(norm1_bias)
        gain_two, shift_two = row(norm2_gain), row(norm2_bias)
        ids = token_ids.reshape(rows // PAIR, 1, PAIR)

        rows_low, rows_f = shape((rows, width), low), shape((rows, width), f32)
        thin = shape((rows, 128), f32)
        query, key_part, value_part, context, hat_one, inv_one, h1 = call(
            functools.partial(attention_forward, n_mp, cols),
            here(after(inputs, out_z[0]), ids, b_q, b_v, row(b_attn), gain_one, shift_one)
            + away(own_qkv, w_attn, *att_parts),
            here(rows_low, rows_low, rows_low, rows_low, rows_f, thin, rows_low),
            [vmem((4, n_mp * cols, width), low), dma((nc,))],
            11,
        )
        out_r = jnp.stack(after(out_z, h1))
        out_near = over_plane(out_r)
        in_parts = over_core(after([in_r] + in_near, h1))
        mid = shape((n_mp, rows, units), low)
        hidden, slope = call(
            functools.partial(ffn_in_forward, n_mp),
            here(h1, b_mid) + away(w_in, *in_parts),
            here(mid, mid),
            [vmem((n_mp, width, units), low), dma((nc,))],
            9,
        )
        out_parts = over_core(after([out_r] + out_near, hidden))
        layer_out, hat_two, inv_two, own_first = call(
            functools.partial(ffn_out_forward, n_mp),
            here(hidden, hat_one, gain_one, shift_one, row(b_out), gain_two, shift_two)
            + away(w_out, *out_parts),
            here(rows_low, rows_f, thin, shape((BLOCK, width), f32)),
            [vmem((n_mp, units, width), low), vmem((rows, width), f32), dma((nc,))],
            6,
        )
        grad_first, grad_pool, grad_b_pool, new_scale = rank_part(
            gather_all(own_first), sents, pair_ids, w_pool, b_pool, scale
        )
        lot = shape((2, 2, 2, n_mp // 2, size, width), low)
        tiny = shape((BLOCK, width), f32)
        grad_z2, small_two, keep_o, send = call(
            functools.partial(out_backward, n_mp),
            here(out_cot, grad_first, hat_two, inv_two, gain_two, hidden),
            here(rows_f, tiny) + away(lot, lot),
            [vmem((n_mp, units, width), low), dma((SLICES * n_mp,))],
            10,
        )
        got_o = dpx(send, 1)
        grad_z1, grad_b_in, small_one, keep_i, send = call(
            functools.partial(in_backward, n_mp),
            here(grad_z2, slope, h1, hat_one, inv_one, gain_one) + away(w_in, w_out, *in_parts, *out_parts),
            here(rows_f, shape((n_mp, 1, units), f32), tiny) + away(lot, lot),
            [
                vmem((n_mp, width, units), low),
                vmem((n_mp, units, width), low),
                vmem((n_mp, width, units), low),
                vmem((rows, width), f32),
                dma((2 * nc,)),
                dma((SLICES * n_mp,)),
            ],
            17,
        )
        got_i = dpx(send, 1)
        step_o = reduce_one(keep_o, after(got_o, grad_z1))
        a_o, b_o = dpx(step_o[0], 2), dpx(step_o[1], 4)
        grad_q, grad_k, grad_v, grad_b_qv, grad_wo = call(
            functools.partial(attention_backward, n_mp, cols),
            here(after(grad_z1, step_o[0], step_o[1]), query, key_part, value_part, context, ids)
            + away(own_qkv, w_attn, *att_parts),
            here(rows_low, rows_low, rows_low, tiny, shape((n_mp * cols, width), low)),
            [vmem((4, n_mp * cols, width), low), vmem((rows, width), low), dma((nc,))],
            12,
        )
        step_i = reduce_one(keep_i, after(got_i, grad_q))
        a_i, b_i = dpx(step_i[0], 2), dpx(step_i[1], 4)
        step_o = reduce_two(step_o[2], step_o[3], after(a_o, grad_q), after(b_o, grad_q))
        a2_o, b2_o = dpx(step_o[0], 4), dpx(step_o[1], 2)
        keep_a, send = call(
            functools.partial(attention_weights, n_mp, cols),
            here(after(inputs, step_i[0], step_i[1], step_o[0], step_o[1]))
            + here(grad_q, grad_k, grad_v, grad_wo),
            away(lot, lot),
            [vmem((4, n_mp * cols, width), low), dma((SLICES * n_mp,))],
            6,
        )
        got_a = dpx(send, 1)
        (input_grad,) = call(
            functools.partial(attention_inputs, n_mp, cols),
            here(grad_z1, after(grad_q, keep_a), grad_k, grad_v)
            + away(own_qkv, w_attn, *att_parts),
            here(rows_f),
            [vmem((4, n_mp * cols, width), low), dma((nc,))],
            6,
        )
        step_a = reduce_one(keep_a, after(got_a, input_grad))
        a_a, b_a = dpx(step_a[0], 2), dpx(step_a[1], 4)
        step_o = after(reduce_three(*step_o[2:], a2_o, b2_o), step_a[0])
        z_o = [mpx(step_o[i], i) for i in range(1, n_mp)]
        step_i = reduce_two(step_i[2], step_i[3], after(a_i, step_o[0]), b_i)
        a2_i, b2_i = dpx(step_i[0], 4), dpx(step_i[1], 2)
        step_a = reduce_two(step_a[2], step_a[3], after(a_a, step_i[0]), after(b_a, step_i[1]))
        a2_a, b2_a = dpx(step_a[0], 4), dpx(step_a[1], 2)
        step_i = after(reduce_three(*step_i[2:], a2_i, b2_i), step_a[0])
        z_i = [mpx(step_i[i], i) for i in range(1, n_mp)]
        step_a = after(reduce_three(*step_a[2:], a2_a, b2_a), step_i)
        z_a = [mpx(step_a[i], i) for i in range(1, n_mp)]
        red_out = reduce_last([step_o[0]] + z_o)
        red_in = reduce_last([step_i[0]] + z_i)
        red_att = reduce_last([step_a[0]] + z_a)
        grad_b_qv = grad_b_qv[:2].reshape(2, n_mp, cols).transpose(1, 0, 2)
        total = jnp.concatenate(
            [
                mp_natural(grad_b_qv).reshape(-1),
                mp_natural(grad_b_in).reshape(-1),
                small_one[:3].reshape(-1),
                small_two[:3].reshape(-1),
            ]
        )
        total = sum_all(after(total, step_a[0]))
        n_qv, n_in = n_mp * 2 * cols, n_mp * units
        take = lax.axis_index("mp")
        out_b_qv = lax.dynamic_slice_in_dim(total[:n_qv].reshape(n_mp, 2, cols), take, 1, 0)[0]
        out_b_in = lax.dynamic_slice_in_dim(
            total[n_qv : n_qv + n_in].reshape(n_mp, -1), take, 1, 0
        )[0]
        total = total[n_qv + n_in :].reshape(6, width)
        whole = shape((SLICES * size, width), f32)

        done_in, done_out = call(
            finish_rows,
            away(*plane_parts(jnp.concatenate([red_in, red_out]))),
            here(whole, whole),
            [vmem((2, SLICES * size, width), low), dma((2 * SLICES,))],
            4,
        )
        done_qkv, done_attn = call(
            functools.partial(finish_att, cols),
            away(*plane_parts(red_att)),
            here(shape((3, width, cols), f32), shape((cols, width), f32)),
            [vmem((4, cols, width), low), dma((SLICES,))],
            3,
        )
        return (
            layer_out,
            input_grad,
            done_qkv,
            out_b_qv,
            done_attn,
            total[0],
            total[1],
            total[2],
            done_in,
            out_b_in,
            done_out,
            total[3],
            total[4],
            total[5],
            grad_pool,
            grad_b_pool,
            new_scale,
        )

    return on_device


def solution(mesh):
    rows, whole = P(("dp", "mp"), None), P()
    in_specs = (
        rows,
        P(("dp", "mp")),
        rows,
        whole,
        P(None, None, "mp"),
        P(None, "mp"),
        P("mp", None),
        whole,
        whole,
        whole,
        P(None, "mp"),
        P("mp"),
        P("mp", None),
        whole,
        whole,
        whole,
        whole,
        whole,
        whole,
    )
    out_specs = (
        rows,
        rows,
        P(None, None, "mp"),
        P(None, "mp"),
        P("mp", None),
        whole,
        whole,
        whole,
        P(None, "mp"),
        P("mp"),
        P("mp", None),
        whole,
        whole,
        whole,
        whole,
        whole,
        whole,
    )
    return jax.shard_map(
        make(mesh), mesh=mesh, in_specs=in_specs, out_specs=out_specs, check_vma=False
    )
```

time: 452 us -> 323 us (0.71); the launches traced: 443 us -> 322 us
  Pallas kernels: 0 us -> 95 us
  matrix products: 85 us -> 3.92 us
  other arithmetic: 86.9 us -> 29.1 us
  local copies, waits for them, and re-layouts: 65.1 us -> 26 us
  starting transfers between devices: 98.6 us -> 78 us
  waiting for transfers between devices: 101 us -> 85.3 us
    pallas_call x0 -> x10, Pallas kernels: none -> 95 us  [call(): pl.pallas_call(body, out_shape=[jax.ShapeDtypeStruct(o.shape, o.dtype) fo...]
    dot_general x23 -> x6, matrix products: 80.4 us -> 3.92 us  [the longest x1 1.92 us: rank_part(): jnp.einsum('sd,se->de', first_rows, grad_ppre, preferred_element_type=f32)]
    select_n x32 -> x8, other arithmetic: 31.3 us -> 2.19 us  [flips(): v = jnp.where(bit_of(axis, bit), jnp.flip(v, dim), v)]
    another operation x33 -> x12, other arithmetic: 23.4 us -> 4.03 us  [the longest x15 8.7 us: gather_plane(): z = jnp.stack([r, at_x, at_y, at_d])]
    ppermute x55 -> x59, waiting for transfers between devices: 71 us -> 56.2 us  [dpx(): return lax.ppermute(x, 'dp', [(i, i ^ bit) for i in range(n_dp)])]
    squeeze x17 -> x2, local copies, waits for them, and re-layouts: 12.5 us -> 0.6 us  [the longest x1 0.58 us: on_device(): lax.dynamic_slice_in_dim(total[:n_qv].reshape(n_mp, 2, cols), take, 1, 0)[0]]
    another operation x15 -> x5, local copies, waits for them, and re-layouts: 11.2 us -> 0.5 us  [the longest x1 0.46 us: rank_part(): jnp.stack([grad_src, grad_tgt], axis=1).reshape(2 * npairs, width)]
    ppermute x28 -> x22, starting transfers between devices: 46.3 us -> 35.8 us  [mpx(): return lax.ppermute(x, 'mp', [(i, i ^ bit) for i in range(n_mp)])]
  transfers between devices with their start and end apart: 83 -> 81, of which waited for: 35 -> 29; matrix products, arithmetic and copies ran while one was open for 30% -> 14% of each run, Pallas kernels for 0% -> 22%
where the time goes in v2:
time: 323 us; the launch traced here: 322 us
  Pallas kernels  95 us (29%)
  waiting for transfers between devices  85.3 us (26%)
  starting transfers between devices  78 us (24%)
  other arithmetic  29.1 us (9%)
  local copies, waits for them, and re-layouts  26 us (8%)
  between operations  5 us (2%)
  matrix products  3.92 us (1%)
    pallas_call x10, Pallas kernels, call(): pl.pallas_call(body, out_shape=[jax.ShapeDtypeStruct(o.shape, o.dtype) fo...  95 us
    ppermute x59, waiting for transfers between devices, dpx(): return lax.ppermute(x, 'dp', [(i, i ^ bit) for i in range(n_dp)])  56.2 us
    ppermute x59, starting transfers between devices, dpx(): return lax.ppermute(x, 'dp', [(i, i ^ bit) for i in range(n_dp)])  42.1 us
    ppermute x22, starting transfers between devices, mpx(): return lax.ppermute(x, 'mp', [(i, i ^ bit) for i in range(n_mp)])  35.8 us
    ppermute x22, waiting for transfers between devices, mpx(): return lax.ppermute(x, 'mp', [(i, i ^ bit) for i in range(n_mp)])  29.1 us
    convert_element_type x12, other arithmetic, add(): return (a.astype(f32) + b.astype(f32)).astype(low)  15.7 us
    unnamed x135, local copies, waits for them, and re-layouts  7.11 us
  transfers between devices with their start and end apart: 81, of which 29 were waited for; matrix products, arithmetic and copies ran while one was open for 14% of the time, Pallas kernels for 22%

profile of v2, /device:TPU:0, one launch (start us, length us, event | category | flops | bytes accessed | tf_op | source)
XLA Modules:
  0.0 322.2 jit_solution(10187417704085907582)
XLA Ops:
  3.3 5.1 %collective-permute-start.2 = (bf16[98,768]{1,0:T(8,128)(2,1)S(1)}, bf16[98,768]{1,0:T(8,128)(2,1)S(1)}, u32[]{:S(2)}, u32[]{:S(2)}) collective-permute-start(bf16[98,768]{1,0:T(8,128)(2,1)S(1)} %pad_maximum_fusion.8), channel_id=1, source_target_pairs={{0,3},{1,2},{2,1},{3,0},{4,7},{5,6},{6,5},{7,4},{8,11},{9,10},{10,... | collective-permute-start | bytes 451592 | tf_op jit(solution)/shard_map/ppermute | solution.py:419
  13.5 8.5 %collective-permute-done.1 = bf16[98,768]{1,0:T(8,128)(2,1)S(1)} collective-permute-done((bf16[98,768]{1,0:T(8,128)(2,1)S(1)}, bf16[98,768]{1,0:T(8,128)(2,1)S(1)}, u32[]{:S(2)}, u32[]{:S(2)}) %collective-permute-start.1) | collective-permute-done | bytes 150560 | tf_op jit(solution)/shard_map/ppermute | solution.py:419
  26.1 3.0 collective-permute-start.4
  33.5 5.7 %collective-permute-done.4 = bf16[96,768]{1,0:T(8,128)(2,1)S(1)} collective-permute-done((bf16[96,768]{1,0:T(8,128)(2,1)S(1)}, bf16[96,768]{1,0:T(8,128)(2,1)S(1)}, u32[]{:S(2)}, u32[]{:S(2)}) %collective-permute-start.4) | collective-permute-done | bytes 147488 | tf_op jit(solution)/shard_map/ppermute | solution.py:419
  44.9 3.8 %collective-permute-done.9.refs_12_.refs_11_.refs_9_ = bf16[3,48,768]{2,1,0:T(8,128)(2,1)S(1)} collective-permute-done((bf16[3,48,768]{2,1,0:T(8,128)(2,1)S(1)}, bf16[3,48,768]{2,1,0:T(8,128)(2,1)S(1)}, u32[]{:S(2)}, u32[]{:S(2)}) %collective-permute-start.9) | collective-permute-done | bytes 221216 | tf_op jit(solution)/shard_map/ppermute | solution.py:416
  55.5 10.8 %shard_map.314 = (bf16[384,768]{1,0:T(8,128)(2,1)}, bf16[384,768]{1,0:T(8,128)(2,1)}, bf16[384,768]{1,0:T(8,128)(2,1)}, bf16[384,768]{1,0:T(8,128)(2,1)}, f32[38...) custom-call(bf16[384,768]{1,0:T(8,128)(2,1)} %refs_0_.3, s32[3,1,128]{2,1,0:T(1,128)} %reshape.301.refs_1_.refs_5_, ...), custom_call_target="tpu_custom_call" | custom-call | flops 12099999744 | tf_op jit(solution)/shard_map/pallas_call | solution.py:54
  66.3 7.9 %collective-permute-done.17.refs_5_.refs_10_ = bf16[3,96,768]{2,1,0:T(8,128)(2,1)S(1)} collective-permute-done((bf16[3,96,768]{2,1,0:T(8,128)(2,1)S(1)}, bf16[3,96,768]{2,1,0:T(8,128)(2,1)S(1)}, u32[]{:S(2)}, u32[]{:S(2)}) %collective-permute-start.17) | collective-permute-done | bytes 442400 | tf_op jit(solution)/shard_map/ppermute | solution.py:416
  80.4 11.4 %shard_map.315 = (bf16[4,384,768]{2,1,0:T(8,128)(2,1)}, bf16[4,384,768]{2,1,0:T(8,128)(2,1)}) custom-call(bf16[384,768]{1,0:T(8,128)(2,1)} %get-tuple-element.92.refs_0_.refs_2_, f32[4,1,768]{2,1,0:T(1,128)} %broadcast_in_dim.57.refs_1_, bf16[768,768]{1,0:T(8,128)(2,1)} %refs_6_.1, bf16[3,96,768]{2,1,0:T(8,128)(2,1)} %copy-done.16, ...), custom_call_target="tpu_custom_call" | custom-call | flops 9900000256 | tf_op jit(solution)/shard_map/pallas_call | solution.py:54
  91.9 6.1 %collective-permute-done.25.refs_10_.refs_18_ = bf16[3,96,768]{2,1,0:T(8,128)(2,1)S(1)} collective-permute-done((bf16[3,96,768]{2,1,0:T(8,128)(2,1)S(1)}, bf16[3,96,768]{2,1,0:T(8,128)(2,1)S(1)}, u32[]{:S(2)}, u32[]{:S(2)}) %collective-permute-start.25) | collective-permute-done | bytes 442400 | tf_op jit(solution)/shard_map/ppermute | solution.py:416
  102.7 8.9 %shard_map.316 = (bf16[384,768]{1,0:T(8,128)(2,1)}, f32[384,768]{1,0:T(8,128)}, f32[384,128]{1,0:T(8,128)}, f32[8,768]{1,0:T(8,128)}) custom-call(bf16[4,384,768]{2,1,0:T(8,128)(2,1)} %get-tuple-element.98.refs_0_.refs_5_, f32[384,768]{1,0:T(8,128)} %get-tuple-element.99.refs_1_.refs_3_, f32[1,768]{1,0:T(1,128)} %reshape.314.refs_5_.refs_2_, ...), custom_call_target="tpu_custom_call" | custom-call | flops 6600000000 | tf_op jit(solution)/shard_map/pallas_call | solution.py:54
  117.2 3.5 %collective-permute-done.33 = bf16[8,768]{1,0:T(8,128)(2,1)S(1)} collective-permute-done((bf16[8,768]{1,0:T(8,128)(2,1)S(1)}, bf16[8,768]{1,0:T(8,128)(2,1)S(1)}, u32[]{:S(2)}, u32[]{:S(2)}) %collective-permute-start.33) | collective-permute-done | bytes 12320 | tf_op jit(solution)/shard_map/ppermute | solution.py:419
  136.3 9.9 %shard_map.317 = (f32[384,768]{1,0:T(8,128)}, f32[8,768]{1,0:T(8,128)}, bf16[2,2,2,2,96,768]{5,4,3,2,1,0:T(8,128)(2,1)}, bf16[2,2,2,2,96,768]{5,4,3,2,1,0:T(8,128)(2,1)}) custom-call(bf16[384,768]{1,0:T(8,128)(2,1)} %refs_0_.2, f32[8,768]{1,0:T(8,128)} %pad.9.refs_1_, f32[384,768]{1,0:T(8,128)} %get-tuple-element.109.refs_2_, ...), custom_call_target="tpu_custom_call" | custom-call | flops 11000000512 | tf_op jit(solution)/shard_map/pallas_call | solution.py:54
  146.4 17.3 %shard_map.318 = (f32[384,768]{1,0:T(8,128)}, f32[4,1,768]{2,1,0:T(1,128)}, f32[8,768]{1,0:T(8,128)}, bf16[2,2,2,2,96,768]{5,4,3,2,1,0:T(8,128)(2,1)}, bf16[2,2,2,2,96,768]{5,4,3,2,1,0:T(8,128)(2,1)}) custom-call(f32[384,768]{1,0:T(8,128)} %get-tuple-element.111.refs_0_, bf16[4,384,768]{2,1,0:T(8,128)(2,1)} %get-tuple-element.112.refs_1_, ...), custom_call_target="tpu_custom_call" | custom-call | flops 18699999232 | tf_op jit(solution)/shard_map/pallas_call | solution.py:54
  174.2 15.4 %shard_map.319 = (bf16[384,768]{1,0:T(8,128)(2,1)}, bf16[384,768]{1,0:T(8,128)(2,1)}, bf16[384,768]{1,0:T(8,128)(2,1)}, f32[8,768]{1,0:T(8,128)}, bf16[768,768]{1,0:T(8,128)(2,1)}) custom-call(f32[384,768]{1,0:T(8,128)} %get-tuple-element.118.refs_0_, bf16[384,768]{1,0:T(8,128)(2,1)} %get-tuple-element.119.refs_1_, ...), custom_call_target="tpu_custom_call" | custom-call | flops 13200000000 | tf_op jit(solution)/shard_map/pallas_call | solution.py:54
  200.2 6.6 %shard_map.320 = (bf16[2,2,2,2,96,768]{5,4,3,2,1,0:T(8,128)(2,1)}, bf16[2,2,2,2,96,768]{5,4,3,2,1,0:T(8,128)(2,1)}) custom-call(bf16[384,768]{1,0:T(8,128)(2,1)} %refs_0_.3, bf16[384,768]{1,0:T(8,128)(2,1)} %get-tuple-element.134.refs_1_, bf16[384,768]{1,0:T(8,128)(2,1)} %get-tuple-element.130.refs_2_, bf16[384,768]{1,0:T(8,128)(2,1)} %get-tuple-element.131.refs_3_, ...), custom_call_target="tpu_custom_call" | custom-call | flops 6600000000 | tf_op jit(solution)/shard_map/pallas_call | solution.py:54
  214.9 7.1 %shard_map.321 = f32[384,768]{1,0:T(8,128)} custom-call(f32[384,768]{1,0:T(8,128)} %get-tuple-element.118.refs_0_, bf16[384,768]{1,0:T(8,128)(2,1)} %get-tuple-element.134.refs_1_, bf16[384,768]{1,0:T(8,128)(2,1)} %get-tuple-element.130.refs_2_, bf16[384,768]{1,0:T(8,128)(2,1)} %get-tuple-element.131.refs_3_, bf16[3,192,768]{2,1,0:T(8,128)(2,1)} %bitcast.230, ...), custom_call_target="tpu_custom_call" | custom-call | flops 6600000000 | tf_op jit(solution)/shard_map/pallas_call | solution.py:54
  232.5 3.7 %collective-permute-done.51 = bf16[2,96,768]{2,1,0:T(8,128)(2,1)S(1)} collective-permute-done((bf16[2,96,768]{2,1,0:T(8,128)(2,1)S(1)}, bf16[2,96,768]{2,1,0:T(8,128)(2,1)S(1)}, u32[]{:S(2)}, u32[]{:S(2)}) %collective-permute-start.51) | collective-permute-done | bytes 294944 | tf_op jit(solution)/shard_map/ppermute | solution.py:416
  238.8 8.7 %collective-permute-done.48 = bf16[2,2,96,768]{3,2,1,0:T(8,128)(2,1)S(1)} collective-permute-done((bf16[2,2,96,768]{3,2,1,0:T(8,128)(2,1)S(1)}, bf16[2,2,96,768]{3,2,1,0:T(8,128)(2,1)S(1)}, u32[]{:S(2)}, u32[]{:S(2)}) %collective-permute-start.48) | collective-permute-done | bytes 589856 | tf_op jit(solution)/shard_map/ppermute | solution.py:416
  249.6 5.7 %collective-permute-done.50 = bf16[2,96,768]{2,1,0:T(8,128)(2,1)S(1)} collective-permute-done((bf16[2,96,768]{2,1,0:T(8,128)(2,1)S(1)}, bf16[2,96,768]{2,1,0:T(8,128)(2,1)S(1)}, u32[]{:S(2)}, u32[]{:S(2)}) %collective-permute-start.50) | collective-permute-done | bytes 294944 | tf_op jit(solution)/shard_map/ppermute | solution.py:416
  267.4 4.0 %collective-permute-done.69 = bf16[96,768]{1,0:T(8,128)(2,1)S(1)} collective-permute-done((bf16[96,768]{1,0:T(8,128)(2,1)S(1)}, bf16[96,768]{1,0:T(8,128)(2,1)S(1)}, u32[]{:S(2)}, u32[]{:S(2)}) %collective-permute-start.69) | collective-permute-done | bytes 147488 | tf_op jit(solution)/shard_map/ppermute | solution.py:419
  275.4 6.2 %collective-permute-start.66 = (f32[9216]{0:T(1024)S(1)}, f32[9216]{0:T(1024)S(1)}, u32[]{:S(2)}, u32[]{:S(2)}) collective-permute-start(f32[9216]{0:T(1024)S(1)} %add.286), channel_id=1, source_target_pairs={{0,1},{1,0},{2,3},{3,2},{4,5},{5,4},{6,7},{7,6},{8,9},{9,8},{10,11... | collective-permute-start | bytes 110600 | tf_op jit(solution)/shard_map/ppermute | solution.py:419
  296.9 6.6 %collective-permute-done.77.refs_4_ = bf16[192,768]{1,0:T(8,128)(2,1)S(1)} collective-permute-done((bf16[192,768]{1,0:T(8,128)(2,1)S(1)}, bf16[192,768]{1,0:T(8,128)(2,1)S(1)}, u32[]{:S(2)}, u32[]{:S(2)}) %collective-permute-start.77) | collective-permute-done | bytes 294944 | tf_op jit(solution)/shard_map/ppermute | solution.py:416
  308.8 3.4 %shard_map.322 = (f32[3,768,192]{2,1,0:T(8,128)}, f32[192,768]{1,0:T(8,128)}) custom-call(bf16[96,768]{1,0:T(8,128)(2,1)} %copy-done.20, bf16[96,768]{1,0:T(8,128)(2,1)} %copy-done.61, bf16[96,768]{1,0:T(8,128)(2,1)} %copy-done.58, bf16[96,768]{1,0:T(8,128)(2,1)} %copy-done.62, bf16[96,768]{1,0:T(8,128)(2,1)} %copy-done.59, bf16[96,768]{1,0:T(8,128)(2,1)} %copy-done.63, ...), custom_call_target="tpu_custom_call" | custom-call | flops 3300000000 | tf_op jit(solution)/shard_map/pallas_call | solution.py:54
  316.8 4.2 %shard_map.323 = (f32[768,768]{1,0:T(8,128)}, f32[768,768]{1,0:T(8,128)}) custom-call(bf16[192,768]{1,0:T(8,128)(2,1)} %copy-done.18, bf16[192,768]{1,0:T(8,128)(2,1)} %copy-done.53, bf16[192,768]{1,0:T(8,128)(2,1)} %copy-done.50, bf16[192,768]{1,0:T(8,128)(2,1)} %copy-done.54, bf16[192,768]{1,0:T(8,128)(2,1)} %copy-done.51, bf16[192,768]{1,0:T(8,128)(2,1)} %copy-done.55, ...), custom_call_target="tpu_custom_call" | custom-call | flops 4400000000 | tf_op jit(solution)/shard_map/pallas_call | solution.py:54
  (398 shorter events, 143.6 us)
Async XLA Ops:
  22.1 17.2 %collective-permute-start.6 = (bf16[3,96,768]{2,1,0:T(8,128)(2,1)S(1)}, bf16[3,96,768]{2,1,0:T(8,128)(2,1)S(1)}, u32[]{:S(2)}, u32[]{:S(2)}) collective-permute-start(bf16[3,96,768]{2,1,0:T(8,128)(2,1)S(1)} %pad_maximum_fusion.2.refs_9_.refs_8_.refs_6_), channel_id=1, source_target_pairs={{0,8},{4,12},{8,0},{12,4},{16,24},{20,28},{24,16},{28,20},{1,9},{5... | collective-permute-start | bytes 1327112 | tf_op jit(solution)/shard_map/ppermute | solution.py:416
  33.5 17.3 %collective-permute-start.11 = (bf16[3,96,768]{2,1,0:T(8,128)(2,1)S(1)}, bf16[3,96,768]{2,1,0:T(8,128)(2,1)}, u32[]{:S(2)}, u32[]{:S(2)}) collective-permute-start(bf16[3,96,768]{2,1,0:T(8,128)(2,1)S(1)} %pad_maximum_fusion.2.refs_9_.refs_8_.refs_6_), channel_id=1, source_target_pairs={{0,4},{4,0},{8,12},{12,8},{16,20},{20,16},{24,28},{28,24},{1,5},{5... | collective-permute-start | bytes 1327112 | tf_op jit(solution)/shard_map/ppermute | solution.py:416
  52.4 21.8 %collective-permute-start.17 = (bf16[3,96,768]{2,1,0:T(8,128)(2,1)S(1)}, bf16[3,96,768]{2,1,0:T(8,128)(2,1)S(1)}, u32[]{:S(2)}, u32[]{:S(2)}) collective-permute-start(bf16[3,96,768]{2,1,0:T(8,128)(2,1)S(1)} %pad_maximum_fusion.3.refs_3_.refs_8_), channel_id=1, source_target_pairs={{0,16},{4,20},{8,24},{12,28},{16,0},{20,4},{24,8},{28,12},{1,17},{... | collective-permute-start | bytes 1327112 | tf_op jit(solution)/shard_map/ppermute | solution.py:416
  52.9 21.3 %collective-permute-start.18 = (bf16[3,96,768]{2,1,0:T(8,128)(2,1)S(1)}, bf16[3,96,768]{2,1,0:T(8,128)(2,1)S(1)}, u32[]{:S(2)}, u32[]{:S(2)}) collective-permute-start(bf16[3,96,768]{2,1,0:T(8,128)(2,1)S(1)} %pad_maximum_fusion.3.refs_3_.refs_8_), channel_id=1, source_target_pairs={{0,24},{4,28},{8,16},{12,20},{16,8},{20,12},{24,0},{28,4},{1,25},{... | collective-permute-start | bytes 1327112 | tf_op jit(solution)/shard_map/ppermute | solution.py:416
  54.4 21.5 %collective-permute-start.23 = (bf16[2,96,768]{2,1,0:T(8,128)(2,1)S(1)}, bf16[2,96,768]{2,1,0:T(8,128)(2,1)S(1)}, u32[]{:S(2)}, u32[]{:S(2)}) collective-permute-start(bf16[2,96,768]{2,1,0:T(8,128)(2,1)S(1)} %pad_maximum_fusion.6), channel_id=1, source_target_pairs={{0,2},{1,3},{2,0},{3,1},{4,6},{5,7},{6,4},{7,5},{8,10},{9,11},{10,... | collective-permute-start | bytes 884744 | tf_op jit(solution)/shard_map/ppermute | solution.py:419
  76.7 21.4 %collective-permute-start.25 = (bf16[3,96,768]{2,1,0:T(8,128)(2,1)S(1)}, bf16[3,96,768]{2,1,0:T(8,128)(2,1)S(1)}, u32[]{:S(2)}, u32[]{:S(2)}) collective-permute-start(bf16[3,96,768]{2,1,0:T(8,128)(2,1)S(1)} %pad_maximum_fusion.4.refs_8_.refs_16_), channel_id=1, source_target_pairs={{0,16},{4,20},{8,24},{12,28},{16,0},{20,4},{24,8},{28,12},{1,17},{... | collective-permute-start | bytes 1327112 | tf_op jit(solution)/shard_map/ppermute | solution.py:416
  77.8 20.2 %collective-permute-start.26 = (bf16[3,96,768]{2,1,0:T(8,128)(2,1)S(1)}, bf16[3,96,768]{2,1,0:T(8,128)(2,1)}, u32[]{:S(2)}, u32[]{:S(2)}) collective-permute-start(bf16[3,96,768]{2,1,0:T(8,128)(2,1)S(1)} %pad_maximum_fusion.4.refs_8_.refs_16_), channel_id=1, source_target_pairs={{0,24},{4,28},{8,16},{12,20},{16,8},{20,12},{24,0},{28,4},{1,25},{... | collective-permute-start | bytes 1327112 | tf_op jit(solution)/shard_map/ppermute | solution.py:416
  146.2 20.8 %collective-permute-start.38 = (bf16[2,2,2,2,96,768]{5,4,3,2,1,0:T(8,128)(2,1)}, bf16[2,2,2,2,96,768]{5,4,3,2,1,0:T(8,128)(2,1)}, u32[]{:S(2)}, u32[]{:S(2)}) collective-permute-start(bf16[2,2,2,2,96,768]{5,4,3,2,1,0:T(8,128)(2,1)} %get-tuple-element.116), channel_id=1, source_target_pairs={{0,4},{4,0},{8,12},{12,8},{16,20},{20,16},{24,28},{28,24},{1,5},{5... | collective-permute-start | bytes 7077896 | tf_op jit(solution)/shard_map/ppermute | solution.py:416
  163.8 25.8 %collective-permute-start.39 = (bf16[2,2,2,2,96,768]{5,4,3,2,1,0:T(8,128)(2,1)}, bf16[2,2,2,2,96,768]{5,4,3,2,1,0:T(8,128)(2,1)}, u32[]{:S(2)}, u32[]{:S(2)}) collective-permute-start(bf16[2,2,2,2,96,768]{5,4,3,2,1,0:T(8,128)(2,1)} %get-tuple-element.125), channel_id=1, source_target_pairs={{0,4},{4,0},{8,12},{12,8},{16,20},{20,16},{24,28},{28,24},{1,5},{5... | collective-permute-start | bytes 7077896 | tf_op jit(solution)/shard_map/ppermute | solution.py:416
  169.5 27.8 %collective-permute-start.41 = (bf16[2,2,96,768]{3,2,1,0:T(8,128)(2,1)}, bf16[2,2,96,768]{3,2,1,0:T(8,128)(2,1)}, u32[]{:S(2)}, u32[]{:S(2)}) collective-permute-start(bf16[2,2,96,768]{3,2,1,0:T(8,128)(2,1)} %get-tuple-element.211), channel_id=1, source_target_pairs={{0,16},{4,20},{8,24},{12,28},{16,0},{20,4},{24,8},{28,12},{1,17},{... | collective-permute-start | bytes 1769480 | tf_op jit(solution)/shard_map/ppermute | solution.py:416
  173.7 23.7 %collective-permute-start.40 = (bf16[2,2,96,768]{3,2,1,0:T(8,128)(2,1)}, bf16[2,2,96,768]{3,2,1,0:T(8,128)(2,1)S(1)}, u32[]{:S(2)}, u32[]{:S(2)}) collective-permute-start(bf16[2,2,96,768]{3,2,1,0:T(8,128)(2,1)} %get-tuple-element.213), channel_id=1, source_target_pairs={{0,8},{4,12},{8,0},{12,4},{16,24},{20,28},{24,16},{28,20},{1,9},{5... | collective-permute-start | bytes 1769480 | tf_op jit(solution)/shard_map/ppermute | solution.py:416
  192.2 20.0 %collective-permute-start.49 = (bf16[2,2,96,768]{3,2,1,0:T(8,128)(2,1)}, bf16[2,2,96,768]{3,2,1,0:T(8,128)(2,1)}, u32[]{:S(2)}, u32[]{:S(2)}) collective-permute-start(bf16[2,2,96,768]{3,2,1,0:T(8,128)(2,1)} %get-tuple-element.203), channel_id=1, source_target_pairs={{0,16},{4,20},{8,24},{12,28},{16,0},{20,4},{24,8},{28,12},{1,17},{... | collective-permute-start | bytes 1769480 | tf_op jit(solution)/shard_map/ppermute | solution.py:416
  195.8 29.4 %collective-permute-start.44 = (bf16[2,2,96,768]{3,2,1,0:T(8,128)(2,1)}, bf16[2,2,96,768]{3,2,1,0:T(8,128)(2,1)}, u32[]{:S(2)}, u32[]{:S(2)}) collective-permute-start(bf16[2,2,96,768]{3,2,1,0:T(8,128)(2,1)} %get-tuple-element.207), channel_id=1, source_target_pairs={{0,8},{4,12},{8,0},{12,4},{16,24},{20,28},{24,16},{28,20},{1,9},{5... | collective-permute-start | bytes 1769480 | tf_op jit(solution)/shard_map/ppermute | solution.py:416
  206.8 18.1 %collective-permute-start.42 = (bf16[2,2,2,2,96,768]{5,4,3,2,1,0:T(8,128)(2,1)}, bf16[2,2,2,2,96,768]{5,4,3,2,1,0:T(8,128)(2,1)S(1)}, u32[]{:S(2)}, u32[]{:S(2)}) collective-permute-start(bf16[2,2,2,2,96,768]{5,4,3,2,1,0:T(8,128)(2,1)} %get-tuple-element.135), channel_id=1, source_target_pairs={{0,4},{4,0},{8,12},{12,8},{16,20},{20,16},{24,28},{28,24},{1,5},{5... | collective-permute-start | bytes 7077896 | tf_op jit(solution)/shard_map/ppermute | solution.py:416
  227.1 20.4 %collective-permute-start.48 = (bf16[2,2,96,768]{3,2,1,0:T(8,128)(2,1)S(1)}, bf16[2,2,96,768]{3,2,1,0:T(8,128)(2,1)S(1)}, u32[]{:S(2)}, u32[]{:S(2)}) collective-permute-start(bf16[2,2,96,768]{3,2,1,0:T(8,128)(2,1)S(1)} %get-tuple-element.204), channel_id=1, source_target_pairs={{0,16},{4,20},{8,24},{12,28},{16,0},{20,4},{24,8},{28,12},{1,17},{... | collective-permute-start | bytes 1769480 | tf_op jit(solution)/shard_map/ppermute | solution.py:416
  229.8 18.4 %collective-permute-start.43 = (bf16[2,2,96,768]{3,2,1,0:T(8,128)(2,1)S(1)}, bf16[2,2,96,768]{3,2,1,0:T(8,128)(2,1)S(1)}, u32[]{:S(2)}, u32[]{:S(2)}) collective-permute-start(bf16[2,2,96,768]{3,2,1,0:T(8,128)(2,1)S(1)} %get-tuple-element.208), channel_id=1, source_target_pairs={{0,8},{4,12},{8,0},{12,4},{16,24},{20,28},{24,16},{28,20},{1,9},{5... | collective-permute-start | bytes 1769480 | tf_op jit(solution)/shard_map/ppermute | solution.py:416
  230.4 27.9 %collective-permute-start.71 = (bf16[96,768]{1,0:T(8,128)(2,1)}, bf16[96,768]{1,0:T(8,128)(2,1)S(1)}, u32[]{:S(2)}, u32[]{:S(2)}) collective-permute-start(bf16[96,768]{1,0:T(8,128)(2,1)} %get-tuple-element.156), channel_id=1, source_target_pairs={{0,1},{1,0},{2,3},{3,2},{4,5},{5,4},{6,7},{7,6},{8,9},{9,8},{10,11... | collective-permute-start | bytes 442376 | tf_op jit(solution)/shard_map/ppermute | solution.py:419
  230.4 30.3 %collective-permute-start.72 = (bf16[96,768]{1,0:T(8,128)(2,1)}, bf16[96,768]{1,0:T(8,128)(2,1)S(1)}, u32[]{:S(2)}, u32[]{:S(2)}) collective-permute-start(bf16[96,768]{1,0:T(8,128)(2,1)} %get-tuple-element.157), channel_id=1, source_target_pairs={{0,2},{1,3},{2,0},{3,1},{4,6},{5,7},{6,4},{7,5},{8,10},{9,11},{10,... | collective-permute-start | bytes 442376 | tf_op jit(solution)/shard_map/ppermute | solution.py:419
  236.2 25.8 %collective-permute-start.73 = (bf16[96,768]{1,0:T(8,128)(2,1)}, bf16[96,768]{1,0:T(8,128)(2,1)S(1)}, u32[]{:S(2)}, u32[]{:S(2)}) collective-permute-start(bf16[96,768]{1,0:T(8,128)(2,1)} %get-tuple-element.158), channel_id=1, source_target_pairs={{0,3},{1,2},{2,1},{3,0},{4,7},{5,6},{6,5},{7,4},{8,11},{9,10},{10,... | collective-permute-start | bytes 442376 | tf_op jit(solution)/shard_map/ppermute | solution.py:419
  262.1 22.9 %collective-permute-start.53 = (bf16[96,768]{1,0:T(8,128)(2,1)S(1)}, bf16[96,768]{1,0:T(8,128)(2,1)S(1)}, u32[]{:S(2)}, u32[]{:S(2)}) collective-permute-start(bf16[96,768]{1,0:T(8,128)(2,1)S(1)} %get-tuple-element.146), channel_id=1, source_target_pairs={{0,1},{1,0},{2,3},{3,2},{4,5},{5,4},{6,7},{7,6},{8,9},{9,8},{10,11... | collective-permute-start | bytes 442376 | tf_op jit(solution)/shard_map/ppermute | solution.py:419
  264.7 22.1 %collective-permute-start.54 = (bf16[96,768]{1,0:T(8,128)(2,1)S(1)}, bf16[96,768]{1,0:T(8,128)(2,1)S(1)}, u32[]{:S(2)}, u32[]{:S(2)}) collective-permute-start(bf16[96,768]{1,0:T(8,128)(2,1)S(1)} %get-tuple-element.147), channel_id=1, source_target_pairs={{0,2},{1,3},{2,0},{3,1},{4,6},{5,7},{6,4},{7,5},{8,10},{9,11},{10,... | collective-permute-start | bytes 442376 | tf_op jit(solution)/shard_map/ppermute | solution.py:419
  265.0 21.7 %collective-permute-start.55 = (bf16[96,768]{1,0:T(8,128)(2,1)S(1)}, bf16[96,768]{1,0:T(8,128)(2,1)S(1)}, u32[]{:S(2)}, u32[]{:S(2)}) collective-permute-start(bf16[96,768]{1,0:T(8,128)(2,1)S(1)} %get-tuple-element.148), channel_id=1, source_target_pairs={{0,3},{1,2},{2,1},{3,0},{4,7},{5,6},{6,5},{7,4},{8,11},{9,10},{10,... | collective-permute-start | bytes 442376 | tf_op jit(solution)/shard_map/ppermute | solution.py:419
  284.1 19.4 %collective-permute-start.77 = (bf16[192,768]{1,0:T(8,128)(2,1)S(1)}, bf16[192,768]{1,0:T(8,128)(2,1)S(1)}, u32[]{:S(2)}, u32[]{:S(2)}) collective-permute-start(bf16[192,768]{1,0:T(8,128)(2,1)S(1)} %pad_maximum_fusion.7.refs_0_), channel_id=1, source_target_pairs={{0,16},{4,20},{8,24},{12,28},{16,0},{20,4},{24,8},{28,12},{1,17},{... | collective-permute-start | bytes 884744 | tf_op jit(solution)/shard_map/ppermute | solution.py:416
  287.7 17.3 %collective-permute-start.59 = (bf16[96,768]{1,0:T(8,128)(2,1)S(1)}, bf16[96,768]{1,0:T(8,128)(2,1)S(1)}, u32[]{:S(2)}, u32[]{:S(2)}) collective-permute-start(bf16[96,768]{1,0:T(8,128)(2,1)S(1)} %add_convert_fusion.14.refs_0_), channel_id=1, source_target_pairs={{0,16},{4,20},{8,24},{12,28},{16,0},{20,4},{24,8},{28,12},{1,17},{... | collective-permute-start | bytes 442376 | tf_op jit(solution)/shard_map/ppermute | solution.py:416
  (121 other events, 1093.8 us)

commit v3 on v2

--- a/solution.py
+++ b/solution.py
@@ -10,7 +10,7 @@
 HEAD_DIM = 64
 SEQ = 64
 SLICES = 8
-PARTS = 10
+PARTS = 16
 PAIR = 2 * SEQ
 LANES = 2 * HEAD_DIM
 BLOCK = 8
@@ -49,7 +49,7 @@
 
 def call(body, ins, outs, scratch, micros):
     def spec(vmem):
-        return pl.BlockSpec(memory_space=pltpu.VMEM if vmem else pl.ANY)
+        return pl.BlockSpec(memory_space=pltpu.VMEM if vmem else pltpu.HBM)
 
     return pl.pallas_call(
         body,
@@ -110,39 +110,48 @@
     copies.append(pltpu.make_async_copy(own_o, dst.at[3, pl.ds(0, cols)], sem.at[3]))
     k = 4
     size = parts[0].shape[1]
-    for part, p, at, n in slices_of(parts):
-        for s in range(part.shape[0]):
-            spot = att_spot(dst, s + 1, p, cols, size, at, n)
-            copies.append(pltpu.make_async_copy(part.at[s], spot, sem.at[k]))
-            k += 1
+    first = 1
+    for group in (parts[:SLICES], parts[SLICES:]):
+        for part, p, at, n in slices_of(group):
+            for s in range(part.shape[0]):
+                spot = att_spot(dst, first + s, p, cols, size, at, n)
+                copies.append(pltpu.make_async_copy(part.at[s], spot, sem.at[k]))
+                k += 1
+        first += group[0].shape[0]
     return start_all(copies)
 
 
 def fetch_rows(own, parts, dst, sem, base):
-    copies = [pltpu.make_async_copy(own, dst.at[0], sem.at[base])]
+    copies = [[pltpu.make_async_copy(own, dst.at[0], sem.at[base])]]
     k = base + 1
     size = parts[0].shape[1]
-    for part, p, at, n in slices_of(parts):
-        for s in range(part.shape[0]):
+    for s in range(parts[0].shape[0]):
+        copies.append([])
+        for part, p, at, n in slices_of(parts):
             spot = row_spot(dst, s + 1, p, size, at, n)
-            copies.append(pltpu.make_async_copy(part.at[s], spot, sem.at[k]))
+            copies[-1].append(pltpu.make_async_copy(part.at[s], spot, sem.at[k]))
             k += 1
-    return start_all(copies)
+    for group in copies:
+        start_all(group)
+    return copies
+
+
+def fetch_each(src, dst, sem):
+    return start_all(
+        [pltpu.make_async_copy(src.at[i], dst.at[i], sem.at[i]) for i in range(src.shape[0])]
+    )
 
 
 def n_copies(n_mp):
     return 4 + PARTS * (n_mp - 1)
 
 
-def send_slices(src_of, g_keep, g_send, sem, n_mp):
+def send_shard(src_of, s, g_keep, g_send, sem, n_mp):
     copies = []
-    k = 0
     for p in range(SLICES):
         dst = g_send if p & 1 else g_keep
-        for s in range(n_mp):
-            spot = dst.at[s // 2, p >> 2, (p >> 1) & 1, s % 2]
-            copies.append(pltpu.make_async_copy(src_of(s, p), spot, sem.at[k]))
-            k += 1
+        spot = dst.at[s // 2, p >> 2, (p >> 1) & 1, s % 2]
+        copies.append(pltpu.make_async_copy(src_of(s, p), spot, sem.at[SLICES * s + p]))
     return start_all(copies)
 
 
@@ -188,10 +197,11 @@
 def attention_forward(n_mp, cols, *refs):
     x, ids, b_q, b_v, b_attn, gain, shift, own_qkv, own_o = refs[:9]
     parts = refs[9 : 9 + PARTS]
-    q, k, v, ctx, hat_out, inv_out, h1 = refs[19:26]
-    w, sem = refs[26:]
+    q, k, v, ctx, hat_out, inv_out, h1, w_all, p_all = refs[25:34]
+    w, p_keep, sem, sem2 = refs[34:]
     copies = fetch_att(own_qkv, own_o, parts, w, sem, cols)
     wait_all(copies)
+    sent = start_all([pltpu.make_async_copy(w, w_all, sem2.at[0])])
     rows, width = x.shape
     q[...] = (nt(x[...], w[0]) + b_q[...]).astype(low)
     k[...] = nt(x[...], w[1]).astype(low)
@@ -204,15 +214,19 @@
         for j in range(width // LANES):
             lanes = slice(j * LANES, (j + 1) * LANES)
             raw = nt(q[at, lanes], split_heads(k[at, lanes]))
-            probs = [softmax_of(raw[:, i * PAIR : (i + 1) * PAIR], mask).astype(low) for i in (0, 1)]
-            out = nn(jnp.concatenate(probs, axis=1), split_heads(v[at, lanes]))
+            probs = [softmax_of(raw[:, i * PAIR : (i + 1) * PAIR], mask) for i in (0, 1)]
+            probs = jnp.concatenate(probs, axis=1)
+            p_keep[t, j] = probs
+            out = nn(probs.astype(low), split_heads(v[at, lanes]))
             ctx[at, lanes] = out.astype(low)
 
+    sent += start_all([pltpu.make_async_copy(p_keep, p_all, sem2.at[1])])
     z = x[...].astype(f32) + nn(ctx[...], w[3]) + b_attn[...]
     hat, inv = norm_rows(z)
     hat_out[...] = hat
     inv_out[...] = jnp.broadcast_to(inv, inv_out.shape)
     h1[...] = (hat * gain[...] + shift[...]).astype(low)
+    wait_all(sent)
 
 
 def gelu_pair(pre):
@@ -231,44 +245,107 @@
 def ffn_in_forward(n_mp, *refs):
     h1, b_mid, own_in = refs[:3]
     parts = refs[3 : 3 + SLICES]
-    hidden, slope, w_in, sem = refs[11:]
-    wait_all(fetch_rows(own_in, parts, w_in, sem, 0))
-
-    @pl.loop(0, n_mp)
-    def _(s):
+    hidden, slope, w_in, act_s, slope_s, sem, sem2 = refs[11:]
+    copies = fetch_rows(own_in, parts, w_in, sem, 0)
+    sent = []
+    for s in range(n_mp):
+        wait_all(copies[s])
         pre = nn(h1[...], w_in[s]) + b_mid[s]
         act, grad = gelu_pair(pre)
-        hidden[s] = act.astype(low)
-        slope[s] = grad.astype(low)
+        act_s[s] = act.astype(low)
+        slope_s[s] = grad.astype(low)
+        sent.append(pltpu.make_async_copy(act_s.at[s], hidden.at[s], sem2.at[2 * s]))
+        sent.append(pltpu.make_async_copy(slope_s.at[s], slope.at[s], sem2.at[2 * s + 1]))
+        start_all(sent[-2:])
+    wait_all(sent)
 
 
 def ffn_out_forward(n_mp, *refs):
-    hidden, hat1, gain1, shift1, b_out, gain2, shift2, own_out = refs[:8]
+    hat1, gain1, shift1, b_out, gain2, shift2, hidden, own_out = refs[:8]
     parts = refs[8 : 8 + SLICES]
     layer_out, hat_out, inv_out, first = refs[16:20]
-    w_out, acc, sem = refs[20:]
+    w_out, act_s, acc, sem, sem2 = refs[20:]
+    acts = fetch_each(hidden, act_s, sem2)
     copies = fetch_rows(own_out, parts, w_out, sem, 0)
     acc[...] = hat1[...] * gain1[...] + shift1[...] + b_out[...]
-    wait_all(copies)
-
-    @pl.loop(0, n_mp)
-    def _(s):
-        acc[...] += nn(hidden[s], w_out[s])
+    for s in range(n_mp):
+        wait_all([acts[s]] + copies[s])
+        acc[...] += nn(act_s[s], w_out[s])
 
     hat, inv = norm_rows(acc[...])
     hat_out[...] = hat
     inv_out[...] = jnp.broadcast_to(inv, inv_out.shape)
     out = (hat * gain2[...] + shift2[...]).astype(low)
     layer_out[...] = out
-    first[...] = jnp.zeros_like(first)
-    for i in range(out.shape[0] // SEQ):
-        first[i : i + 1] = out[i * SEQ : i * SEQ + 1].astype(f32)
+    rows = [out[i * SEQ : i * SEQ + 1].astype(f32) for i in range(out.shape[0] // SEQ)]
+    rows.append(jnp.zeros((BLOCK - len(rows), out.shape[1]), f32))
+    first[...] = jnp.concatenate(rows, axis=0).astype(low)
+
+
+def ranking(n_mp, sents, *refs):
+    ids_row, ids_col, w_pool, b_pool, scale = refs[:5]
+    parts = refs[5:9]
+    g_first, rows_out, g_out, g_bias, scale_out = refs[9:14]
+    got, g_all, sem = refs[14:]
+    me = lax.axis_index("mp")
+    copies = []
+    for p in range(SLICES):
+        for s in range(n_mp):
+            spot = got.at[slot(p) * n_mp + jnp.bitwise_xor(me, s)]
+            copies.append(
+                pltpu.make_async_copy(parts[p >> 1].at[s, p & 1], spot, sem.at[p * n_mp + s])
+            )
+    wait_all(start_all(copies))
+    n = ids_row.shape[1]
+    first = got[...].astype(f32).reshape(n, -1).astype(low)
+    rows_out[...] = first
+    pooled = jnp.tanh(nn(first, w_pool[...]) + b_pool[...])
+    inv_len = lax.rsqrt(jnp.sum(pooled * pooled, axis=-1, keepdims=True) + eps_norm)
+    emb = pooled * inv_len
+    emb_low = emb.astype(low)
+    cosine = nt(emb_low, emb_low)
+    row = lax.broadcasted_iota(jnp.int32, (n, n), 0)
+    col = lax.broadcasted_iota(jnp.int32, (n, n), 1)
+    even = lax.rem(row, 2) == 0
+    in_row = jnp.logical_and(even, lax.rem(row, BLOCK) < sents)
+    in_col = jnp.logical_and(lax.rem(col, 2) == 1, lax.rem(col, BLOCK) < sents)
+    in_both = jnp.logical_and(in_row, in_col)
+    same = jnp.logical_and(in_both, ids_col[...] == ids_row[...])
+    one = same.astype(f32)
+    diag = jnp.logical_and(in_both, col == row + 1).astype(f32)
+    shifted = cosine - margin * diag
+    logits = jnp.where(same, scale[...] * shifted, masked_low)
+    grad = jnp.zeros_like(cosine)
+    for axis in (1, 0):
+        expd = jnp.exp(logits - jnp.max(logits, axis=axis, keepdims=True))
+        expd = jnp.where(same, expd, 0.0)
+        total = jnp.maximum(jnp.sum(expd, axis=axis, keepdims=True), 1e-30)
+        count = jnp.maximum(jnp.sum(one, axis=axis, keepdims=True), 1.0)
+        grad = grad + (expd / total - diag) / count
+    scale_grad = jnp.sum(jnp.sum(grad * shifted, axis=1, keepdims=True), axis=0, keepdims=True)
+    scale_out[...] = scale[...] - step_rate * jnp.broadcast_to(scale_grad, scale_out.shape)
+    both = grad + grad.T
+    g_emb = jnp.zeros_like(pooled)
+    for _ in range(3):
+        part = both.astype(low)
+        both = both - part.astype(f32)
+        g_emb = g_emb + nn(part, emb_low)
+    g_emb = scale[0:1, 0:1] * g_emb
+    g_pooled = inv_len * (g_emb - emb * jnp.sum(emb * g_emb, axis=-1, keepdims=True))
+    g_pre = (g_pooled * (1.0 - pooled * pooled)).astype(low)
+    g_out[...] = g_pre
+    g_all[...] = g_pre.astype(f32)
+    g_bias[...] = jnp.sum(g_all[...], axis=0, keepdims=True)
+    at = (lax.axis_index("dp") * n_mp + me) * BLOCK
+    own = g_all[pl.ds(pl.multiple_of(at, BLOCK), BLOCK)].astype(low)
+    g_first[...] = nt(own, w_pool[...])
 
 
 def out_backward(n_mp, *refs):
     cot, g_first, hat, inv, gain, hidden = refs[:6]
     g_z2, small, keep, send = refs[6:10]
-    g_w, sem = refs[10:]
+    g_w, act_s, sem, sem2 = refs[10:]
+    acts = fetch_each(hidden, act_s, sem2)
     rows = cot.shape[0]
     g_z2[...] = cot[...].astype(f32)
     for i in range(rows // SEQ):
@@ -282,35 +359,36 @@
     small[0:1] = jnp.sum(g_z, axis=0, keepdims=True)
     g_ffn = g_z.astype(low)
 
-    @pl.loop(0, n_mp)
-    def _(s):
-        g_w[s] = tn(hidden[s], g_ffn).astype(low)
-
     size = keep.shape[-2]
-    wait_all(send_slices(lambda s, p: row_spot(g_w, s, p, size), keep, send, sem, n_mp))
+    sent = []
+    for s in range(n_mp):
+        acts[s].wait()
+        g_w[s] = tn(act_s[s], g_ffn).astype(low)
+        sent += send_shard(lambda s, p: row_spot(g_w, s, p, size), s, keep, send, sem, n_mp)
+    wait_all(sent)
 
 
 def in_backward(n_mp, *refs):
-    g_z2, slope, h1, hat, inv, gain, own_in, own_out = refs[:8]
+    g_z2, h1, hat, inv, gain, slope, own_in, own_out = refs[:8]
     in_parts = refs[8 : 8 + SLICES]
     out_parts = refs[16 : 16 + SLICES]
     g_z1, g_mid, small, keep, send = refs[24:29]
-    w_in, w_out, g_w, acc, sem, sem2 = refs[29:]
-    copies = fetch_rows(own_in, in_parts, w_in, sem, 0)
-    copies += fetch_rows(own_out, out_parts, w_out, sem, n_copies(n_mp))
-    wait_all(copies)
+    w_in, w_out, slope_s, g_w, acc, sem, sem2, sem3 = refs[29:]
+    slopes = fetch_each(slope, slope_s, sem3)
+    out_copies = fetch_rows(own_out, out_parts, w_out, sem, 0)
+    in_copies = fetch_rows(own_in, in_parts, w_in, sem, n_copies(n_mp))
     acc[...] = g_z2[...]
     g_ffn = g_z2[...].astype(low)
-
-    @pl.loop(0, n_mp)
-    def _(s):
-        g_pre = (nt(g_ffn, w_out[s]) * slope[s].astype(f32)).astype(low)
+    size = keep.shape[-2]
+    copies = []
+    for s in range(n_mp):
+        wait_all([slopes[s]] + out_copies[s])
+        g_pre = (nt(g_ffn, w_out[s]) * slope_s[s].astype(f32)).astype(low)
         g_mid[s] = jnp.sum(g_pre.astype(f32), axis=0, keepdims=True)
         g_w[s] = tn(h1[...], g_pre).astype(low)
+        copies += send_shard(lambda s, p: row_spot(g_w, s, p, size), s, keep, send, sem2, n_mp)
+        wait_all(in_copies[s])
         acc[...] += nt(g_pre, w_in[s])
-
-    size = keep.shape[-2]
-    copies = send_slices(lambda s, p: row_spot(g_w, s, p, size), keep, send, sem2, n_mp)
     g_h1 = acc[...]
     small[...] = jnp.zeros_like(small)
     small[1:2] = jnp.sum(g_h1 * hat[...], axis=0, keepdims=True)
@@ -322,43 +400,46 @@
 
 
 def attention_backward(n_mp, cols, *refs):
-    g_z1, q, k, v, ctx, ids, own_qkv, own_o = refs[:8]
-    parts = refs[8 : 8 + PARTS]
-    g_q, g_k, g_v, g_bias, g_wo = refs[18:23]
-    w, g_ctx, sem = refs[23:]
-    copies = fetch_att(own_qkv, own_o, parts, w, sem, cols)
+    g_z1, q, k, v, ctx, g_mid, small_one, small_two, w_all, p_all = refs[:10]
+    g_q, g_k, g_v, total, g_wo = refs[10:15]
+    w, p_keep, g_ctx, sem, sem2 = refs[15:]
+    fetch = start_all([pltpu.make_async_copy(w_all.at[3], w, sem.at[0])])
+    probs = fetch_each(p_all, p_keep, sem2)
     rows, width = g_z1.shape
     g_attn = g_z1[...].astype(low)
-    wait_all(copies)
-    g_ctx[...] = nt(g_attn, w[3]).astype(low)
-
-    @pl.loop(0, rows // PAIR)
-    def _(t):
-        at = pl.ds(pl.multiple_of(t * PAIR, PAIR), PAIR)
-        mask = pair_mask(ids[t])
+    wait_all(fetch)
+    g_ctx[...] = nt(g_attn, w[...]).astype(low)
+    for t in range(rows // PAIR):
+        at = slice(t * PAIR, (t + 1) * PAIR)
+        probs[t].wait()
         for j in range(width // LANES):
             lanes = slice(j * LANES, (j + 1) * LANES)
             q2, g2 = q[at, lanes], g_ctx[at, lanes]
             k2, v2 = split_heads(k[at, lanes]), split_heads(v[at, lanes])
-            raw = nt(q2, k2)
+            p = p_keep[t, j]
             g_p = nt(g2, v2)
-            p_low, g_raw = [], []
+            g_raw = []
             for i in (0, 1):
                 half = slice(i * PAIR, (i + 1) * PAIR)
-                p = softmax_of(raw[:, half], mask)
-                inner = jnp.sum(p * g_p[:, half], axis=-1, keepdims=True)
-                p_low.append(p.astype(low))
-                g_raw.append((p * (g_p[:, half] - inner) * 0.125).astype(low))
-            p_low = jnp.concatenate(p_low, axis=1)
+                inner = jnp.sum(p[:, half] * g_p[:, half], axis=-1, keepdims=True)
+                g_raw.append((p[:, half] * (g_p[:, half] - inner) * 0.125).astype(low))
             g_raw = jnp.concatenate(g_raw, axis=1)
-            g_v[at, lanes] = join_heads(tn(p_low, g2)).astype(low)
+            g_v[at, lanes] = join_heads(tn(p.astype(low), g2)).astype(low)
             g_q[at, lanes] = nn(g_raw, k2).astype(low)
             g_k[at, lanes] = join_heads(tn(g_raw, q2)).astype(low)
 
     g_wo[...] = tn(ctx[...], g_attn).astype(low)
-    g_bias[...] = jnp.zeros_like(g_bias)
-    g_bias[0:1] = jnp.sum(g_q[...].astype(f32), axis=0, keepdims=True)
-    g_bias[1:2] = jnp.sum(g_v[...].astype(f32), axis=0, keepdims=True)
+    total[...] = jnp.zeros_like(total)
+    total[0:3] = small_one[0:3]
+    total[3:6] = small_two[0:3]
+    b_q = jnp.sum(g_q[...].astype(f32), axis=0, keepdims=True)
+    b_v = jnp.sum(g_v[...].astype(f32), axis=0, keepdims=True)
+    for s in range(n_mp):
+        at = jnp.bitwise_xor(lax.axis_index("mp"), s)
+        total[pl.ds(BLOCK + at, 1)] = g_mid[s]
+        lanes = slice(s * cols, (s + 1) * cols)
+        total[pl.ds(BLOCK + n_mp + at, 1), 0:cols] = b_q[:, lanes]
+        total[pl.ds(BLOCK + n_mp + at, 1), cols : 2 * cols] = b_v[:, lanes]
 
 
 def attention_weights(n_mp, cols, *refs):
@@ -368,44 +449,45 @@
     g_w[1] = tn(g_k[...], x[...]).astype(low)
     g_w[2] = tn(g_v[...], x[...]).astype(low)
     size = keep.shape[-2]
-    wait_all(send_slices(lambda s, p: att_spot(g_w, s, p, cols, size), keep, send, sem, n_mp))
+    sent = []
+    for s in range(n_mp):
+        sent += send_shard(lambda s, p: att_spot(g_w, s, p, cols, size), s, keep, send, sem, n_mp)
+    wait_all(sent)
 
 
 def attention_inputs(n_mp, cols, *refs):
-    g_z1, g_q, g_k, g_v, own_qkv, own_o = refs[:6]
-    parts = refs[6 : 6 + PARTS]
-    g_x, w, sem = refs[16:]
-    wait_all(fetch_att(own_qkv, own_o, parts, w, sem, cols))
-    g_x[...] = g_z1[...] + nn(g_q[...], w[0]) + nn(g_k[...], w[1]) + nn(g_v[...], w[2])
-
-
-def finish_rows(*refs):
+    g_z1, g_q, g_k, g_v, w_all, g_x, w, sem = refs
+    fetch = start_all([pltpu.make_async_copy(w_all.at[i], w.at[i], sem.at[i]) for i in range(3)])
+    total = g_z1[...]
+    for i, g in enumerate((g_q, g_k, g_v)):
+        fetch[i].wait()
+        total = total + nn(g[...], w[i])
+    g_x[...] = total
+
+
+def finish_rows(cols, *refs):
     parts = refs[:SLICES]
-    out_a, out_b, got, sem = refs[SLICES:]
-    size = parts[0].shape[0] // 2
-    copies = []
+    if cols:
+        out, out_qkv, out_o, got, sem, got_att, sem_att = refs[SLICES:]
+    else:
+        out, got, sem = refs[SLICES:]
+    size = parts[0].shape[0] // (2 if cols else 1)
+    copies, more = [], []
     for p in range(SLICES):
-        for i in (0, 1):
-            part = parts[p].at[pl.ds(i * size, size)]
-            spot = row_spot(got, i, p, size)
-            copies.append(pltpu.make_async_copy(part, spot, sem.at[2 * p + i]))
-    wait_all(start_all(copies))
-    out_a[...] = got[0].astype(f32)
-    out_b[...] = got[1].astype(f32)
-
-
-def finish_att(cols, *refs):
-    parts = refs[:SLICES]
-    out_qkv, out_o, got, sem = refs[SLICES:]
-    size = parts[0].shape[0]
-    copies = [
-        pltpu.make_async_copy(parts[p], att_spot(got, 0, p, cols, size), sem.at[p])
-        for p in range(SLICES)
-    ]
-    wait_all(start_all(copies))
-    for i in range(3):
-        out_qkv[i] = got[i].astype(f32).T
-    out_o[...] = got[3].astype(f32)
+        part = parts[p].at[pl.ds(0, size)]
+        copies.append(pltpu.make_async_copy(part, row_spot(got, 0, p, size), sem.at[p]))
+        if cols:
+            part = parts[p].at[pl.ds(size, size)]
+            spot = att_spot(got_att, 0, p, cols, size)
+            more.append(pltpu.make_async_copy(part, spot, sem_att.at[p]))
+    start_all(copies + more)
+    wait_all(copies)
+    out[...] = got[0].astype(f32)
+    if cols:
+        wait_all(more)
+        for i in range(3):
+            out_qkv[i] = got_att[i].astype(f32)
+        out_o[...] = got_att[3].astype(f32)
 
 
 def make(mesh):
@@ -437,16 +519,17 @@
     def over_z(piece):
         return [mpx(piece, i) for i in range(1, n_mp)]
 
-    def over_xy(r):
-        return [dpx(r, 2), dpx(r, 4)]
+    def over_z_slow(own):
+        got = [mpx(own, 1)]
+        bit = 2
+        while bit < n_mp:
+            far = mpx(jnp.stack([own] + got), bit)
+            got += [far[i] for i in range(bit)]
+            bit *= 2
+        return got
 
     def over_plane(r):
         return [dpx(r, 2), dpx(r, 4), dpx(r, 6)]
-
-    def over_corner(near):
-        at_x, at_y = near
-        half = at_x.shape[1] // 2
-        return [dpx(at_y[:, :half], 2), dpx(at_x[:, half:], 4)]
 
     def over_core(parts):
         return parts + [dpx(part, 1) for part in parts]
@@ -488,17 +571,6 @@
         for w in u[1:]:
             total = total + w.astype(f32)
         return total.astype(low)
-
-    def sum_all(v):
-        bit = 1
-        while bit < n_dp:
-            v = v + dpx(v, bit)
-            bit *= 2
-        bit = 1
-        while bit < n_mp:
-            v = v + mpx(v, bit)
-            bit *= 2
-        return v
 
     def mp_natural(v):
         bits = [1 << i for i in reversed(range(n_mp.bit_length() - 1))]
@@ -605,18 +677,15 @@
         small = jnp.stack([small] + [r[size:] for r in att_r]).reshape(n_mp, -1).astype(f32)
         b_q, b_v = small[:, :cols].reshape(1, -1), small[:, cols : 2 * cols].reshape(1, -1)
         b_mid = small[:, None, 2 * cols : 2 * cols + units]
-        att_r = jnp.stack([r[:size] for r in att_r])
-        att_near = over_xy(att_r)
-        in_r = jnp.stack(over_z(after(own_piece(w_in), att_r)))
-        att_parts = over_core([att_r] + att_near + over_corner(att_near))
-        in_near = over_plane(after(in_r, *att_near))
-        out_own = after(own_piece(w_out), in_r, *att_near)
-        out_z = [mpx(out_own, 1)]
-        bit = 2
-        while bit < n_mp:
-            far = mpx(jnp.stack([out_own] + out_z), bit)
-            out_z += [far[i] for i in range(bit)]
-            bit *= 2
+        att_one = att_r[0][None, :size]
+        att_near = over_plane(att_one)
+        att_r = jnp.stack([r[:size] for r in after(att_r[1:], att_near[0])])
+        att_far = over_plane(att_r)
+        in_z = over_z(after(own_piece(w_in), att_r, *att_near))
+        att_parts = over_core([att_one] + att_near) + over_core([att_r] + att_far)
+        in_r = jnp.stack(in_z)
+        in_near = over_plane(after(in_r, *att_far))
+        out_z = over_z_slow(after(own_piece(w_out), in_r))
         nc = n_copies(n_mp)
         own_qkv = att_shard[: 3 * cols].reshape(3, cols, width)
 
@@ -632,72 +701,108 @@
 
         rows_low, rows_f = shape((rows, width), low), shape((rows, width), f32)
         thin = shape((rows, 128), f32)
-        query, key_part, value_part, context, hat_one, inv_one, h1 = call(
+        w_shape = shape((4, n_mp * cols, width), low)
+        p_shape = shape((rows // PAIR, width // LANES, PAIR, 2 * PAIR), f32)
+        query, key_part, value_part, context, hat_one, inv_one, h1, w_all, p_all = call(
             functools.partial(attention_forward, n_mp, cols),
             here(after(inputs, out_z[0]), ids, b_q, b_v, row(b_attn), gain_one, shift_one)
             + away(own_qkv, w_attn, *att_parts),
-            here(rows_low, rows_low, rows_low, rows_low, rows_f, thin, rows_low),
-            [vmem((4, n_mp * cols, width), low), dma((nc,))],
+            here(rows_low, rows_low, rows_low, rows_low, rows_f, thin, rows_low)
+            + away(w_shape, p_shape),
+            [vmem(w_shape.shape, low), vmem(p_shape.shape, f32), dma((nc,)), dma((2,))],
             11,
         )
         out_r = jnp.stack(after(out_z, h1))
         out_near = over_plane(out_r)
         in_parts = over_core(after([in_r] + in_near, h1))
         mid = shape((n_mp, rows, units), low)
+        tiny_shape = shape((BLOCK, width), f32)
+        ids_row = jnp.repeat(pair_ids.reshape(-1, sents // 2), 2, axis=1)
+        ids_row = jnp.pad(ids_row, ((0, 0), (0, BLOCK - sents))).reshape(1, -1)
         hidden, slope = call(
             functools.partial(ffn_in_forward, n_mp),
             here(h1, b_mid) + away(w_in, *in_parts),
-            here(mid, mid),
-            [vmem((n_mp, width, units), low), dma((nc,))],
+            away(mid, mid),
+            [vmem((n_mp, width, units), low), vmem(mid.shape, low), vmem(mid.shape, low)]
+            + [dma((nc,)), dma((2 * n_mp,))],
             9,
         )
         out_parts = over_core(after([out_r] + out_near, hidden))
         layer_out, hat_two, inv_two, own_first = call(
             functools.partial(ffn_out_forward, n_mp),
-            here(hidden, hat_one, gain_one, shift_one, row(b_out), gain_two, shift_two)
-            + away(w_out, *out_parts),
-            here(rows_low, rows_f, thin, shape((BLOCK, width), f32)),
-            [vmem((n_mp, units, width), low), vmem((rows, width), f32), dma((nc,))],
+            here(hat_one, gain_one, shift_one, row(b_out), gain_two, shift_two)
+            + away(hidden, w_out, *out_parts),
+            here(rows_low, rows_f, thin, shape((BLOCK, width), low)),
+            [vmem((n_mp, units, width), low), vmem(mid.shape, low), vmem((rows, width), f32)]
+            + [dma((nc,)), dma((n_mp,))],
             6,
         )
-        grad_first, grad_pool, grad_b_pool, new_scale = rank_part(
-            gather_all(own_first), sents, pair_ids, w_pool, b_pool, scale
-        )
+        if n_dp == SLICES:
+            n = n_dp * n_mp * BLOCK
+            r = jnp.stack([own_first, dpx(own_first, 1)])
+            r = jnp.stack([r] + over_z(r))
+            grad_first, all_first, all_ppre, grad_b_pool, new_scale = call(
+                functools.partial(ranking, n_mp, sents),
+                here(ids_row, ids_row.reshape(n, 1), w_pool, row(b_pool))
+                + here(jnp.broadcast_to(scale[None], (1, n)))
+                + away(r, *over_plane(r)),
+                here(tiny_shape, shape((n, width), low), shape((n, width), low))
+                + here(shape((1, width), f32), shape((1, n), f32)),
+                [vmem((n_dp * n_mp, BLOCK, width), low), vmem((n, width), f32)]
+                + [dma((n_dp * n_mp,))],
+                6,
+            )
+            grad_b_pool, new_scale = grad_b_pool[0], new_scale[0, :1]
+        else:
+            grad_first, grad_pool, grad_b_pool, new_scale = rank_part(
+                gather_all(own_first), sents, pair_ids, w_pool, b_pool, scale
+            )
         lot = shape((2, 2, 2, n_mp // 2, size, width), low)
         tiny = shape((BLOCK, width), f32)
         grad_z2, small_two, keep_o, send = call(
             functools.partial(out_backward, n_mp),
-            here(out_cot, grad_first, hat_two, inv_two, gain_two, hidden),
+            here(out_cot, grad_first, hat_two, inv_two, gain_two) + away(hidden),
             here(rows_f, tiny) + away(lot, lot),
-            [vmem((n_mp, units, width), low), dma((SLICES * n_mp,))],
+            [vmem((n_mp, units, width), low), vmem(mid.shape, low)]
+            + [dma((SLICES * n_mp,)), dma((n_mp,))],
             10,
         )
         got_o = dpx(send, 1)
         grad_z1, grad_b_in, small_one, keep_i, send = call(
             functools.partial(in_backward, n_mp),
-            here(grad_z2, slope, h1, hat_one, inv_one, gain_one) + away(w_in, w_out, *in_parts, *out_parts),
+            here(grad_z2, h1, hat_one, inv_one, gain_one)
+            + away(slope, w_in, w_out, *in_parts, *out_parts),
             here(rows_f, shape((n_mp, 1, units), f32), tiny) + away(lot, lot),
             [
                 vmem((n_mp, width, units), low),
                 vmem((n_mp, units, width), low),
+                vmem(mid.shape, low),
                 vmem((n_mp, width, units), low),
                 vmem((rows, width), f32),
                 dma((2 * nc,)),
                 dma((SLICES * n_mp,)),
+                dma((n_mp,)),
             ],
             17,
         )
         got_i = dpx(send, 1)
         step_o = reduce_one(keep_o, after(got_o, grad_z1))
         a_o, b_o = dpx(step_o[0], 2), dpx(step_o[1], 4)
-        grad_q, grad_k, grad_v, grad_b_qv, grad_wo = call(
+        grad_q, grad_k, grad_v, total, grad_wo = call(
             functools.partial(attention_backward, n_mp, cols),
-            here(after(grad_z1, step_o[0], step_o[1]), query, key_part, value_part, context, ids)
-            + away(own_qkv, w_attn, *att_parts),
-            here(rows_low, rows_low, rows_low, tiny, shape((n_mp * cols, width), low)),
-            [vmem((4, n_mp * cols, width), low), vmem((rows, width), low), dma((nc,))],
-            12,
-        )
+            here(after(grad_z1, step_o[0], step_o[1]), query, key_part, value_part, context)
+            + here(grad_b_in, small_one, small_two)
+            + away(w_all, p_all),
+            here(rows_low, rows_low, rows_low, shape((BLOCK + 2 * n_mp, width), f32))
+            + here(shape((n_mp * cols, width), low)),
+            [vmem((n_mp * cols, width), low), vmem(p_shape.shape, f32), vmem((rows, width), low)]
+            + [dma((1,)), dma((rows // PAIR,))],
+            15,
+        )
+        hops = [functools.partial(mpx, bit=1 << i) for i in range(n_mp.bit_length() - 1)]
+        hops += [functools.partial(dpx, bit=1)]
+        hops += [functools.partial(dpx, bit=1 << i) for i in range(3, n_dp.bit_length() - 1)]
+        hop = hops[0](total)
         step_i = reduce_one(keep_i, after(got_i, grad_q))
         a_i, b_i = dpx(step_i[0], 2), dpx(step_i[1], 4)
         step_o = reduce_two(step_o[2], step_o[3], after(a_o, grad_q), after(b_o, grad_q))
@@ -708,69 +813,69 @@
             + here(grad_q, grad_k, grad_v, grad_wo),
             away(lot, lot),
             [vmem((4, n_mp * cols, width), low), dma((SLICES * n_mp,))],
-            6,
+            7,
         )
         got_a = dpx(send, 1)
+        total = total + after(hop, keep_a)
+        hop = hops[1](total)
         (input_grad,) = call(
             functools.partial(attention_inputs, n_mp, cols),
-            here(grad_z1, after(grad_q, keep_a), grad_k, grad_v)
-            + away(own_qkv, w_attn, *att_parts),
+            here(grad_z1, after(grad_q, keep_a), grad_k, grad_v) + away(w_all),
             here(rows_f),
-            [vmem((4, n_mp * cols, width), low), dma((nc,))],
-            6,
+            [vmem((3, n_mp * cols, width), low), dma((3,))],
+            7,
         )
         step_a = reduce_one(keep_a, after(got_a, input_grad))
         a_a, b_a = dpx(step_a[0], 2), dpx(step_a[1], 4)
-        step_o = after(reduce_three(*step_o[2:], a2_o, b2_o), step_a[0])
+        step_o = reduce_three(*step_o[2:], *after([a2_o, b2_o], step_a[0], step_a[1]))
         z_o = [mpx(step_o[i], i) for i in range(1, n_mp)]
-        step_i = reduce_two(step_i[2], step_i[3], after(a_i, step_o[0]), b_i)
+        total = total + after(hop, step_a[0])
+        hop = hops[2](total)
+        step_i = reduce_two(step_i[2], step_i[3], *after([a_i, b_i], step_a[0], step_a[1]))
         a2_i, b2_i = dpx(step_i[0], 4), dpx(step_i[1], 2)
-        step_a = reduce_two(step_a[2], step_a[3], after(a_a, step_i[0]), after(b_a, step_i[1]))
+        step_a = reduce_two(step_a[2], step_a[3], *after([a_a, b_a], step_i[0], step_i[1]))
         a2_a, b2_a = dpx(step_a[0], 4), dpx(step_a[1], 2)
-        step_i = after(reduce_three(*step_i[2:], a2_i, b2_i), step_a[0])
+        red_out = reduce_last(after([step_o[0]] + z_o, step_a[0]))
+        total = total + after(hop, step_a[0])
+        for h in hops[3:]:
+            total = total + h(total)
+        step_i = reduce_three(*step_i[2:], *after([a2_i, b2_i], step_a[0], step_a[1]))
         z_i = [mpx(step_i[i], i) for i in range(1, n_mp)]
-        step_a = after(reduce_three(*step_a[2:], a2_a, b2_a), step_i)
+        step_a = reduce_three(*step_a[2:], *after([a2_a, b2_a], step_i[0]))
         z_a = [mpx(step_a[i], i) for i in range(1, n_mp)]
-        red_out = reduce_last([step_o[0]] + z_o)
-        red_in = reduce_last([step_i[0]] + z_i)
-        red_att = reduce_last([step_a[0]] + z_a)
-        grad_b_qv = grad_b_qv[:2].reshape(2, n_mp, cols).transpose(1, 0, 2)
-        total = jnp.concatenate(
-            [
-                mp_natural(grad_b_qv).reshape(-1),
-                mp_natural(grad_b_in).reshape(-1),
-                small_one[:3].reshape(-1),
-                small_two[:3].reshape(-1),
-            ]
-        )
-        total = sum_all(after(total, step_a[0]))
-        n_qv, n_in = n_mp * 2 * cols, n_mp * units
+        red_in = reduce_last(after([step_i[0]] + z_i, step_a[0]))
+        out_own = plane_parts(red_out)
+        total = total + dpx(after(total, step_a[0]), 2)
+        total = total + dpx(total, 4)
+        red_att = reduce_last(after([step_a[0]] + z_a, total))
+        last_own = plane_parts(jnp.concatenate([red_in, red_att]))
+        if n_dp == SLICES:
+            grad_pool = tn(after(all_first, step_a[0]), all_ppre)
         take = lax.axis_index("mp")
-        out_b_qv = lax.dynamic_slice_in_dim(total[:n_qv].reshape(n_mp, 2, cols), take, 1, 0)[0]
-        out_b_in = lax.dynamic_slice_in_dim(
-            total[n_qv : n_qv + n_in].reshape(n_mp, -1), take, 1, 0
-        )[0]
-        total = total[n_qv + n_in :].reshape(6, width)
+        out_b_in = lax.dynamic_slice_in_dim(total, BLOCK + take, 1, 0)[0]
+        out_b_qv = lax.dynamic_slice_in_dim(total, BLOCK + n_mp + take, 1, 0)
+        out_b_qv = out_b_qv[0, : 2 * cols].reshape(2, cols)
         whole = shape((SLICES * size, width), f32)
 
-        done_in, done_out = call(
-            finish_rows,
-            away(*plane_parts(jnp.concatenate([red_in, red_out]))),
-            here(whole, whole),
-            [vmem((2, SLICES * size, width), low), dma((2 * SLICES,))],
+        (done_out,) = call(
+            functools.partial(finish_rows, 0),
+            away(*out_own),
+            here(whole),
+            [vmem((1, SLICES * size, width), low), dma((SLICES,))],
+            3,
+        )
+        done_in, done_qkv, done_attn = call(
+            functools.partial(finish_rows, cols),
+            away(*last_own),
+            here(whole, shape((3, cols, width), f32), shape((cols, width), f32)),
+            [vmem((1, SLICES * size, width), low), dma((SLICES,))]
+            + [vmem((4, cols, width), low), dma((SLICES,))],
             4,
-        )
-        done_qkv, done_attn = call(
-            functools.partial(finish_att, cols),
-            away(*plane_parts(red_att)),
-            here(shape((3, width, cols), f32), shape((cols, width), f32)),
-            [vmem((4, cols, width), low), dma((SLICES,))],
-            3,
         )
         return (
             layer_out,
             input_grad,
-            done_qkv,
+            done_qkv.transpose(0, 2, 1),
             out_b_qv,
             done_attn,
             total[0],

time: 323 us -> 303 us (0.938); the launches traced: 322 us -> 298 us
  waiting for transfers between devices: 85.3 us -> 76 us
  other arithmetic: 29.1 us -> 20.9 us
  local copies, waits for them, and re-layouts: 26 us -> 19 us
  starting transfers between devices: 78 us -> 82.2 us
    ppermute x22, waiting for transfers between devices: 29.1 us -> 21.6 us  [mpx(): return lax.ppermute(x, 'mp', [(i, i ^ bit) for i in range(n_mp)])]
    ppermute x59 -> x64, starting transfers between devices: 42.1 us -> 45.5 us  [dpx(): return lax.ppermute(x, 'dp', [(i, i ^ bit) for i in range(n_dp)])]
    ppermute x59 -> x64, waiting for transfers between devices: 56.2 us -> 54.4 us  [dpx(): return lax.ppermute(x, 'dp', [(i, i ^ bit) for i in range(n_dp)])]
    unnamed x135 -> x143, local copies, waits for them, and re-layouts: 7.11 us -> 5.52 us
    pallas_call x10 -> x11, Pallas kernels: 95 us -> 95.7 us  [call(): pl.pallas_call(body, out_shape=[jax.ShapeDtypeStruct(o.shape, o.dtype) fo...]
  transfers between devices with their start and end apart: 81 -> 86, of which waited for: 29 -> 29; matrix products, arithmetic and copies ran while one was open for 14% -> 10% of each run, Pallas kernels for 22% -> 20%
where the time goes in v3:
time: 303 us; the launch traced here: 298 us
  Pallas kernels  95.7 us (32%)
  starting transfers between devices  82.2 us (27%)
  waiting for transfers between devices  76 us (25%)
  other arithmetic  20.9 us (7%)
  local copies, waits for them, and re-layouts  19 us (6%)
    pallas_call x11, Pallas kernels, call(): pl.pallas_call(body, out_shape=[jax.ShapeDtypeStruct(o.shape, o.dtype) fo...  95.7 us
    ppermute x64, waiting for transfers between devices, dpx(): return lax.ppermute(x, 'dp', [(i, i ^ bit) for i in range(n_dp)])  54.4 us
    ppermute x64, starting transfers between devices, dpx(): return lax.ppermute(x, 'dp', [(i, i ^ bit) for i in range(n_dp)])  45.5 us
    ppermute x22, starting transfers between devices, mpx(): return lax.ppermute(x, 'mp', [(i, i ^ bit) for i in range(n_mp)])  36.7 us
    ppermute x22, waiting for transfers between devices, mpx(): return lax.ppermute(x, 'mp', [(i, i ^ bit) for i in range(n_mp)])  21.6 us
    convert_element_type x12, other arithmetic, add(): return (a.astype(f32) + b.astype(f32)).astype(low)  12.7 us
  transfers between devices with their start and end apart: 86, of which 29 were waited for; matrix products, arithmetic and copies ran while one was open for 10% of the time, Pallas kernels for 20%

profile of v3, /device:TPU:0, one launch (start us, length us, event | category | flops | bytes accessed | tf_op | source)
XLA Modules:
  0.0 298.3 jit_solution(15684647400204360575)
XLA Ops:
  3.2 3.1 %collective-permute-start.2 = (bf16[98,768]{1,0:T(8,128)(2,1)S(1)}, bf16[98,768]{1,0:T(8,128)(2,1)S(1)}, u32[]{:S(2)}, u32[]{:S(2)}) collective-permute-start(bf16[98,768]{1,0:T(8,128)(2,1)S(1)} %pad_maximum_fusion.5), channel_id=1, source_target_pairs={{0,1},{1,0},{2,3},{3,2},{4,5},{5,4},{6,7},{7,6},{8,9},{9,8},{10,11... | collective-permute-start | bytes 451592 | tf_op jit(solution)/shard_map/ppermute | solution.py:501
  8.9 3.9 %collective-permute-done.2 = bf16[98,768]{1,0:T(8,128)(2,1)S(1)} collective-permute-done((bf16[98,768]{1,0:T(8,128)(2,1)S(1)}, bf16[98,768]{1,0:T(8,128)(2,1)S(1)}, u32[]{:S(2)}, u32[]{:S(2)}) %collective-permute-start.2) | collective-permute-done | bytes 150560 | tf_op jit(solution)/shard_map/ppermute | solution.py:501
  21.2 2.8 collective-permute-done.4.refs_11_
  26.4 4.0 %collective-permute-start.8 = (bf16[96,768]{1,0:T(8,128)(2,1)S(1)}, bf16[96,768]{1,0:T(8,128)(2,1)S(1)}, u32[]{:S(2)}, u32[]{:S(2)}) collective-permute-start(bf16[96,768]{1,0:T(8,128)(2,1)S(1)} %constant_dynamic-slice_fusion), channel_id=1, source_target_pairs={{0,3},{1,2},{2,1},{3,0},{4,7},{5,6},{6,5},{7,4},{8,11},{9,10},{10,... | collective-permute-start | bytes 442376 | tf_op jit(solution)/shard_map/ppermute | solution.py:501
  36.0 3.1 %collective-permute-done.7 = bf16[96,768]{1,0:T(8,128)(2,1)S(1)} collective-permute-done((bf16[96,768]{1,0:T(8,128)(2,1)S(1)}, bf16[96,768]{1,0:T(8,128)(2,1)S(1)}, u32[]{:S(2)}, u32[]{:S(2)}) %collective-permute-start.7) | collective-permute-done | bytes 147488 | tf_op jit(solution)/shard_map/ppermute | solution.py:501
  43.6 3.1 %collective-permute-done.9 = bf16[96,768]{1,0:T(8,128)(2,1)S(1)} collective-permute-done((bf16[96,768]{1,0:T(8,128)(2,1)S(1)}, bf16[96,768]{1,0:T(8,128)(2,1)S(1)}, u32[]{:S(2)}, u32[]{:S(2)}) %collective-permute-start.9) | collective-permute-done | bytes 147488 | tf_op jit(solution)/shard_map/ppermute | solution.py:501
  53.5 11.9 %shard_map.314 = (bf16[384,768]{1,0:T(8,128)(2,1)}, bf16[384,768]{1,0:T(8,128)(2,1)}, bf16[384,768]{1,0:T(8,128)(2,1)}, bf16[384,768]{1,0:T(8,128)(2,1)}, f32[38...) custom-call(bf16[384,768]{1,0:T(8,128)(2,1)} %refs_0_.3, ...), custom_call_target="tpu_custom_call" | custom-call | flops 12099999744 | tf_op jit(solution)/shard_map/pallas_call | solution.py:54
  65.5 4.1 %collective-permute-done.22.refs_5_.refs_10_ = bf16[3,96,768]{2,1,0:T(8,128)(2,1)S(1)} collective-permute-done((bf16[3,96,768]{2,1,0:T(8,128)(2,1)S(1)}, bf16[3,96,768]{2,1,0:T(8,128)(2,1)S(1)}, u32[]{:S(2)}, u32[]{:S(2)}) %collective-permute-start.22) | collective-permute-done | bytes 442400 | tf_op jit(solution)/shard_map/ppermute | solution.py:498
  78.2 9.8 %shard_map.315 = (bf16[4,384,768]{2,1,0:T(8,128)(2,1)}, bf16[4,384,768]{2,1,0:T(8,128)(2,1)}) custom-call(bf16[384,768]{1,0:T(8,128)(2,1)} %get-tuple-element.114.refs_0_.refs_1_, f32[4,1,768]{2,1,0:T(1,128)} %broadcast_in_dim.65.refs_1_, bf16[768,768]{1,0:T(8,128)(2,1)} %refs_6_.1, bf16[3,96,768]{2,1,0:T(8,128)(2,1)} %copy-done.9, ...), custom_call_target="tpu_custom_call" | custom-call | flops 9900000256 | tf_op jit(solution)/shard_map/pallas_call | solution.py:54
  87.9 7.4 %collective-permute-done.30.refs_10_.refs_18_ = bf16[3,96,768]{2,1,0:T(8,128)(2,1)S(1)} collective-permute-done((bf16[3,96,768]{2,1,0:T(8,128)(2,1)S(1)}, bf16[3,96,768]{2,1,0:T(8,128)(2,1)S(1)}, u32[]{:S(2)}, u32[]{:S(2)}) %collective-permute-start.30) | collective-permute-done | bytes 442400 | tf_op jit(solution)/shard_map/ppermute | solution.py:498
  99.9 8.9 %shard_map.316 = (bf16[384,768]{1,0:T(8,128)(2,1)}, f32[384,768]{1,0:T(8,128)}, f32[384,128]{1,0:T(8,128)}, bf16[8,768]{1,0:T(8,128)(2,1)}) custom-call(f32[384,768]{1,0:T(8,128)} %get-tuple-element.113.refs_0_.refs_2_, f32[1,768]{1,0:T(1,128)} %reshape.221.refs_5_.refs_1_.refs_4_, f32[1,768]{1,0:T(1,128)} %reshape.222.refs_6_.refs_2_, ...), custom_call_target="tpu_custom_call" | custom-call | flops 6600000000 | tf_op jit(solution)/shard_map/pallas_call | solution.py:54
  126.7 5.9 %shard_map.317 = (f32[8,768]{1,0:T(8,128)}, bf16[256,768]{1,0:T(8,128)(2,1)}, bf16[256,768]{1,0:T(8,128)(2,1)}, f32[1,768]{1,0:T(1,128)}, f32[1,256]{1,0:T(1,128)}) custom-call(s32[1,256]{1,0:T(1,128)} %reshape.219.refs_0_, s32[256,1]{1,0:T(8,128)} %reshape_reshape.4.refs_1_, bf16[768,768]{1,0:T(8,128)(2,1)} %refs_2_.3, f32[1,768]{1,0:T(1,128)} %reshape.226.refs_3_, ...), custom_call_target="tpu_custom_call" | custom-call | flops 6600000000 | tf_op jit(solution)/shard_map/pallas_call | solution.py:54
  132.7 9.2 %shard_map.318 = (f32[384,768]{1,0:T(8,128)}, f32[8,768]{1,0:T(8,128)}, bf16[2,2,2,2,96,768]{5,4,3,2,1,0:T(8,128)(2,1)}, bf16[2,2,2,2,96,768]{5,4,3,2,1,0:T(8,128)(2,1)}) custom-call(bf16[384,768]{1,0:T(8,128)(2,1)} %refs_0_.2, f32[8,768]{1,0:T(8,128)} %get-tuple-element.130.refs_1_, f32[384,768]{1,0:T(8,128)} %get-tuple-element.131.refs_2_, ...), custom_call_target="tpu_custom_call" | custom-call | flops 11000000512 | tf_op jit(solution)/shard_map/pallas_call | solution.py:54
  141.9 18.2 %shard_map.319 = (f32[384,768]{1,0:T(8,128)}, f32[4,1,768]{2,1,0:T(1,128)}, f32[8,768]{1,0:T(8,128)}, bf16[2,2,2,2,96,768]{5,4,3,2,1,0:T(8,128)(2,1)}, bf16[2,2,2,2,96,768]{5,4,3,2,1,0:T(8,128)(2,1)}) custom-call(f32[384,768]{1,0:T(8,128)} %get-tuple-element.133.refs_0_, bf16[384,768]{1,0:T(8,128)(2,1)} %get-tuple-element.114.refs_0_.refs_1_, ...), custom_call_target="tpu_custom_call" | custom-call | flops 18699999232 | tf_op jit(solution)/shard_map/pallas_call | solution.py:54
  164.9 11.6 %shard_map.320 = (bf16[384,768]{1,0:T(8,128)(2,1)}, bf16[384,768]{1,0:T(8,128)(2,1)}, bf16[384,768]{1,0:T(8,128)(2,1)}, f32[16,768]{1,0:T(8,128)}, bf16[768,768]{1,0:T(8,128)(2,1)}) custom-call(f32[384,768]{1,0:T(8,128)} %get-tuple-element.140.refs_0_, bf16[384,768]{1,0:T(8,128)(2,1)} %get-tuple-element.141.refs_1_, ...), custom_call_target="tpu_custom_call" | custom-call | flops 16499999744 | tf_op jit(solution)/shard_map/pallas_call | solution.py:54
  184.2 6.5 %shard_map.321 = (bf16[2,2,2,2,96,768]{5,4,3,2,1,0:T(8,128)(2,1)}, bf16[2,2,2,2,96,768]{5,4,3,2,1,0:T(8,128)(2,1)}) custom-call(bf16[384,768]{1,0:T(8,128)(2,1)} %refs_0_.3, bf16[384,768]{1,0:T(8,128)(2,1)} %get-tuple-element.161.refs_1_, bf16[384,768]{1,0:T(8,128)(2,1)} %get-tuple-element.157.refs_2_, bf16[384,768]{1,0:T(8,128)(2,1)} %get-tuple-element.158.refs_3_, ...), custom_call_target="tpu_custom_call" | custom-call | flops 7699999744 | tf_op jit(solution)/shard_map/pallas_call | solution.py:54
  195.9 6.6 %shard_map.322 = f32[384,768]{1,0:T(8,128)} custom-call(f32[384,768]{1,0:T(8,128)} %get-tuple-element.140.refs_0_, bf16[384,768]{1,0:T(8,128)(2,1)} %get-tuple-element.161.refs_1_, bf16[384,768]{1,0:T(8,128)(2,1)} %get-tuple-element.157.refs_2_, bf16[384,768]{1,0:T(8,128)(2,1)} %get-tuple-element.158.refs_3_, ...), custom_call_target="tpu_custom_call" | custom-call | flops 7699999744 | tf_op jit(solution)/shard_map/pallas_call | solution.py:54
  218.3 8.9 %collective-permute-done.52 = bf16[2,2,96,768]{3,2,1,0:T(8,128)(2,1)S(1)} collective-permute-done((bf16[2,2,96,768]{3,2,1,0:T(8,128)(2,1)S(1)}, bf16[2,2,96,768]{3,2,1,0:T(8,128)(2,1)S(1)}, u32[]{:S(2)}, u32[]{:S(2)}) %collective-permute-start.52) | collective-permute-done | bytes 589856 | tf_op jit(solution)/shard_map/ppermute | solution.py:498
  230.6 3.4 %collective-permute-done.50 = bf16[2,96,768]{2,1,0:T(8,128)(2,1)S(1)} collective-permute-done((bf16[2,96,768]{2,1,0:T(8,128)(2,1)S(1)}, bf16[2,96,768]{2,1,0:T(8,128)(2,1)S(1)}, u32[]{:S(2)}, u32[]{:S(2)}) %collective-permute-start.50) | collective-permute-done | bytes 294944 | tf_op jit(solution)/shard_map/ppermute | solution.py:498
  256.2 6.2 %collective-permute-start.59 = (bf16[96,768]{1,0:T(8,128)(2,1)S(1)}, bf16[96,768]{1,0:T(8,128)(2,1)S(1)}, u32[]{:S(2)}, u32[]{:S(2)}) collective-permute-start(bf16[96,768]{1,0:T(8,128)(2,1)S(1)} %get-tuple-element.228), channel_id=1, source_target_pairs={{0,1},{1,0},{2,3},{3,2},{4,5},{5,4},{6,7},{7,6},{8,9},{9,8},{10,11... | collective-permute-start | bytes 442376 | tf_op jit(solution)/shard_map/ppermute | solution.py:501
  265.7 6.0 %collective-permute-done.60 = bf16[96,768]{1,0:T(8,128)(2,1)S(1)} collective-permute-done((bf16[96,768]{1,0:T(8,128)(2,1)S(1)}, bf16[96,768]{1,0:T(8,128)(2,1)S(1)}, u32[]{:S(2)}, u32[]{:S(2)}) %collective-permute-start.60) | collective-permute-done | bytes 147488 | tf_op jit(solution)/shard_map/ppermute | solution.py:501
  276.7 3.0 shard_map.324
  281.7 6.9 %collective-permute-done.70.refs_4_ = bf16[192,768]{1,0:T(8,128)(2,1)S(1)} collective-permute-done((bf16[192,768]{1,0:T(8,128)(2,1)S(1)}, bf16[192,768]{1,0:T(8,128)(2,1)S(1)}, u32[]{:S(2)}, u32[]{:S(2)}) %collective-permute-start.70) | collective-permute-done | bytes 294944 | tf_op jit(solution)/shard_map/ppermute | solution.py:498
  294.0 4.1 %shard_map.323 = (f32[768,768]{1,0:T(8,128)}, f32[3,192,768]{2,1,0:T(8,128)}, f32[192,768]{1,0:T(8,128)}) custom-call(bf16[192,768]{1,0:T(8,128)(2,1)} %copy-done.15, bf16[192,768]{1,0:T(8,128)(2,1)} %copy-done.47, bf16[192,768]{1,0:T(8,128)(2,1)} %copy-done.44, bf16[192,768]{1,0:T(8,128)(2,1)} %copy-done.48, bf16[192,768]{1,0:T(8,128)(2,1)} %copy-done.45, ...), custom_call_target="tpu_custom_call" | custom-call | flops 4400000000 | tf_op jit(solution)/shard_map/pallas_call | solution.py:54
  (379 shorter events, 137.1 us)
Async XLA Ops:
  6.3 14.8 %collective-permute-start = (bf16[98,768]{1,0:T(8,128)(2,1)S(1)}, bf16[98,768]{1,0:T(8,128)(2,1)S(1)}, u32[]{:S(2)}, u32[]{:S(2)}) collective-permute-start(bf16[98,768]{1,0:T(8,128)(2,1)S(1)} %pad_maximum_fusion.5), channel_id=1, source_target_pairs={{0,2},{1,3},{2,0},{3,1},{4,6},{5,7},{6,4},{7,5},{8,10},{9,11},{10,... | collective-permute-start | bytes 451592 | tf_op jit(solution)/shard_map/ppermute | solution.py:501
  48.2 17.3 %collective-permute-start.21 = (bf16[3,96,768]{2,1,0:T(8,128)(2,1)S(1)}, bf16[3,96,768]{2,1,0:T(8,128)(2,1)S(1)}, u32[]{:S(2)}, u32[]{:S(2)}) collective-permute-start(bf16[3,96,768]{2,1,0:T(8,128)(2,1)S(1)} %pad_maximum_fusion.refs_3_.refs_8_), channel_id=1, source_target_pairs={{0,8},{4,12},{8,0},{12,4},{16,24},{20,28},{24,16},{28,20},{1,9},{5... | collective-permute-start | bytes 1327112 | tf_op jit(solution)/shard_map/ppermute | solution.py:498
  48.9 20.7 %collective-permute-start.22 = (bf16[3,96,768]{2,1,0:T(8,128)(2,1)S(1)}, bf16[3,96,768]{2,1,0:T(8,128)(2,1)S(1)}, u32[]{:S(2)}, u32[]{:S(2)}) collective-permute-start(bf16[3,96,768]{2,1,0:T(8,128)(2,1)S(1)} %pad_maximum_fusion.refs_3_.refs_8_), channel_id=1, source_target_pairs={{0,16},{4,20},{8,24},{12,28},{16,0},{20,4},{24,8},{28,12},{1,17},{... | collective-permute-start | bytes 1327112 | tf_op jit(solution)/shard_map/ppermute | solution.py:498
  50.3 21.0 %collective-permute-start.23 = (bf16[3,96,768]{2,1,0:T(8,128)(2,1)S(1)}, bf16[3,96,768]{2,1,0:T(8,128)(2,1)S(1)}, u32[]{:S(2)}, u32[]{:S(2)}) collective-permute-start(bf16[3,96,768]{2,1,0:T(8,128)(2,1)S(1)} %pad_maximum_fusion.refs_3_.refs_8_), channel_id=1, source_target_pairs={{0,24},{4,28},{8,16},{12,20},{16,8},{20,12},{24,0},{28,4},{1,25},{... | collective-permute-start | bytes 1327112 | tf_op jit(solution)/shard_map/ppermute | solution.py:498
  51.7 21.2 %collective-permute-start.28 = (bf16[2,96,768]{2,1,0:T(8,128)(2,1)S(1)}, bf16[2,96,768]{2,1,0:T(8,128)(2,1)S(1)}, u32[]{:S(2)}, u32[]{:S(2)}) collective-permute-start(bf16[2,96,768]{2,1,0:T(8,128)(2,1)S(1)} %pad_maximum_fusion.3), channel_id=1, source_target_pairs={{0,2},{1,3},{2,0},{3,1},{4,6},{5,7},{6,4},{7,5},{8,10},{9,11},{10,... | collective-permute-start | bytes 884744 | tf_op jit(solution)/shard_map/ppermute | solution.py:501
  73.0 14.9 %collective-permute-start.29 = (bf16[3,96,768]{2,1,0:T(8,128)(2,1)S(1)}, bf16[3,96,768]{2,1,0:T(8,128)(2,1)S(1)}, u32[]{:S(2)}, u32[]{:S(2)}) collective-permute-start(bf16[3,96,768]{2,1,0:T(8,128)(2,1)S(1)} %pad_maximum_fusion.1.refs_8_.refs_16_), channel_id=1, source_target_pairs={{0,8},{4,12},{8,0},{12,4},{16,24},{20,28},{24,16},{28,20},{1,9},{5... | collective-permute-start | bytes 1327112 | tf_op jit(solution)/shard_map/ppermute | solution.py:498
  74.0 21.4 %collective-permute-start.30 = (bf16[3,96,768]{2,1,0:T(8,128)(2,1)S(1)}, bf16[3,96,768]{2,1,0:T(8,128)(2,1)S(1)}, u32[]{:S(2)}, u32[]{:S(2)}) collective-permute-start(bf16[3,96,768]{2,1,0:T(8,128)(2,1)S(1)} %pad_maximum_fusion.1.refs_8_.refs_16_), channel_id=1, source_target_pairs={{0,16},{4,20},{8,24},{12,28},{16,0},{20,4},{24,8},{28,12},{1,17},{... | collective-permute-start | bytes 1327112 | tf_op jit(solution)/shard_map/ppermute | solution.py:498
  75.5 19.8 %collective-permute-start.31 = (bf16[3,96,768]{2,1,0:T(8,128)(2,1)S(1)}, bf16[3,96,768]{2,1,0:T(8,128)(2,1)S(1)}, u32[]{:S(2)}, u32[]{:S(2)}) collective-permute-start(bf16[3,96,768]{2,1,0:T(8,128)(2,1)S(1)} %pad_maximum_fusion.1.refs_8_.refs_16_), channel_id=1, source_target_pairs={{0,24},{4,28},{8,16},{12,20},{16,8},{20,12},{24,0},{28,4},{1,25},{... | collective-permute-start | bytes 1327112 | tf_op jit(solution)/shard_map/ppermute | solution.py:498
  141.8 18.9 %collective-permute-start.43 = (bf16[2,2,2,2,96,768]{5,4,3,2,1,0:T(8,128)(2,1)}, bf16[2,2,2,2,96,768]{5,4,3,2,1,0:T(8,128)(2,1)S(1)}, u32[]{:S(2)}, u32[]{:S(2)}) collective-permute-start(bf16[2,2,2,2,96,768]{5,4,3,2,1,0:T(8,128)(2,1)} %get-tuple-element.138), channel_id=1, source_target_pairs={{0,4},{4,0},{8,12},{12,8},{16,20},{20,16},{24,28},{28,24},{1,5},{5... | collective-permute-start | bytes 7077896 | tf_op jit(solution)/shard_map/ppermute | solution.py:498
  160.2 16.4 %collective-permute-start.44 = (bf16[2,2,2,2,96,768]{5,4,3,2,1,0:T(8,128)(2,1)}, bf16[2,2,2,2,96,768]{5,4,3,2,1,0:T(8,128)(2,1)}, u32[]{:S(2)}, u32[]{:S(2)}) collective-permute-start(bf16[2,2,2,2,96,768]{5,4,3,2,1,0:T(8,128)(2,1)} %get-tuple-element.152), channel_id=1, source_target_pairs={{0,4},{4,0},{8,12},{12,8},{16,20},{20,16},{24,28},{28,24},{1,5},{5... | collective-permute-start | bytes 7077896 | tf_op jit(solution)/shard_map/ppermute | solution.py:498
  161.8 19.5 %collective-permute-start.45 = (bf16[2,2,96,768]{3,2,1,0:T(8,128)(2,1)S(1)}, bf16[2,2,96,768]{3,2,1,0:T(8,128)(2,1)}, u32[]{:S(2)}, u32[]{:S(2)}) collective-permute-start(bf16[2,2,96,768]{3,2,1,0:T(8,128)(2,1)S(1)} %get-tuple-element.217), channel_id=1, source_target_pairs={{0,8},{4,12},{8,0},{12,4},{16,24},{20,28},{24,16},{28,20},{1,9},{5... | collective-permute-start | bytes 1769480 | tf_op jit(solution)/shard_map/ppermute | solution.py:498
  164.4 16.9 %collective-permute-start.46 = (bf16[2,2,96,768]{3,2,1,0:T(8,128)(2,1)S(1)}, bf16[2,2,96,768]{3,2,1,0:T(8,128)(2,1)S(1)}, u32[]{:S(2)}, u32[]{:S(2)}) collective-permute-start(bf16[2,2,96,768]{3,2,1,0:T(8,128)(2,1)S(1)} %get-tuple-element.215), channel_id=1, source_target_pairs={{0,16},{4,20},{8,24},{12,28},{16,0},{20,4},{24,8},{28,12},{1,17},{... | collective-permute-start | bytes 1769480 | tf_op jit(solution)/shard_map/ppermute | solution.py:498
  191.9 16.4 %collective-permute-start.47 = (bf16[2,2,96,768]{3,2,1,0:T(8,128)(2,1)}, bf16[2,2,96,768]{3,2,1,0:T(8,128)(2,1)}, u32[]{:S(2)}, u32[]{:S(2)}) collective-permute-start(bf16[2,2,96,768]{3,2,1,0:T(8,128)(2,1)} %get-tuple-element.211), channel_id=1, source_target_pairs={{0,8},{4,12},{8,0},{12,4},{16,24},{20,28},{24,16},{28,20},{1,9},{5... | collective-permute-start | bytes 1769480 | tf_op jit(solution)/shard_map/ppermute | solution.py:498
  193.1 16.5 %collective-permute-start.48 = (bf16[2,2,96,768]{3,2,1,0:T(8,128)(2,1)}, bf16[2,2,96,768]{3,2,1,0:T(8,128)(2,1)}, u32[]{:S(2)}, u32[]{:S(2)}) collective-permute-start(bf16[2,2,96,768]{3,2,1,0:T(8,128)(2,1)} %get-tuple-element.209), channel_id=1, source_target_pairs={{0,16},{4,20},{8,24},{12,28},{16,0},{20,4},{24,8},{28,12},{1,17},{... | collective-permute-start | bytes 1769480 | tf_op jit(solution)/shard_map/ppermute | solution.py:498
  194.7 21.2 %collective-permute-start.74 = (bf16[2,96,768]{2,1,0:T(8,128)(2,1)}, bf16[2,96,768]{2,1,0:T(8,128)(2,1)}, u32[]{:S(2)}, u32[]{:S(2)}) collective-permute-start(bf16[2,96,768]{2,1,0:T(8,128)(2,1)} %fusion.30), channel_id=1, source_target_pairs={{0,16},{4,20},{8,24},{12,28},{16,0},{20,4},{24,8},{28,12},{1,17},{... | collective-permute-start | bytes 884744 | tf_op jit(solution)/shard_map/ppermute | solution.py:498
  202.5 14.3 %collective-permute-start.75 = (bf16[2,96,768]{2,1,0:T(8,128)(2,1)S(1)}, bf16[2,96,768]{2,1,0:T(8,128)(2,1)S(1)}, u32[]{:S(2)}, u32[]{:S(2)}) collective-permute-start(bf16[2,96,768]{2,1,0:T(8,128)(2,1)S(1)} %copy-done.13), channel_id=1, source_target_pairs={{0,8},{4,12},{8,0},{12,4},{16,24},{20,28},{24,16},{28,20},{1,9},{5... | collective-permute-start | bytes 884744 | tf_op jit(solution)/shard_map/ppermute | solution.py:498
  208.3 18.9 %collective-permute-start.52 = (bf16[2,2,96,768]{3,2,1,0:T(8,128)(2,1)S(1)}, bf16[2,2,96,768]{3,2,1,0:T(8,128)(2,1)S(1)}, u32[]{:S(2)}, u32[]{:S(2)}) collective-permute-start(bf16[2,2,96,768]{3,2,1,0:T(8,128)(2,1)S(1)} %get-tuple-element.212), channel_id=1, source_target_pairs={{0,8},{4,12},{8,0},{12,4},{16,24},{20,28},{24,16},{28,20},{1,9},{5... | collective-permute-start | bytes 1769480 | tf_op jit(solution)/shard_map/ppermute | solution.py:498
  209.6 18.9 %collective-permute-start.53 = (bf16[2,2,96,768]{3,2,1,0:T(8,128)(2,1)S(1)}, bf16[2,2,96,768]{3,2,1,0:T(8,128)(2,1)S(1)}, u32[]{:S(2)}, u32[]{:S(2)}) collective-permute-start(bf16[2,2,96,768]{3,2,1,0:T(8,128)(2,1)S(1)} %get-tuple-element.207), channel_id=1, source_target_pairs={{0,16},{4,20},{8,24},{12,28},{16,0},{20,4},{24,8},{28,12},{1,17},{... | collective-permute-start | bytes 1769480 | tf_op jit(solution)/shard_map/ppermute | solution.py:498
  211.5 22.5 %collective-permute-start.50 = (bf16[2,96,768]{2,1,0:T(8,128)(2,1)S(1)}, bf16[2,96,768]{2,1,0:T(8,128)(2,1)S(1)}, u32[]{:S(2)}, u32[]{:S(2)}) collective-permute-start(bf16[2,96,768]{2,1,0:T(8,128)(2,1)S(1)} %fusion.32), channel_id=1, source_target_pairs={{0,16},{4,20},{8,24},{12,28},{16,0},{20,4},{24,8},{28,12},{1,17},{... | collective-permute-start | bytes 884744 | tf_op jit(solution)/shard_map/ppermute | solution.py:498
  215.9 19.7 %collective-permute-start.51 = (bf16[2,96,768]{2,1,0:T(8,128)(2,1)S(1)}, bf16[2,96,768]{2,1,0:T(8,128)(2,1)S(1)}, u32[]{:S(2)}, u32[]{:S(2)}) collective-permute-start(bf16[2,96,768]{2,1,0:T(8,128)(2,1)S(1)} %fusion.33), channel_id=1, source_target_pairs={{0,8},{4,12},{8,0},{12,4},{16,24},{20,28},{24,16},{28,20},{1,9},{5... | collective-permute-start | bytes 884744 | tf_op jit(solution)/shard_map/ppermute | solution.py:498
  216.7 21.9 %collective-permute-start.64 = (f32[16,768]{1,0:T(8,128)S(1)}, f32[16,768]{1,0:T(8,128)S(1)}, u32[]{:S(2)}, u32[]{:S(2)}) collective-permute-start(f32[16,768]{1,0:T(8,128)S(1)} %add.232), channel_id=1, source_target_pairs={{0,4},{4,0},{8,12},{12,8},{16,20},{20,16},{24,28},{28,24},{1,5},{5... | collective-permute-start | bytes 147464 | tf_op jit(solution)/shard_map/ppermute | solution.py:498
  244.8 17.6 %collective-permute-start.80 = (bf16[96,768]{1,0:T(8,128)(2,1)S(1)}, bf16[96,768]{1,0:T(8,128)(2,1)S(1)}, u32[]{:S(2)}, u32[]{:S(2)}) collective-permute-start(bf16[96,768]{1,0:T(8,128)(2,1)S(1)} %add_convert_fusion.12.refs_0_), channel_id=1, source_target_pairs={{0,8},{4,12},{8,0},{12,4},{16,24},{20,28},{24,16},{28,20},{1,9},{5... | collective-permute-start | bytes 442376 | tf_op jit(solution)/shard_map/ppermute | solution.py:498
  273.1 15.5 %collective-permute-start.70 = (bf16[192,768]{1,0:T(8,128)(2,1)S(1)}, bf16[192,768]{1,0:T(8,128)(2,1)S(1)}, u32[]{:S(2)}, u32[]{:S(2)}) collective-permute-start(bf16[192,768]{1,0:T(8,128)(2,1)S(1)} %pad_maximum_fusion.4.refs_0_), channel_id=1, source_target_pairs={{0,16},{4,20},{8,24},{12,28},{16,0},{20,4},{24,8},{28,12},{1,17},{... | collective-permute-start | bytes 884744 | tf_op jit(solution)/shard_map/ppermute | solution.py:498
  273.2 15.4 %collective-permute-start.72 = (bf16[192,768]{1,0:T(8,128)(2,1)S(1)}, bf16[192,768]{1,0:T(8,128)(2,1)S(1)}, u32[]{:S(2)}, u32[]{:S(2)}) collective-permute-start(bf16[192,768]{1,0:T(8,128)(2,1)S(1)} %pad_maximum_fusion.4.refs_0_), channel_id=1, source_target_pairs={{0,24},{4,28},{8,16},{12,20},{16,8},{20,12},{24,0},{28,4},{1,25},{... | collective-permute-start | bytes 884744 | tf_op jit(solution)/shard_map/ppermute | solution.py:498
  (130 other events, 1181.0 us)
